TPU v7x, 256 devices: a whole 4x4x8 slice. The times are simulated.
256 devices in a mesh: sec: 64 (over z, y, core), xs: 4 (over x).
Axes of the slice: x: 4, y: 4, z: 8, core: 2. Of those that a mesh axis runs over, the one named last changes fastest.
Arguments:
- q_block: float32 [512, 4, 8192], P('sec', None, 'xs'), may hold values from -0.0029296875 to 0.0029296875
- q_prev: float32 [512, 4, 8192], P('sec', None, 'xs'), may hold values from -0.0029296875 to 0.0029296875
- b_prev: float32 [4, 4], replicated, as said below
- stiff_blocks: float32 [64, 5, 128, 128], P('xs'), as said below
- couple_blocks: float32 [64, 5, 128, 128], P('xs'), as said below
- block_cols: int32 [64, 5], P('xs'), may hold values from 0 to 63, as said below
- assign: int32 [64], replicated, may hold values from 0 to 255, as said below
Outputs:
- q_next: float32 [512, 4, 8192], P('sec', None, 'xs')
- alphas: float32 [3, 4, 4], replicated
- betas: float32 [3, 4, 4], replicated
Inputs may be any that keep to these rules, and one draw needn't show every extreme that they name: `block_cols`: slot k of block row r refers to offset k - 2: it holds r + k - 2 where that block is coupled and r itself otherwise; offsets -1, 0 and 1 are coupled wherever the column lies in the cross-section; coupling is symmetric between rows. `stiff_blocks`: block (r, k) is the transpose of block (r + k - 2, 4 - k); blocks of uncoupled slots are zero. `couple_blocks`: block (r, k) is the transpose of block (r + k - 2, 4 - k); blocks of uncoupled slots are zero. `b_prev`: upper triangular with a positive diagonal. `assign`: 64 different harmonics, among them 0 and 255.
All inputs are finite; a program needn't handle non-finite values.
Results may differ from a plain program's by a relative error of at most 0.0003.
Values sent between devices are 32-bit elements; how exact they have to be, the bound alone decides.
No kernel may reach another device: no remote copies, remote signals or barrier semaphores. Data moves between devices by JAX's collectives and lax.ppermute only.
A program may use at most 128 MiB of HBM per device.

v0:
```python
import math

import jax
import jax.numpy as jnp
from jax import lax
from jax.sharding import PartitionSpec as P

REACH = 2
ITERS = 3


def extended(value, sides, width):
    for axis, dim in sides:
        count, length = (lax.axis_size(axis), value.shape[dim])
        up = [(i, (i + 1) % count) for i in range(count - 1)]
        down = [(j, i) for i, j in up]
        last = lax.slice_in_dim(value, length - width, length, axis=dim)
        initial = lax.slice_in_dim(value, 0, width, axis=dim)
        before = lax.ppermute(last, axis, up)
        after = lax.ppermute(initial, axis, down)
        value = jnp.concatenate([before, value, after], axis=dim)
    return value


def spectrum_rows(assign, sectors, total):
    harmonic = jnp.repeat(assign, 2)
    parity = jnp.arange(harmonic.shape[0], dtype=jnp.int32) % 2
    phases = harmonic[:, None] * sectors[None, :] % total
    angles = 2.0 * math.pi / total * phases.astype(jnp.float32)
    weights = jnp.where(harmonic == 0, math.sqrt(1.0 / total), math.sqrt(2.0 / total)).astype(
        jnp.float32
    )
    values = jnp.where(parity[:, None] == 0, jnp.cos(angles), -jnp.sin(angles))
    return values * weights[:, None]


def apply_harmonic(field, stiff_blocks, couple_blocks, local_index, factor):
    padded = extended(field, (("xs", 1),), REACH)
    picked = jnp.take(padded, local_index, axis=1)
    own = jnp.einsum("cnkj,nkij->cni", picked, stiff_blocks, precision=lax.Precision.HIGHEST)
    cross = jnp.einsum("cnkj,nkij->cni", picked, couple_blocks, precision=lax.Precision.HIGHEST)
    return own + factor * cross


def per_device(q_block, q_prev, b_prev, stiff_blocks, couple_blocks, block_cols, assign):
    highest = lax.Precision.HIGHEST
    sec_count = lax.axis_size("sec")
    my_sector = lax.axis_index("sec")
    my_slab = lax.axis_index("xs")
    sec_dev, columns_count, dofs = q_block.shape
    nb_dev = stiff_blocks.shape[0]
    block_size = stiff_blocks.shape[-1]
    total = sec_dev * sec_count
    width = columns_count * dofs
    local_index = block_cols - my_slab * nb_dev + REACH
    factors = jnp.cos(2.0 * math.pi / total * (assign % total).astype(jnp.float32))
    factor = factors[my_sector]
    mine = my_sector * sec_dev + jnp.arange(sec_dev, dtype=jnp.int32)
    forward_local = spectrum_rows(assign, mine, total)
    current, previous, coupling = (q_block, q_prev, b_prev)
    alpha_list = []
    beta_list = []
    for step in range(ITERS):
        flat = current.reshape(sec_dev, width)
        spectrum = lax.psum_scatter(
            jnp.dot(forward_local, flat, precision=highest, preferred_element_type=jnp.float32),
            "sec",
            scatter_dimension=0,
            tiled=True,
        )
        field = spectrum.reshape(2 * columns_count, nb_dev, block_size)
        applied = apply_harmonic(field, stiff_blocks, couple_blocks, local_index, factor)
        applied = applied.reshape(2, width)
        image = jnp.dot(
            forward_local.T,
            lax.all_gather(applied, "sec", axis=0, tiled=True),
            precision=highest,
            preferred_element_type=jnp.float32,
        )
        image = image.reshape(sec_dev, columns_count, dofs)
        image = image - jnp.einsum("slp,il->sip", previous, coupling, precision=highest)
        block_alpha = lax.psum(
            jnp.einsum("sip,sjp->ij", current, image, precision=highest), ("sec", "xs")
        )
        residual = image - jnp.einsum("slp,li->sip", current, block_alpha, precision=highest)
        gram = lax.psum(
            jnp.einsum("sip,sjp->ij", residual, residual, precision=highest), ("sec", "xs")
        )
        lower = jnp.linalg.cholesky(gram)
        inverse = jax.scipy.linalg.solve_triangular(
            lower, jnp.eye(columns_count, dtype=jnp.float32), lower=True
        )
        following = jnp.einsum("slp,il->sip", residual, inverse, precision=highest)
        alpha_list.append(block_alpha)
        beta_list.append(lower.T)
        previous, current, coupling = (current, following, lower.T)
    return (current, jnp.stack(alpha_list), jnp.stack(beta_list))


def solution(mesh):
    in_specs = (
        P("sec", None, "xs"),
        P("sec", None, "xs"),
        P(),
        P("xs", None, None, None),
        P("xs", None, None, None),
        P("xs", None),
        P(),
    )
    out_specs = (P("sec", None, "xs"), P(), P())
    return jax.shard_map(
        per_device, mesh=mesh, in_specs=in_specs, out_specs=out_specs, check_vma=False
    )
```

profile of v0, /device:TPU:1, one launch (start us, length us, event | category | flops | bytes accessed | tf_op | source)
XLA Modules:
  0.0 1429.7 jit_solution(7697981031854836661)
XLA Ops:
  9.3 5.5 fusion.52
  16.4 196.8 %all-reduce.7.cloned.1.call-done = f32[128,8192]{1,0:T(8,128)} async-done(((f32[128,8192]{1,0:T(8,128)}), f32[128,8192]{1,0:T(8,128)}) %all-reduce.7.cloned.1.call-update) | async-done | bytes 4194320
  222.4 7.7 fusion.12
  230.1 7.0 fusion.14
  237.9 81.0 %all-gather.7.cloned.1.call-done = f32[64,2,8192]{2,1,0:T(2,128)} async-done(((f32[1,2,8192]{2,1,0:T(2,128)}), f32[64,2,8192]{2,1,0:T(2,128)}) %all-gather.7.cloned.1.call-update) | async-done | bytes 4194320 | tf_op jit(solution)/shard_map/all_gather | solution.py:76
  318.9 6.0 reshape.121
  331.4 75.4 %psum.42 = f32[4,4]{0,1:T(4,128)S(1)} all-reduce(f32[4,4]{0,1:T(4,128)S(1)} %convolution_bitcast_fusion.18), channel_id=1, replica_groups=mesh['sec'=64,'xs'=4] {'sec','xs'}, use_global_device_ids=true, to_apply=%region_1.3 | all-reduce | flops 16 | bytes 128 | tf_op jit(solution)/shard_map/psum | solution.py:82
  408.6 73.0 %psum.43 = f32[4,4]{0,1:T(4,128)S(1)} all-reduce(f32[4,4]{0,1:T(4,128)S(1)} %convolution_bitcast_fusion.17), channel_id=1, replica_groups=mesh['sec'=64,'xs'=4] {'sec','xs'}, use_global_device_ids=true, to_apply=%region_2.4 | all-reduce | flops 16 | bytes 128 | tf_op jit(solution)/shard_map/psum | solution.py:86
  484.7 5.5 fusion.50
  490.3 190.5 %all-reduce.9.cloned.1.call-done = f32[128,8192]{1,0:T(8,128)} async-done(((f32[128,8192]{1,0:T(8,128)}), f32[128,8192]{1,0:T(8,128)}) %all-reduce.9.cloned.1.call-update) | async-done | bytes 4194320
  690.0 7.7 fusion.9
  697.7 7.0 fusion.11
  705.7 80.8 %all-gather.9.cloned.1.call-done = f32[64,2,8192]{2,1,0:T(2,128)} async-done(((f32[1,2,8192]{2,1,0:T(2,128)}), f32[64,2,8192]{2,1,0:T(2,128)}) %all-gather.9.cloned.1.call-update) | async-done | bytes 4194320 | tf_op jit(solution)/shard_map/all_gather | solution.py:76
  786.5 6.0 reshape.123
  799.7 75.0 %psum.44 = f32[4,4]{1,0:T(4,128)S(1)} all-reduce(f32[4,4]{1,0:T(4,128)S(1)} %convolution_bitcast_fusion.16), channel_id=1, replica_groups=mesh['sec'=64,'xs'=4] {'sec','xs'}, use_global_device_ids=true, to_apply=%region_6.10 | all-reduce | flops 16 | bytes 128 | tf_op jit(solution)/shard_map/psum | solution.py:82
  876.5 73.0 %psum.45 = f32[4,4]{0,1:T(4,128)S(1)} all-reduce(f32[4,4]{0,1:T(4,128)S(1)} %convolution_bitcast_fusion.15), channel_id=1, replica_groups=mesh['sec'=64,'xs'=4] {'sec','xs'}, use_global_device_ids=true, to_apply=%region_7.11 | all-reduce | flops 16 | bytes 128 | tf_op jit(solution)/shard_map/psum | solution.py:86
  952.7 5.5 fusion.48
  958.3 190.4 %all-reduce.11.cloned.1.call-done = f32[128,8192]{1,0:T(8,128)} async-done(((f32[128,8192]{1,0:T(8,128)}), f32[128,8192]{1,0:T(8,128)}) %all-reduce.11.cloned.1.call-update) | async-done | bytes 4194320
  1158.0 7.7 fusion.6
  1165.6 7.0 fusion.8
  1173.5 81.0 %all-gather.11.cloned.1.call-done = f32[64,2,8192]{2,1,0:T(2,128)} async-done(((f32[1,2,8192]{2,1,0:T(2,128)}), f32[64,2,8192]{2,1,0:T(2,128)}) %all-gather.11.cloned.1.call-update) | async-done | bytes 4194320 | tf_op jit(solution)/shard_map/all_gather | solution.py:76
  1254.4 6.1 reshape.125
  1267.7 75.0 %psum.46 = f32[4,4]{1,0:T(4,128)S(1)} all-reduce(f32[4,4]{1,0:T(4,128)S(1)} %convolution_bitcast_fusion.14), channel_id=1, replica_groups=mesh['sec'=64,'xs'=4] {'sec','xs'}, use_global_device_ids=true, to_apply=%region_9.13 | all-reduce | flops 16 | bytes 128 | tf_op jit(solution)/shard_map/psum | solution.py:82
  1344.7 73.0 %psum.47 = f32[4,4]{0,1:T(4,128)S(1)} all-reduce(f32[4,4]{0,1:T(4,128)S(1)} %convolution_bitcast_fusion.13), channel_id=1, replica_groups=mesh['sec'=64,'xs'=4] {'sec','xs'}, use_global_device_ids=true, to_apply=%region_10.14 | all-reduce | flops 16 | bytes 128 | tf_op jit(solution)/shard_map/psum | solution.py:86
  (126 shorter events, 70.5 us)
Async XLA Ops:
  7.2 322.3 %copy-start = (f32[8,4,2048]{2,1,0:T(4,128)S(1)}, f32[8,4,2048]{2,1,0:T(4,128)}, u32[]{:S(2)}) copy-start(f32[8,4,2048]{2,1,0:T(4,128)} %param.13) | copy-start | bytes 786436
  7.2 206.0 %all-reduce.7.cloned.1.call-start = ((), (), s32[]{:S(2)}) async-start(), calls=%async_computation.3 | async-start | bytes 8388608
  9.3 5.7 copy-start.3
  9.3 5.8 copy-start.6
  9.3 7.1 copy-start.5
  14.8 304.1 %all-gather.7.cloned.1.call-start = ((), (), s32[]{:S(2)}) async-start(), calls=%async_computation | async-start | bytes 4259840 | tf_op jit(solution)/shard_map/all_gather | solution.py:76
  214.3 5.1 collective-permute-start
  217.4 4.4 collective-permute-start.1
  237.9 442.9 %all-reduce.9.cloned.1.call-start = ((), (), s32[]{:S(2)}) async-start(), calls=%async_computation.4 | async-start | bytes 8388608
  325.0 4.5 copy-start.4
  325.0 5.2 copy-start.2
  490.3 296.3 %all-gather.9.cloned.1.call-start = ((), (), s32[]{:S(2)}) async-start(), calls=%async_computation.1 | async-start | bytes 4259840 | tf_op jit(solution)/shard_map/all_gather | solution.py:76
  681.9 4.4 collective-permute-start.2
  685.0 4.4 collective-permute-start.3
  705.5 443.2 %all-reduce.11.cloned.1.call-start = ((), (), s32[]{:S(2)}) async-start(), calls=%async_computation.5 | async-start | bytes 8388608
  958.2 296.2 %all-gather.11.cloned.1.call-start = ((), (), s32[]{:S(2)}) async-start(), calls=%async_computation.2 | async-start | bytes 4259840 | tf_op jit(solution)/shard_map/all_gather | solution.py:76
  1149.8 4.6 collective-permute-start.4
  1152.9 4.4 collective-permute-start.5
  1254.4 168.2 %copy-start.1 = (f32[8,4,2048]{2,1,0:T(4,128)S(1)}, f32[8,4,2048]{2,1,0:T(4,128)}, u32[]{:S(2)}) copy-start(f32[8,4,2048]{2,1,0:T(4,128)} %param.13) | copy-start | bytes 786436
Sparse Core Ops, SparseCore 0:
  15.0 198.1 all-reduce.6
  238.0 80.8 all-gather.6
  490.4 190.3 all-reduce.8
  705.6 80.8 all-gather.8
  958.3 190.3 all-reduce.10
  1173.5 80.8 all-gather.10
where the time goes:
time: 1440 us; the launch traced here: 1430 us
  waiting for transfers between devices  829 us (58%)
  blocking collectives  444 us (31%)
  matrix products  89.8 us (6%)
  local copies, waits for them, and re-layouts  29.8 us (2%)
  between operations  15.5 us (1%)
    unnamed x9, waiting for transfers between devices  578 us
    all_gather x3, waiting for transfers between devices, per_device(): lax.all_gather(applied, 'sec', axis=0, tiled=True)  243 us
    psum x3, blocking collectives, per_device(): lax.psum(jnp.einsum('sip,sjp->ij', current, image, precision=highest), ('...  225 us
    psum x3, blocking collectives, per_device(): lax.psum(jnp.einsum('sip,sjp->ij', residual, residual, precision=highest)...  219 us
  transfers between devices with their start and end apart: 12, of which 9 were waited for; matrix products, arithmetic and copies ran while one was open for 0% of the time, Pallas kernels for 0%

commit v1 on v0

v1 whole, which is shorter than its diff:
```python
import math

import jax
import jax.numpy as jnp
from jax import lax
from jax.experimental import pallas as pl
from jax.experimental.pallas import tpu as pltpu
from jax.sharding import Mesh
from jax.sharding import PartitionSpec as P

HI = lax.Precision.HIGHEST
SEC = ("z", "y", "core")
BLOCKS = ("z", "core", "xs")
SECTORS = 512
NT = (((1,), (1,)), ((), ()))
VMEM_LIMIT = 32 * 1024 * 1024


def call(kernel, out, *args, specs=None, **kw):
    return pl.pallas_call(
        kernel,
        out_shape=out,
        compiler_params=pltpu.CompilerParams(vmem_limit_bytes=VMEM_LIMIT),
        **kw,
    )(*args)


def f32(*shape):
    return jax.ShapeDtypeStruct(shape, jnp.float32)


def dot(a, b, dims=(((1,), (0,)), ((), ()))):
    return lax.dot_general(a, b, dims, precision=HI, preferred_element_type=jnp.float32)


def pack_kernel(q_ref, p_ref, out_ref, gram_ref):
    for block in range(16):
        for col in range(4):
            place = (block // 2 * 4 + col) * 2 + block % 2
            lanes = pl.ds(block * 128, 128)
            out_ref[place, 0] = q_ref[:, col, lanes]
            out_ref[place, 1] = p_ref[:, col, lanes]
    total = jnp.zeros((8, 8), jnp.float32)
    for s in range(8):
        rows = jnp.concatenate([q_ref[s], p_ref[s]], axis=0)
        total += dot(rows, rows, NT)
    gram_ref[...] = jnp.zeros((8, 128), jnp.float32)
    gram_ref[:, 64:72] = total


def stats_kernel(s_ref, c_ref, out_ref):
    step = pl.program_id(0)
    row = lax.broadcasted_iota(jnp.int32, (128, 128), 0)
    col = lax.broadcasted_iota(jnp.int32, (128, 128), 1)
    big = jnp.float32(3.0e38)
    found = []
    for ref in (s_ref, c_ref):
        largest = jnp.max(jnp.abs(ref[0]), axis=0)
        largest = jnp.max(largest.reshape(16, 8, 128), axis=0)
        middle = ref[0, 2]
        top = jnp.max(jnp.where(row == col, middle, -big).reshape(16, 8, 128), axis=0)
        low = jnp.max(jnp.where(row == col, -middle, -big).reshape(16, 8, 128), axis=0)
        found += [largest, top, low]

    @pl.when(step == 0)
    def _():
        for i, v in enumerate(found):
            out_ref[i] = v

    @pl.when(step > 0)
    def _():
        for i, v in enumerate(found):
            out_ref[i] = jnp.maximum(out_ref[i], v)


def forward_kernel(f_ref, r_ref, out_ref):
    for t in range(2):
        field = r_ref[:, t].reshape(SECTORS, 128)
        out_ref[:, t] = dot(f_ref[...], field).reshape(4, 32, 128)


def inverse_kernel(f_ref, r_ref, out_ref):
    field = r_ref[...].reshape(128, 128)
    out_ref[...] = dot(f_ref[...], field, (((0,), (0,)), ((), ()))).reshape(64, 8, 128)


def apply_kernel(order, index_ref, m2, m1, v0, p1, p2, s_ref, c_ref, f_ref, k_ref, out_ref):
    def rows(ref):
        if order == "ct":
            return jnp.concatenate([ref[:, 0].reshape(128, 128), ref[:, 1].reshape(128, 128)], 0)
        return ref[...].reshape(-1, 128)

    own = rows(v0)
    count = own.shape[0]
    left = jnp.concatenate([rows(m2), rows(m1), own, rows(p1), rows(p2)], axis=1)
    right = jnp.concatenate(
        [
            jnp.concatenate([s_ref[0, k] for k in range(5)], axis=1),
            jnp.concatenate([c_ref[0, k] for k in range(5)], axis=1),
        ],
        axis=0,
    )
    both = dot(left, right, NT)
    factor = f_ref[...][None]
    value = both[:, :128].reshape(-1, 32, 128) + factor * both[:, 128:].reshape(-1, 32, 128)
    value = (value - k_ref[0:1, :][None] * own.reshape(-1, 32, 128)) * k_ref[1:2, :][None]
    out_ref[...] = value.reshape(out_ref.shape)


def apply_op(order, parts, stiff, couple, factor, scales, block, out_shape):
    whole = pl.BlockSpec(memory_space=pltpu.VMEM)
    picked = pl.BlockSpec((1, 5, 128, 128), lambda i, b: (b[0], 0, 0, 0))
    return pl.pallas_call(
        lambda *refs: apply_kernel(order, *refs),
        out_shape=f32(*out_shape),
        grid_spec=pltpu.PrefetchScalarGridSpec(
            num_scalar_prefetch=1,
            grid=(1,),
            in_specs=[whole] * 5 + [picked, picked, whole, whole],
            out_specs=whole,
        ),
        compiler_params=pltpu.CompilerParams(vmem_limit_bytes=VMEM_LIMIT),
    )(block, *parts, stiff, couple, factor, scales)


def gram_kernel(k0, k1, k2, k3, m_ref, out_ref):
    total = jnp.zeros((32, 32), jnp.float32)
    for r in range(32):
        rows = jnp.concatenate(
            [
                k0[:, 0, r, :],
                k0[:, 1, r, :],
                k1[0, :, r, :],
                k1[1, :, r, :],
                k2[0, :, r, :],
                k2[1, :, r, :],
                k3[:, r, :],
                jnp.zeros((4, 128), jnp.float32),
            ],
            axis=0,
        )
        total += dot(rows, rows, NT)
    out_ref[...] = jnp.zeros((32, 128), jnp.float32)
    out_ref[:, 0:32] = total
    out_ref[0:8, 64:128] = m_ref[:, 64:128]


def mixed(weights, rows):
    total = weights[:, 0:1] * rows[0:1, :]
    for l in range(1, 4):
        total += weights[:, l : l + 1] * rows[l : l + 1, :]
    return total


def solve_kernel(g_ref, b_ref, k_ref, k0, k1, k2, k3, z_ref, coef_ref, alpha_ref, beta_ref):
    lane = lax.broadcasted_iota(jnp.int32, (4, 128), 1)
    row = lax.broadcasted_iota(jnp.int32, (4, 128), 0)
    spectral = lane < 28
    sigma, scale = k_ref[0:1, :], k_ref[2:3, :]
    full = g_ref[...]
    wide = lax.broadcasted_iota(jnp.int32, (32, 128), 1)
    gram = jnp.where(wide < 28, full, 0.0)
    shifted = jnp.concatenate([gram[8:32], jnp.zeros((8, 128), jnp.float32)], axis=0)
    rest = jnp.where(
        (wide[0:8] >= 64) & (wide[0:8] < 72), full[0:8] - pltpu.roll(full[0:8], 64, 1), 0.0
    )
    first = gram[0:8] + rest
    cur = ((lane == row) | (lane == row + 64)).astype(jnp.float32)
    prev = ((lane == row + 4) | (lane == row + 68)).astype(jnp.float32)
    cur_g, prev_g = first[0:4], first[4:8]
    coupling = b_ref[...]
    for step in range(3):
        seen = jnp.where(spectral, cur, 0.0)
        w = scale * pltpu.roll(seen, 8, 1) + sigma * seen - mixed(coupling, prev)
        w_g = (
            scale * dot(cur[:, 0:32], shifted)
            + sigma * jnp.where(spectral, cur_g, 0.0)
            - mixed(coupling, prev_g)
        )
        turned = jnp.concatenate(
            [jnp.sum(w_g * cur[l : l + 1, :], axis=1, keepdims=True) for l in range(4)], axis=1
        )
        alpha_ref[step] = jnp.concatenate(
            [jnp.sum(cur_g * w[l : l + 1, :], axis=1, keepdims=True) for l in range(4)], axis=1
        )
        r = w - mixed(turned, cur)
        r_g = w_g - mixed(turned, cur_g)
        square = jnp.concatenate(
            [jnp.sum(r_g * r[l : l + 1, :], axis=1, keepdims=True) for l in range(4)], axis=1
        )
        small_row = lax.broadcasted_iota(jnp.int32, (4, 4), 0)
        small_col = lax.broadcasted_iota(jnp.int32, (4, 4), 1)
        pivots = jnp.zeros((4, 1), jnp.float32)
        one_row = lax.broadcasted_iota(jnp.int32, (4, 1), 0)
        for i in range(4):
            pivot = square[i : i + 1, i : i + 1]
            pivots = jnp.where(one_row == i, pivot, pivots)
            if i < 3:
                times = jnp.where(one_row > i, square[:, i : i + 1] / pivot, 0.0)
                r = r - times * r[i : i + 1, :]
                r_g = r_g - times * r_g[i : i + 1, :]
                square = square - times * square[i : i + 1, :]
        root = 1.0 / jnp.sqrt(pivots)
        upper = jnp.where(small_col >= small_row, square * root, 0.0)
        beta_ref[step] = upper
        prev, prev_g, coupling = cur, cur_g, upper
        cur, cur_g = r * root, r_g * root
    coef_ref[...] = cur
    weights = cur - jnp.where(lane < 8, pltpu.roll(cur, 64, 1), 0.0)
    basis = (
        [k0[c, 0] for c in range(4)]
        + [k0[c, 1] for c in range(4)]
        + [k1[t, c] for t in range(2) for c in range(4)]
        + [k2[t, c] for t in range(2) for c in range(4)]
        + [k3[c] for c in range(4)]
    )
    for i in range(4):
        total = weights[i : i + 1, 0:1] * basis[0]
        for k in range(1, 28):
            total += weights[i : i + 1, k : k + 1] * basis[k]
        z_ref[i] = total


def last_kernel(r_ref, q_ref, coef_ref, out_ref):
    coef = coef_ref[...]
    scalars = [
        [coef[c : c + 1, 64 + k : 65 + k] + jnp.zeros((8, 128), jnp.float32) for k in range(8)]
        for c in range(4)
    ]
    for block in range(16):
        places = [(block // 2 * 4 + c) * 2 + block % 2 for c in range(4)]
        tiles = [q_ref[p, 0] for p in places] + [q_ref[p, 1] for p in places]
        for c in range(4):
            total = r_ref[places[c]]
            for k in range(8):
                total += scalars[c][k] * tiles[k]
            out_ref[:, c, pl.ds(block * 128, 128)] = total


def table(assign):
    harmonic = jnp.repeat(assign, 2)
    parity = jnp.arange(harmonic.shape[0], dtype=jnp.int32) % 2
    sectors = jnp.arange(SECTORS, dtype=jnp.int32)
    phases = (harmonic[:, None] * sectors[None, :] + 128 * parity[:, None]) % SECTORS
    weights = jnp.where(harmonic == 0, math.sqrt(1.0 / SECTORS), math.sqrt(2.0 / SECTORS))
    weights = jnp.where((harmonic == 0) & (parity == 1), 0.0, weights).astype(jnp.float32)
    return jnp.cos(2.0 * math.pi / SECTORS * phases.astype(jnp.float32)) * weights[:, None]


def neighbour(value, offset):
    pairs = []
    for b in range(64):
        if 0 <= b + offset < 64:
            place = [(i % 16) * 4 + i // 16 for i in (b, b + offset)]
            pairs.append(tuple(place))
    return lax.ppermute(value, BLOCKS, pairs)


def around(value):
    return [neighbour(value, 2), neighbour(value, 1), value, neighbour(value, -1), neighbour(value, -2)]


def exchange(value, axis, count, step, combine):
    return combine(value, lax.ppermute(value, axis, [(i, i ^ step) for i in range(count)]))


def per_device(q_block, q_prev, b_prev, stiff_blocks, couple_blocks, block_cols, assign):
    block = lax.axis_index("z") * 2 + lax.axis_index("core")
    group = lax.axis_index("y")
    forward = table(assign)
    factors = jnp.cos(2.0 * math.pi / SECTORS * assign.astype(jnp.float32))
    mine = lax.dynamic_slice_in_dim(factors, group * 16, 16)
    factor = jnp.broadcast_to(jnp.repeat(mine, 2)[:, None], (32, 128))

    found = pl.pallas_call(
        stats_kernel,
        out_shape=f32(6, 8, 128),
        grid=(16,),
        in_specs=[pl.BlockSpec((1, 5, 128, 128), lambda i: (i, 0, 0, 0))] * 2,
        out_specs=pl.BlockSpec((6, 8, 128), lambda i: (0, 0, 0)),
        compiler_params=pltpu.CompilerParams(vmem_limit_bytes=VMEM_LIMIT),
    )(stiff_blocks, couple_blocks)
    found = jnp.broadcast_to(jnp.max(found, axis=(1, 2))[:, None], (6, 128))
    found = exchange(found, "xs", 4, 1, jnp.maximum)
    found = exchange(found, "xs", 4, 2, jnp.maximum)
    sigma = 0.5 * (found[1] - found[2]) + jnp.mean(factors) * (0.5 * (found[4] - found[5]))
    scale = found[0] + found[3]
    scale = jnp.where(scale > 0, scale, 1.0)
    scales = jnp.stack([sigma, 1.0 / scale, scale] + [scale] * 5)

    packed, gram_raw = call(pack_kernel, (f32(64, 2, 8, 128), f32(8, 128)), q_block, q_prev)
    received = lax.all_to_all(packed, SEC, 0, 0, tiled=True)
    spectrum = call(forward_kernel, f32(4, 2, 32, 128), forward, received)
    k0 = lax.all_to_all(spectrum, "y", 0, 0, tiled=True)
    where = block.astype(jnp.int32).reshape(1)
    k1 = apply_op("ct", around(k0), stiff_blocks, couple_blocks, factor, scales, where, (2, 4, 32, 128))
    k2 = apply_op("tc", around(k1), stiff_blocks, couple_blocks, factor, scales, where, (2, 4, 32, 128))
    k3 = apply_op("tc", around(k2[0]), stiff_blocks, couple_blocks, factor, scales, where, (4, 32, 128))
    gram = call(gram_kernel, f32(32, 128), k0, k1, k2, k3, gram_raw)
    for axis, count in (("core", 2), ("xs", 4), ("y", 4), ("z", 8)):
        step = 1
        while step < count:
            gram = exchange(gram, axis, count, step, jnp.add)
            step *= 2
    mix, coef, alphas, betas = call(
        solve_kernel,
        (f32(4, 32, 128), f32(4, 128), f32(3, 4, 4), f32(3, 4, 4)),
        gram, b_prev, scales, k0, k1, k2, k3,
    )
    rows = lax.all_to_all(mix, "y", 0, 0, tiled=True)
    image = call(inverse_kernel, f32(64, 8, 128), forward, rows)
    back = lax.all_to_all(image, SEC, 0, 0, tiled=True)
    out = call(last_kernel, f32(8, 4, 2048), back, packed, coef)
    return out, alphas, betas


def solution(mesh):
    fine = Mesh(mesh.devices.reshape(8, 4, 2, 4), ("z", "y", "core", "xs"))
    in_specs = (
        P(SEC, None, "xs"),
        P(SEC, None, "xs"),
        P(),
        P("xs", None, None, None),
        P("xs", None, None, None),
        P("xs", None),
        P(),
    )
    out_specs = (P(SEC, None, "xs"), P(), P())
    return jax.shard_map(
        per_device, mesh=fine, in_specs=in_specs, out_specs=out_specs, check_vma=False
    )
```

time: 1440 us -> 171 us (0.12)
  waiting for transfers between devices: 829 us -> 36.1 us
  blocking collectives: 444 us -> 33.5 us
  matrix products: 89.8 us -> 0 us
  starting transfers between devices: 13.8 us -> 71 us
  local copies, waits for them, and re-layouts: 29.8 us -> 12.5 us
    unnamed x9 -> x0, waiting for transfers between devices: 578 us -> none
    psum x6 -> x0, blocking collectives: 444 us -> none  [the longest x3 225 us: per_device(): lax.psum(jnp.einsum('sip,sjp->ij', current, image, precision=highest), ('...]
    all_gather x3 -> x0, waiting for transfers between devices: 243 us -> none  [per_device(): lax.all_gather(applied, 'sec', axis=0, tiled=True)]
    dot_general x27 -> x0, matrix products: 89.3 us -> none  [the longest x3 23.1 us: apply_harmonic(): jnp.einsum('cnkj,nkij->cni', picked, couple_blocks, precision=lax.Precisi...]
    ppermute x6 -> x22, starting transfers between devices: 13.4 us -> 54.6 us  [the longest x12 36.3 us: neighbour(): return lax.ppermute(value, BLOCKS, pairs)]
    all_to_all x0 -> x2, blocking collectives: none -> 33.5 us  [the longest x1 26.7 us: per_device(): back = lax.all_to_all(image, SEC, 0, 0, tiled=True)]
    ppermute x6 -> x22, waiting for transfers between devices: 8.36 us -> 26.9 us  [the longest x10 20.5 us: exchange(): lax.ppermute(value, axis, [(i, i ^ step) for i in range(count)])]
    all_to_all x0 -> x2, starting transfers between devices: none -> 16.5 us  [the longest x1 13.2 us: per_device(): received = lax.all_to_all(packed, SEC, 0, 0, tiled=True)]
  transfers between devices with their start and end apart: 12 -> 24, of which waited for: 9 -> 14; matrix products, arithmetic and copies ran while one was open for 0% -> 2% of each run, Pallas kernels for 0% -> 1%
where the time goes in v1:
time: 171 us; the launch traced here: 170 us
  starting transfers between devices  71 us (42%)
  waiting for transfers between devices  36.1 us (21%)
  blocking collectives  33.5 us (20%)
  Pallas kernels  13.2 us (8%)
  local copies, waits for them, and re-layouts  12.5 us (7%)
  other arithmetic  2.04 us (1%)
    ppermute x12, starting transfers between devices, neighbour(): return lax.ppermute(value, BLOCKS, pairs)  36.3 us
    all_to_all x1, blocking collectives, per_device(): back = lax.all_to_all(image, SEC, 0, 0, tiled=True)  26.7 us
    ppermute x10, waiting for transfers between devices, exchange(): lax.ppermute(value, axis, [(i, i ^ step) for i in range(count)])  20.5 us
    ppermute x10, starting transfers between devices, exchange(): lax.ppermute(value, axis, [(i, i ^ step) for i in range(count)])  18.3 us
    all_to_all x1, starting transfers between devices, per_device(): received = lax.all_to_all(packed, SEC, 0, 0, tiled=True)  13.2 us
    unnamed x16, local copies, waits for them, and re-layouts  11.8 us
    pallas_call x6, Pallas kernels, call(): pl.pallas_call(kernel, out_shape=out, compiler_params=pltpu.CompilerParam...  9.84 us
    all_to_all x1, blocking collectives, per_device(): rows = lax.all_to_all(mix, 'y', 0, 0, tiled=True)  6.83 us
  transfers between devices with their start and end apart: 24, of which 14 were waited for; matrix products, arithmetic and copies ran while one was open for 2% of the time, Pallas kernels for 1%

profile of v1, /device:TPU:1, one launch (start us, length us, event | category | flops | bytes accessed | tf_op | source)
XLA Modules:
  0.0 169.9 jit_solution(8582250294475469571)
XLA Ops:
  4.7 13.2 %all-to-all-start = ((f32[64,2,8,128]{3,2,1,0:T(8,128)}), f32[64,2,8,128]{3,2,1,0:T(8,128)S(1)}, u32[]{:S(2)}, u32[]{:S(2)}) async-start(f32[64,2,8,128]{3,2,1,0:T(8,128)} %get-tuple-element.9.q_ref), calls=%async_computation | async-start | bytes 1048576 | tf_op jit(solution)/shard_map/all_to_all | solution.py:292
  26.8 2.7 %collective-permute-start.5 = (f32[6,128]{1,0:T(8,128)S(1)}, f32[6,128]{1,0:T(8,128)S(1)}, u32[]{:S(2)}, u32[]{:S(2)}) collective-permute-start(f32[6,128]{1,0:T(8,128)S(1)} %broadcast_maximum_fusion), channel_id=1, source_target_pairs={{0,2},{1,3},{2,0},{3,1},{4,6},{5,7},{6,4},{7,5},{8,10},{9,11},{10,... | collective-permute-start | bytes 9224 | tf_op jit(solution)/shard_map/ppermute | solution.py:264
  31.1 4.5 %all-to-all-done.r_ref = f32[64,2,8,128]{3,2,1,0:T(8,128)S(1)} async-done(((f32[64,2,8,128]{3,2,1,0:T(8,128)}), f32[64,2,8,128]{3,2,1,0:T(8,128)S(1)}, u32[]{:S(2)}, u32[]{:S(2)}) %all-to-all-start) | async-done | bytes 524320 | tf_op jit(solution)/shard_map/all_to_all | solution.py:292
  36.8 3.3 %all-to-all-start.1 = ((f32[4,2,32,128]{3,2,1,0:T(8,128)}), f32[4,2,32,128]{3,2,1,0:T(8,128)S(1)}, u32[]{:S(2)}, u32[]{:S(2)}) async-start(f32[4,2,32,128]{3,2,1,0:T(8,128)} %shard_map.86), calls=%async_computation.1 | async-start | bytes 262144 | tf_op jit(solution)/shard_map/all_to_all | solution.py:294
  40.2 4.7 %all-to-all-done.1.refs_3_.k0 = f32[4,2,32,128]{3,2,1,0:T(8,128)S(1)} async-done(((f32[4,2,32,128]{3,2,1,0:T(8,128)}), f32[4,2,32,128]{3,2,1,0:T(8,128)S(1)}, u32[]{:S(2)}, u32[]{:S(2)}) %all-to-all-start.1) | async-done | bytes 131104 | tf_op jit(solution)/shard_map/all_to_all | solution.py:294
  46.2 4.4 %collective-permute-start.2 = (f32[4,2,32,128]{3,2,1,0:T(8,128)S(1)}, f32[4,2,32,128]{3,2,1,0:T(8,128)S(1)}, u32[]{:S(2)}, u32[]{:S(2)}) collective-permute-start(f32[4,2,32,128]{3,2,1,0:T(8,128)S(1)} %all-to-all-done.1.refs_3_.k0), channel_id=1, source_target_pairs={{4,0},{32,4},{36,32},{64,36},{68,64},{96,68},{100,96},{128,100},{1... | collective-permute-start | bytes 393224 | tf_op jit(solution)/shard_map/ppermute | solution.py:256
  50.6 4.2 %collective-permute-start.1 = (f32[4,2,32,128]{3,2,1,0:T(8,128)S(1)}, f32[4,2,32,128]{3,2,1,0:T(8,128)S(1)}, u32[]{:S(2)}, u32[]{:S(2)}) collective-permute-start(f32[4,2,32,128]{3,2,1,0:T(8,128)S(1)} %all-to-all-done.1.refs_3_.k0), channel_id=1, source_target_pairs={{0,4},{4,32},{32,36},{36,64},{64,68},{68,96},{96,100},{100,128},{1... | collective-permute-start | bytes 393224 | tf_op jit(solution)/shard_map/ppermute | solution.py:256
  57.2 2.5 %collective-permute-done.refs_1_ = f32[4,2,32,128]{3,2,1,0:T(8,128)S(1)} collective-permute-done((f32[4,2,32,128]{3,2,1,0:T(8,128)S(1)}, f32[4,2,32,128]{3,2,1,0:T(8,128)S(1)}, u32[]{:S(2)}, u32[]{:S(2)}) %collective-permute-start) | collective-permute-done | bytes 131104 | tf_op jit(solution)/shard_map/ppermute | solution.py:256
  59.7 2.5 %copy-done.1 = f32[16,5,128,128]{3,2,1,0:T(8,128)S(1)} copy-done((f32[16,5,128,128]{3,2,1,0:T(8,128)S(1)}, f32[16,5,128,128]{3,2,1,0:T(8,128)}, u32[]{:S(2)}) %copy-start.1) | copy-done | bytes 5242904
  66.9 3.0 %collective-permute-start.8 = (f32[2,4,32,128]{3,2,1,0:T(8,128)S(1)}, f32[2,4,32,128]{3,2,1,0:T(8,128)S(1)}, u32[]{:S(2)}, u32[]{:S(2)}) collective-permute-start(f32[2,4,32,128]{3,2,1,0:T(8,128)S(1)} %shard_map.88.refs_3_.k1), channel_id=1, source_target_pairs={{4,0},{32,4},{36,32},{64,36},{68,64},{96,68},{100,96},{128,100},{1... | collective-permute-start | bytes 393224 | tf_op jit(solution)/shard_map/ppermute | solution.py:256
  69.9 4.6 %collective-permute-start.7 = (f32[2,4,32,128]{3,2,1,0:T(8,128)S(1)}, f32[2,4,32,128]{3,2,1,0:T(8,128)S(1)}, u32[]{:S(2)}, u32[]{:S(2)}) collective-permute-start(f32[2,4,32,128]{3,2,1,0:T(8,128)S(1)} %shard_map.88.refs_3_.k1), channel_id=1, source_target_pairs={{0,4},{4,32},{32,36},{36,64},{64,68},{68,96},{96,100},{100,128},{1... | collective-permute-start | bytes 393224 | tf_op jit(solution)/shard_map/ppermute | solution.py:256
  74.5 3.6 %collective-permute-start.6 = (f32[2,4,32,128]{3,2,1,0:T(8,128)S(1)}, f32[2,4,32,128]{3,2,1,0:T(8,128)S(1)}, u32[]{:S(2)}, u32[]{:S(2)}) collective-permute-start(f32[2,4,32,128]{3,2,1,0:T(8,128)S(1)} %shard_map.88.refs_3_.k1), channel_id=1, source_target_pairs={{0,32},{4,36},{32,64},{36,68},{64,96},{68,100},{96,128},{100,132},... | collective-permute-start | bytes 393224 | tf_op jit(solution)/shard_map/ppermute | solution.py:256
  78.2 2.6 %collective-permute-done.6.refs_1_ = f32[2,4,32,128]{3,2,1,0:T(8,128)S(1)} collective-permute-done((f32[2,4,32,128]{3,2,1,0:T(8,128)S(1)}, f32[2,4,32,128]{3,2,1,0:T(8,128)S(1)}, u32[]{:S(2)}, u32[]{:S(2)}) %collective-permute-start.6) | collective-permute-done | bytes 131104 | tf_op jit(solution)/shard_map/ppermute | solution.py:256
  84.9 4.4 %collective-permute-start.11 = (f32[4,32,128]{2,1,0:T(8,128)S(1)}, f32[4,32,128]{2,1,0:T(8,128)S(1)}, u32[]{:S(2)}, u32[]{:S(2)}) collective-permute-start(f32[4,32,128]{2,1,0:T(8,128)S(1)} %slice_bitcast_fusion.refs_3_), channel_id=1, source_target_pairs={{0,4},{4,32},{32,36},{36,64},{64,68},{68,96},{96,100},{100,128},{1... | collective-permute-start | bytes 196616 | tf_op jit(solution)/shard_map/ppermute | solution.py:256
  89.3 4.0 %collective-permute-start.10 = (f32[4,32,128]{2,1,0:T(8,128)S(1)}, f32[4,32,128]{2,1,0:T(8,128)S(1)}, u32[]{:S(2)}, u32[]{:S(2)}) collective-permute-start(f32[4,32,128]{2,1,0:T(8,128)S(1)} %slice_bitcast_fusion.refs_3_), channel_id=1, source_target_pairs={{0,32},{4,36},{32,64},{36,68},{64,96},{68,100},{96,128},{100,132},... | collective-permute-start | bytes 196616 | tf_op jit(solution)/shard_map/ppermute | solution.py:256
  97.5 8.7 %collective-permute-start.15 = (f32[32,128]{1,0:T(8,128)S(1)}, f32[32,128]{1,0:T(8,128)S(1)}, u32[]{:S(2)}, u32[]{:S(2)}) collective-permute-start(f32[32,128]{1,0:T(8,128)S(1)} %add.76), channel_id=1, source_target_pairs={{0,1},{1,0},{2,3},{3,2},{4,5},{5,4},{6,7},{7,6},{8,9},{9,8},{10,11... | collective-permute-start | bytes 49160 | tf_op jit(solution)/shard_map/ppermute | solution.py:264
  107.3 3.0 %collective-permute-start.16 = (f32[32,128]{1,0:T(8,128)S(1)}, f32[32,128]{1,0:T(8,128)S(1)}, u32[]{:S(2)}, u32[]{:S(2)}) collective-permute-start(f32[32,128]{1,0:T(8,128)S(1)} %add.77), channel_id=1, source_target_pairs={{0,2},{1,3},{2,0},{3,1},{4,6},{5,7},{6,4},{7,5},{8,10},{9,11},{10,... | collective-permute-start | bytes 49160 | tf_op jit(solution)/shard_map/ppermute | solution.py:264
  114.6 3.5 %collective-permute-done.18 = f32[32,128]{1,0:T(8,128)S(1)} collective-permute-done((f32[32,128]{1,0:T(8,128)S(1)}, f32[32,128]{1,0:T(8,128)S(1)}, u32[]{:S(2)}, u32[]{:S(2)}) %collective-permute-start.18) | collective-permute-done | bytes 16416 | tf_op jit(solution)/shard_map/ppermute | solution.py:264
  118.1 2.6 %collective-permute-done.19 = f32[32,128]{1,0:T(8,128)S(1)} collective-permute-done((f32[32,128]{1,0:T(8,128)S(1)}, f32[32,128]{1,0:T(8,128)S(1)}, u32[]{:S(2)}, u32[]{:S(2)}) %collective-permute-start.19) | collective-permute-done | bytes 16416 | tf_op jit(solution)/shard_map/ppermute | solution.py:264
  120.9 3.5 %collective-permute-done.20 = f32[32,128]{1,0:T(8,128)S(1)} collective-permute-done((f32[32,128]{1,0:T(8,128)S(1)}, f32[32,128]{1,0:T(8,128)S(1)}, u32[]{:S(2)}, u32[]{:S(2)}) %collective-permute-start.20) | collective-permute-done | bytes 16416 | tf_op jit(solution)/shard_map/ppermute | solution.py:264
  126.0 4.9 %collective-permute-done.21 = f32[32,128]{1,0:T(8,128)S(1)} collective-permute-done((f32[32,128]{1,0:T(8,128)S(1)}, f32[32,128]{1,0:T(8,128)S(1)}, u32[]{:S(2)}, u32[]{:S(2)}) %collective-permute-start.21) | collective-permute-done | bytes 16416 | tf_op jit(solution)/shard_map/ppermute | solution.py:264
  130.9 3.0 %shard_map.92 = (f32[4,32,128]{2,1,0:T(8,128)S(1)}, f32[4,128]{1,0:T(4,128)S(1)}, f32[3,4,4]{2,1,0:T(4,128)}, f32[3,4,4]{2,1,0:T(4,128)}) custom-call(f32[32,128]{1,0:T(8,128)S(1)} %add.83.g_ref, f32[4,4]{1,0:T(4,128)S(1)} %copy-done.6, f32[8,128]{1,0:T(8,128)S(1)} %stack.2.refs_9_.k_ref, f32[4,2,32,128]{3,2,1,0:T(8,128)S(1)} %all-to-all-done.1.refs_3_.k0, ...), custom_call_target="tpu_custom_call" | custom-call | tf_op jit(solution)/shard_map/pallas_call | solution.py:20
  133.9 6.8 %all_to_all.20.r_ref = f32[4,32,128]{2,1,0:T(8,128)S(1)} all-to-all(f32[4,32,128]{2,1,0:T(8,128)S(1)} %get-tuple-element.11), channel_id=1, replica_groups=mesh['z'=8,'y'=4,'core'=2,'xs'=4] {'y'}, dimensions={0} | all-to-all | bytes 131072 | tf_op jit(solution)/shard_map/all_to_all | solution.py:310
  141.1 26.7 %all_to_all.21.r_ref = f32[64,8,128]{2,1,0:T(8,128)S(1)} all-to-all(f32[64,8,128]{2,1,0:T(8,128)S(1)} %shard_map.93), channel_id=1, replica_groups=mesh['z'=8,'y'=4,'core'=2,'xs'=4] {'z','y','core'}, dimensions={0} | all-to-all | bytes 524288 | tf_op jit(solution)/shard_map/all_to_all | solution.py:312
  (77 shorter events, 41.5 us)
Async XLA Ops:
  4.7 30.9 %all-to-all-start = ((f32[64,2,8,128]{3,2,1,0:T(8,128)}), f32[64,2,8,128]{3,2,1,0:T(8,128)S(1)}, u32[]{:S(2)}, u32[]{:S(2)}) async-start(f32[64,2,8,128]{3,2,1,0:T(8,128)} %get-tuple-element.9.q_ref), calls=%async_computation | async-start | bytes 1048576 | tf_op jit(solution)/shard_map/all_to_all | solution.py:292
  24.0 2.8 %collective-permute-start.4 = (f32[6,128]{1,0:T(8,128)S(1)}, f32[6,128]{1,0:T(8,128)S(1)}, u32[]{:S(2)}, u32[]{:S(2)}) collective-permute-start(f32[6,128]{1,0:T(8,128)S(1)} %broadcast_in_dim.45), channel_id=1, source_target_pairs={{0,1},{1,0},{2,3},{3,2},{4,5},{5,4},{6,7},{7,6},{8,9},{9,8},{10,11... | collective-permute-start | bytes 9224 | tf_op jit(solution)/shard_map/ppermute | solution.py:264
  26.8 13.3 %collective-permute-start.5 = (f32[6,128]{1,0:T(8,128)S(1)}, f32[6,128]{1,0:T(8,128)S(1)}, u32[]{:S(2)}, u32[]{:S(2)}) collective-permute-start(f32[6,128]{1,0:T(8,128)S(1)} %broadcast_maximum_fusion), channel_id=1, source_target_pairs={{0,2},{1,3},{2,0},{3,1},{4,6},{5,7},{6,4},{7,5},{8,10},{9,11},{10,... | collective-permute-start | bytes 9224 | tf_op jit(solution)/shard_map/ppermute | solution.py:264
  36.8 8.1 %all-to-all-start.1 = ((f32[4,2,32,128]{3,2,1,0:T(8,128)}), f32[4,2,32,128]{3,2,1,0:T(8,128)S(1)}, u32[]{:S(2)}, u32[]{:S(2)}) async-start(f32[4,2,32,128]{3,2,1,0:T(8,128)} %shard_map.86), calls=%async_computation.1 | async-start | bytes 262144 | tf_op jit(solution)/shard_map/all_to_all | solution.py:294
  44.9 12.2 %collective-permute-start.3 = (f32[4,2,32,128]{3,2,1,0:T(8,128)S(1)}, f32[4,2,32,128]{3,2,1,0:T(8,128)S(1)}, u32[]{:S(2)}, u32[]{:S(2)}) collective-permute-start(f32[4,2,32,128]{3,2,1,0:T(8,128)S(1)} %all-to-all-done.1.refs_3_.k0), channel_id=1, source_target_pairs={{32,0},{36,4},{64,32},{68,36},{96,64},{100,68},{128,96},{132,100},... | collective-permute-start | bytes 393224 | tf_op jit(solution)/shard_map/ppermute | solution.py:256
  46.2 10.9 %collective-permute-start.2 = (f32[4,2,32,128]{3,2,1,0:T(8,128)S(1)}, f32[4,2,32,128]{3,2,1,0:T(8,128)S(1)}, u32[]{:S(2)}, u32[]{:S(2)}) collective-permute-start(f32[4,2,32,128]{3,2,1,0:T(8,128)S(1)} %all-to-all-done.1.refs_3_.k0), channel_id=1, source_target_pairs={{4,0},{32,4},{36,32},{64,36},{68,64},{96,68},{100,96},{128,100},{1... | collective-permute-start | bytes 393224 | tf_op jit(solution)/shard_map/ppermute | solution.py:256
  50.6 6.5 %collective-permute-start.1 = (f32[4,2,32,128]{3,2,1,0:T(8,128)S(1)}, f32[4,2,32,128]{3,2,1,0:T(8,128)S(1)}, u32[]{:S(2)}, u32[]{:S(2)}) collective-permute-start(f32[4,2,32,128]{3,2,1,0:T(8,128)S(1)} %all-to-all-done.1.refs_3_.k0), channel_id=1, source_target_pairs={{0,4},{4,32},{32,36},{36,64},{64,68},{68,96},{96,100},{100,128},{1... | collective-permute-start | bytes 393224 | tf_op jit(solution)/shard_map/ppermute | solution.py:256
  54.8 4.9 %collective-permute-start = (f32[4,2,32,128]{3,2,1,0:T(8,128)S(1)}, f32[4,2,32,128]{3,2,1,0:T(8,128)S(1)}, u32[]{:S(2)}, u32[]{:S(2)}) collective-permute-start(f32[4,2,32,128]{3,2,1,0:T(8,128)S(1)} %all-to-all-done.1.refs_3_.k0), channel_id=1, source_target_pairs={{0,32},{4,36},{32,64},{36,68},{64,96},{68,100},{96,128},{100,132},... | collective-permute-start | bytes 393224 | tf_op jit(solution)/shard_map/ppermute | solution.py:256
  65.6 12.6 %collective-permute-start.9 = (f32[2,4,32,128]{3,2,1,0:T(8,128)S(1)}, f32[2,4,32,128]{3,2,1,0:T(8,128)S(1)}, u32[]{:S(2)}, u32[]{:S(2)}) collective-permute-start(f32[2,4,32,128]{3,2,1,0:T(8,128)S(1)} %shard_map.88.refs_3_.k1), channel_id=1, source_target_pairs={{32,0},{36,4},{64,32},{68,36},{96,64},{100,68},{128,96},{132,100},... | collective-permute-start | bytes 393224 | tf_op jit(solution)/shard_map/ppermute | solution.py:256
  66.9 11.3 %collective-permute-start.8 = (f32[2,4,32,128]{3,2,1,0:T(8,128)S(1)}, f32[2,4,32,128]{3,2,1,0:T(8,128)S(1)}, u32[]{:S(2)}, u32[]{:S(2)}) collective-permute-start(f32[2,4,32,128]{3,2,1,0:T(8,128)S(1)} %shard_map.88.refs_3_.k1), channel_id=1, source_target_pairs={{4,0},{32,4},{36,32},{64,36},{68,64},{96,68},{100,96},{128,100},{1... | collective-permute-start | bytes 393224 | tf_op jit(solution)/shard_map/ppermute | solution.py:256
  69.9 8.3 %collective-permute-start.7 = (f32[2,4,32,128]{3,2,1,0:T(8,128)S(1)}, f32[2,4,32,128]{3,2,1,0:T(8,128)S(1)}, u32[]{:S(2)}, u32[]{:S(2)}) collective-permute-start(f32[2,4,32,128]{3,2,1,0:T(8,128)S(1)} %shard_map.88.refs_3_.k1), channel_id=1, source_target_pairs={{0,4},{4,32},{32,36},{36,64},{64,68},{68,96},{96,100},{100,128},{1... | collective-permute-start | bytes 393224 | tf_op jit(solution)/shard_map/ppermute | solution.py:256
  74.5 6.3 %collective-permute-start.6 = (f32[2,4,32,128]{3,2,1,0:T(8,128)S(1)}, f32[2,4,32,128]{3,2,1,0:T(8,128)S(1)}, u32[]{:S(2)}, u32[]{:S(2)}) collective-permute-start(f32[2,4,32,128]{3,2,1,0:T(8,128)S(1)} %shard_map.88.refs_3_.k1), channel_id=1, source_target_pairs={{0,32},{4,36},{32,64},{36,68},{64,96},{68,100},{96,128},{100,132},... | collective-permute-start | bytes 393224 | tf_op jit(solution)/shard_map/ppermute | solution.py:256
  81.7 11.6 %collective-permute-start.13 = (f32[4,32,128]{2,1,0:T(8,128)S(1)}, f32[4,32,128]{2,1,0:T(8,128)S(1)}, u32[]{:S(2)}, u32[]{:S(2)}) collective-permute-start(f32[4,32,128]{2,1,0:T(8,128)S(1)} %slice_bitcast_fusion.refs_3_), channel_id=1, source_target_pairs={{32,0},{36,4},{64,32},{68,36},{96,64},{100,68},{128,96},{132,100},... | collective-permute-start | bytes 196616 | tf_op jit(solution)/shard_map/ppermute | solution.py:256
  83.0 10.3 %collective-permute-start.12 = (f32[4,32,128]{2,1,0:T(8,128)S(1)}, f32[4,32,128]{2,1,0:T(8,128)S(1)}, u32[]{:S(2)}, u32[]{:S(2)}) collective-permute-start(f32[4,32,128]{2,1,0:T(8,128)S(1)} %slice_bitcast_fusion.refs_3_), channel_id=1, source_target_pairs={{4,0},{32,4},{36,32},{64,36},{68,64},{96,68},{100,96},{128,100},{1... | collective-permute-start | bytes 196616 | tf_op jit(solution)/shard_map/ppermute | solution.py:256
  84.9 8.4 %collective-permute-start.11 = (f32[4,32,128]{2,1,0:T(8,128)S(1)}, f32[4,32,128]{2,1,0:T(8,128)S(1)}, u32[]{:S(2)}, u32[]{:S(2)}) collective-permute-start(f32[4,32,128]{2,1,0:T(8,128)S(1)} %slice_bitcast_fusion.refs_3_), channel_id=1, source_target_pairs={{0,4},{4,32},{32,36},{36,64},{64,68},{68,96},{96,100},{100,128},{1... | collective-permute-start | bytes 196616 | tf_op jit(solution)/shard_map/ppermute | solution.py:256
  89.3 5.3 %collective-permute-start.10 = (f32[4,32,128]{2,1,0:T(8,128)S(1)}, f32[4,32,128]{2,1,0:T(8,128)S(1)}, u32[]{:S(2)}, u32[]{:S(2)}) collective-permute-start(f32[4,32,128]{2,1,0:T(8,128)S(1)} %slice_bitcast_fusion.refs_3_), channel_id=1, source_target_pairs={{0,32},{4,36},{32,64},{36,68},{64,96},{68,100},{96,128},{100,132},... | collective-permute-start | bytes 196616 | tf_op jit(solution)/shard_map/ppermute | solution.py:256
  96.3 1.2 collective-permute-start.14
  97.5 9.8 %collective-permute-start.15 = (f32[32,128]{1,0:T(8,128)S(1)}, f32[32,128]{1,0:T(8,128)S(1)}, u32[]{:S(2)}, u32[]{:S(2)}) collective-permute-start(f32[32,128]{1,0:T(8,128)S(1)} %add.76), channel_id=1, source_target_pairs={{0,1},{1,0},{2,3},{3,2},{4,5},{5,4},{6,7},{7,6},{8,9},{9,8},{10,11... | collective-permute-start | bytes 49160 | tf_op jit(solution)/shard_map/ppermute | solution.py:264
  107.3 4.1 %collective-permute-start.16 = (f32[32,128]{1,0:T(8,128)S(1)}, f32[32,128]{1,0:T(8,128)S(1)}, u32[]{:S(2)}, u32[]{:S(2)}) collective-permute-start(f32[32,128]{1,0:T(8,128)S(1)} %add.77), channel_id=1, source_target_pairs={{0,2},{1,3},{2,0},{3,1},{4,6},{5,7},{6,4},{7,5},{8,10},{9,11},{10,... | collective-permute-start | bytes 49160 | tf_op jit(solution)/shard_map/ppermute | solution.py:264
  111.4 2.6 %collective-permute-start.17 = (f32[32,128]{1,0:T(8,128)S(1)}, f32[32,128]{1,0:T(8,128)S(1)}, u32[]{:S(2)}, u32[]{:S(2)}) collective-permute-start(f32[32,128]{1,0:T(8,128)S(1)} %add.78), channel_id=1, source_target_pairs={{0,8},{8,0},{16,24},{24,16},{1,9},{9,1},{17,25},{25,17},{2,10},{10... | collective-permute-start | bytes 49160 | tf_op jit(solution)/shard_map/ppermute | solution.py:264
  114.0 4.1 %collective-permute-start.18 = (f32[32,128]{1,0:T(8,128)S(1)}, f32[32,128]{1,0:T(8,128)S(1)}, u32[]{:S(2)}, u32[]{:S(2)}) collective-permute-start(f32[32,128]{1,0:T(8,128)S(1)} %add.79), channel_id=1, source_target_pairs={{0,16},{8,24},{16,0},{24,8},{1,17},{9,25},{17,1},{25,9},{2,18},{10... | collective-permute-start | bytes 49160 | tf_op jit(solution)/shard_map/ppermute | solution.py:264
  118.1 2.6 %collective-permute-start.19 = (f32[32,128]{1,0:T(8,128)S(1)}, f32[32,128]{1,0:T(8,128)S(1)}, u32[]{:S(2)}, u32[]{:S(2)}) collective-permute-start(f32[32,128]{1,0:T(8,128)S(1)} %add.80), channel_id=1, source_target_pairs={{0,32},{32,0},{64,96},{96,64},{128,160},{160,128},{192,224},{224,1... | collective-permute-start | bytes 49160 | tf_op jit(solution)/shard_map/ppermute | solution.py:264
  120.7 3.7 %collective-permute-start.20 = (f32[32,128]{1,0:T(8,128)S(1)}, f32[32,128]{1,0:T(8,128)S(1)}, u32[]{:S(2)}, u32[]{:S(2)}) collective-permute-start(f32[32,128]{1,0:T(8,128)S(1)} %add.81), channel_id=1, source_target_pairs={{0,64},{32,96},{64,0},{96,32},{128,192},{160,224},{192,128},{224,1... | collective-permute-start | bytes 49160 | tf_op jit(solution)/shard_map/ppermute | solution.py:264
  124.4 6.5 %collective-permute-start.21 = (f32[32,128]{1,0:T(8,128)S(1)}, f32[32,128]{1,0:T(8,128)S(1)}, u32[]{:S(2)}, u32[]{:S(2)}) collective-permute-start(f32[32,128]{1,0:T(8,128)S(1)} %add.82), channel_id=1, source_target_pairs={{0,128},{32,160},{64,192},{96,224},{128,0},{160,32},{192,64},{224,... | collective-permute-start | bytes 49160 | tf_op jit(solution)/shard_map/ppermute | solution.py:264
  (8 other events, 63.5 us)

commit v2 on v1

v2 whole, which is shorter than its diff:
```python
import math

import jax
import jax.numpy as jnp
from jax import lax
from jax.experimental import pallas as pl
from jax.experimental.pallas import tpu as pltpu
from jax.sharding import Mesh
from jax.sharding import PartitionSpec as P

HI = lax.Precision.HIGHEST
SEC = ("z", "y", "core")
GROUP = ("y", "core")
RING = ("z", "xs")
SECTORS = 512
NT = (((1,), (1,)), ((), ()))
TN = (((0,), (0,)), ((), ()))
VMEM_LIMIT = 32 * 1024 * 1024


def f32(*shape):
    return jax.ShapeDtypeStruct(shape, jnp.float32)


def dot(a, b, dims=(((1,), (0,)), ((), ()))):
    return lax.dot_general(a, b, dims, precision=HI, preferred_element_type=jnp.float32)


def call(kernel, out, *args, scalar=None, **kw):
    whole = pl.BlockSpec(memory_space=pltpu.VMEM)
    specs = [whole] * len(args)
    if scalar is not None:
        specs = [pl.BlockSpec(memory_space=pltpu.SMEM)] + specs
        args = (scalar,) + args
    return pl.pallas_call(
        kernel,
        out_shape=out,
        in_specs=specs,
        out_specs=jax.tree.map(lambda _: whole, out),
        compiler_params=pltpu.CompilerParams(vmem_limit_bytes=VMEM_LIMIT),
        **kw,
    )(*args)


def turned(pair, flip):
    return pair + flip * (7 - 2 * pair)


def pack_kernel(flip_ref, q_ref, p_ref, out_ref):
    flip = flip_ref[0]
    for pair in range(8):
        place = turned(pair, flip) * 8
        lanes = pl.ds(pair * 256, 256)
        for col in range(4):
            out_ref[place + col] = q_ref[:, col, lanes]
            out_ref[place + 4 + col] = p_ref[:, col, lanes]


def raw_kernel(q_ref, p_ref, gram_ref):
    total = jnp.zeros((8, 8), jnp.float32)
    for s in range(8):
        rows = jnp.concatenate([q_ref[s], p_ref[s]], axis=0)
        total += dot(rows, rows, NT)
    gram_ref[...] = jnp.zeros((8, 128), jnp.float32)
    gram_ref[:, 0:8] = total


def stats_kernel(pair_ref, s_ref, c_ref, out_ref, own_ref):
    step = pl.program_id(0)
    row = lax.broadcasted_iota(jnp.int32, (128, 128), 0)
    col = lax.broadcasted_iota(jnp.int32, (128, 128), 1)
    big = jnp.float32(3.0e38)
    found = []
    for ref in (s_ref, c_ref):
        largest = jnp.max(jnp.abs(ref[0]), axis=0)
        largest = jnp.max(largest.reshape(16, 8, 128), axis=0)
        middle = ref[0, 2]
        top = jnp.max(jnp.where(row == col, middle, -big).reshape(16, 8, 128), axis=0)
        low = jnp.max(jnp.where(row == col, -middle, -big).reshape(16, 8, 128), axis=0)
        found += [largest, top, low]

    @pl.when(step == 0)
    def _():
        for i, v in enumerate(found):
            out_ref[i] = v

    @pl.when(step > 0)
    def _():
        for i, v in enumerate(found):
            out_ref[i] = jnp.maximum(out_ref[i], v)

    for half in range(2):

        @pl.when(step == pair_ref[0] * 2 + half)
        def _():
            for k in range(5):
                lanes = pl.ds(k * 128, 128)
                own_ref[half, 0:128, lanes] = s_ref[0, k]
                own_ref[half, 128:256, lanes] = c_ref[0, k]


def forward_kernel(f_ref, r_ref, out_ref):
    out_ref[...] = dot(f_ref[...], r_ref[...].reshape(SECTORS, 256)).reshape(8, 16, 256)


def apply_kernel(shift, left_ref, own_ref, right_ref, w_ref, f_ref, k_ref, *out_refs):
    count = own_ref.shape[0]
    rows = count * 16
    own = own_ref[...].reshape(rows, 256)
    wide = jnp.concatenate(
        [left_ref[...].reshape(rows, 256), own, right_ref[...].reshape(rows, 256)], axis=1
    )
    factor = f_ref[...][None]
    sigma, inverse = k_ref[0:1, :][None], k_ref[1:2, :][None]
    for half in range(2):
        both = dot(wide[:, half * 128 : half * 128 + 640], w_ref[half], NT)
        value = both[:, :128].reshape(count, 16, 128)
        value = value + factor * both[:, 128:].reshape(count, 16, 128)
        if shift:
            mine = own[:, half * 128 : half * 128 + 128].reshape(count, 16, 128)
            value = value - sigma * mine
        value = value * inverse
        size = count // len(out_refs)
        for i, ref in enumerate(out_refs):
            ref[:, :, half * 128 : half * 128 + 128] = value[i * size : (i + 1) * size]


def share_kernel(k0, k1, k2x, k2y, k3, raw_ref, out_ref):
    total = jnp.zeros((32, 32), jnp.float32)
    for r in range(16):
        rows = jnp.concatenate(
            [k0[:, r, :], k1[:, r, :], k2x[:, r, :], k2y[:, r, :], k3[:, r, :], jnp.zeros((4, 256), jnp.float32)],
            axis=0,
        )
        total += dot(rows, rows, NT)
    first = jnp.concatenate([raw_ref[:, 0:8], total[0:8, 8:32]], axis=1)
    packed = jnp.concatenate([first, total[8:16], total[16:24], total[24:32]], axis=1)
    group = lax.broadcasted_iota(jnp.int32, (16, 128), 1) // 32
    sets = (
        [k1[c] for c in range(4)],
        [k1[4 + c] for c in range(4)],
        [k2x[c] for c in range(4)],
        [k2y[c] for c in range(4)],
        [k3[c] for c in range(4)],
    )
    for m, columns in enumerate(sets):
        for half in range(2):
            tiles = [v[:, half * 128 : half * 128 + 128] for v in columns]
            for q in range(4):
                value = None
                for c in range(4):
                    by = (c - q) % 4 * 32
                    moved = pltpu.roll(tiles[c], by, 1) if by else tiles[c]
                    value = moved if value is None else jnp.where(group == c, moved, value)
                out_ref[half * 4 + q, m * 16 : m * 16 + 16] = value
    for d in range(8):
        out_ref[d, 80:88] = packed


def total_kernel(v_ref, out_ref):
    total = v_ref[0, 80:88]
    for d in range(1, 8):
        total += v_ref[d, 80:88]
    for d in range(32):
        out_ref[d] = total


def mixed(weights, rows):
    total = weights[:, 0:1] * rows[0:1, :]
    for l in range(1, 4):
        total += weights[:, l : l + 1] * rows[l : l + 1, :]
    return total


def products(a, b):
    return jnp.concatenate(
        [jnp.sum(a * b[l : l + 1, :], axis=1, keepdims=True) for l in range(4)], axis=1
    )


def solve_kernel(g_ref, b_ref, k_ref, v_ref, f_ref, image_ref, coef_ref, alpha_ref, beta_ref):
    lane = lax.broadcasted_iota(jnp.int32, (4, 128), 1)
    row = lax.broadcasted_iota(jnp.int32, (4, 128), 0)
    sigma, scale = k_ref[0:1, :], k_ref[2:3, :]
    packed = g_ref[0]
    for d in range(1, 32):
        packed += g_ref[d]
    narrow = lax.broadcasted_iota(jnp.int32, (8, 128), 1) < 32
    gram = jnp.concatenate(
        [
            jnp.where(narrow, packed if q == 0 else pltpu.roll(packed, 128 - 32 * q, 1), 0.0)
            for q in range(4)
        ],
        axis=0,
    )
    cur = (lane == row).astype(jnp.float32)
    prev = (lane == row + 4).astype(jnp.float32)
    cur_g, prev_g = gram[0:4], gram[4:8]
    coupling = b_ref[...]
    one_row = lax.broadcasted_iota(jnp.int32, (4, 1), 0)
    small_row = lax.broadcasted_iota(jnp.int32, (4, 4), 0)
    small_col = lax.broadcasted_iota(jnp.int32, (4, 4), 1)
    for step in range(3):
        moved = scale * pltpu.roll(jnp.where(lane < 20, cur, 0.0), 8, 1)
        moved += sigma * jnp.where(lane >= 8, cur, 0.0)
        w = moved - mixed(coupling, prev)
        w_g = dot(moved[:, 0:32], gram) - mixed(coupling, prev_g)
        across = products(w_g, cur)
        alpha_ref[step] = products(cur_g, w)
        r = w - mixed(across, cur)
        r_g = w_g - mixed(across, cur_g)
        square = products(r_g, r)
        pivots = jnp.zeros((4, 1), jnp.float32)
        for i in range(4):
            pivot = square[i : i + 1, i : i + 1]
            pivots = jnp.where(one_row == i, pivot, pivots)
            if i < 3:
                times = jnp.where(one_row > i, square[:, i : i + 1] / pivot, 0.0)
                r = r - times * r[i : i + 1, :]
                r_g = r_g - times * r_g[i : i + 1, :]
                square = square - times * square[i : i + 1, :]
        root = 1.0 / jnp.sqrt(pivots)
        upper = jnp.where(small_col >= small_row, square * root, 0.0)
        beta_ref[step] = upper
        prev, prev_g, coupling = cur, cur_g, upper
        cur, cur_g = r * root, r_g * root
    coef_ref[...] = cur
    spread = (lane // 32 == row).astype(jnp.float32)
    weights = dot(cur, spread, TN)
    same = lax.broadcasted_iota(jnp.int32, (32, 128), 1) % 32 == lax.broadcasted_iota(jnp.int32, (32, 128), 0)
    mixing = jnp.concatenate([jnp.where(same, weights[8 + k : 9 + k, :], 0.0) for k in range(20)], axis=0)
    vectors = jnp.concatenate([v_ref[:, m * 16 : m * 16 + 16].reshape(128, 128) for m in range(5)], axis=1)
    field = dot(vectors, mixing)
    image_ref[...] = dot(f_ref[...], field, TN).reshape(64, 8, 128)


def base_kernel(flip_ref, q_ref, coef_ref, out_ref):
    flip = flip_ref[0]
    coef = coef_ref[...]
    scalars = [
        [coef[c : c + 1, k : k + 1] + jnp.zeros((8, 256), jnp.float32) for k in range(8)]
        for c in range(4)
    ]
    for pair in range(8):
        place = turned(pair, flip) * 8
        tiles = [q_ref[place + k] for k in range(8)]
        for c in range(4):
            total = scalars[c][0] * tiles[0]
            for k in range(1, 8):
                total += scalars[c][k] * tiles[k]
            out_ref[pair, c] = total


def last_kernel(flip_ref, r_ref, base_ref, out_ref):
    flip = flip_ref[0]
    group = lax.broadcasted_iota(jnp.int32, (8, 128), 1) // 32
    for pair in range(8):
        place = turned(pair, flip) * 8
        for half in range(2):
            tiles = [r_ref[place + half * 4 + q] for q in range(4)]
            for c in range(4):
                value = None
                for q in range(4):
                    by = (q - c) % 4 * 32
                    moved = pltpu.roll(tiles[q], by, 1) if by else tiles[q]
                    value = moved if value is None else jnp.where(group == q, moved, value)
                value += base_ref[pair, c, :, half * 128 : half * 128 + 128]
                out_ref[:, c, pl.ds(pair * 256 + half * 128, 128)] = value


def table(assign):
    harmonic = jnp.repeat(assign, 2)
    parity = jnp.arange(harmonic.shape[0], dtype=jnp.int32) % 2
    sectors = jnp.arange(SECTORS, dtype=jnp.int32)
    phases = (harmonic[:, None] * sectors[None, :] + 128 * parity[:, None]) % SECTORS
    weights = jnp.where(harmonic == 0, math.sqrt(1.0 / SECTORS), math.sqrt(2.0 / SECTORS))
    weights = jnp.where((harmonic == 0) & (parity == 1), 0.0, weights).astype(jnp.float32)
    return jnp.cos(2.0 * math.pi / SECTORS * phases.astype(jnp.float32)) * weights[:, None]


def ring_place(pair):
    slab, at = pair // 8 % 4, pair % 8
    return (at if slab % 2 == 0 else 7 - at) * 4 + slab


def beside(value):
    after = [(ring_place(i), ring_place(i + 1)) for i in range(32)]
    before = [(j, i) for i, j in after]
    return lax.ppermute(value, RING, after), lax.ppermute(value, RING, before)


def highest(value, step):
    return jnp.maximum(value, lax.ppermute(value, "xs", [(i, i ^ step) for i in range(4)]))


def per_device(q_block, q_prev, b_prev, stiff_blocks, couple_blocks, block_cols, assign):
    flip = (lax.axis_index("xs") % 2).astype(jnp.int32).reshape(1)
    pair = turned(lax.axis_index("z"), flip)
    group = lax.axis_index("y") * 2 + lax.axis_index("core")

    packed = call(pack_kernel, f32(64, 8, 256), q_block, q_prev, scalar=flip)
    received = lax.all_to_all(packed, SEC, 0, 0, tiled=True)

    forward = table(assign)
    factors = jnp.cos(2.0 * math.pi / SECTORS * assign.astype(jnp.float32))
    mine = lax.dynamic_slice_in_dim(factors, group * 8, 8)
    factor = jnp.broadcast_to(jnp.repeat(mine, 2)[:, None], (16, 128))
    raw = call(raw_kernel, f32(8, 128), q_block, q_prev)
    found, own = pl.pallas_call(
        stats_kernel,
        out_shape=(f32(6, 8, 128), f32(2, 256, 640)),
        grid_spec=pltpu.PrefetchScalarGridSpec(
            num_scalar_prefetch=1,
            grid=(16,),
            in_specs=[pl.BlockSpec((1, 5, 128, 128), lambda i, p: (i, 0, 0, 0))] * 2,
            out_specs=(
                pl.BlockSpec((6, 8, 128), lambda i, p: (0, 0, 0)),
                pl.BlockSpec((2, 256, 640), lambda i, p: (0, 0, 0)),
            ),
        ),
        compiler_params=pltpu.CompilerParams(vmem_limit_bytes=VMEM_LIMIT),
    )(pair, stiff_blocks, couple_blocks)
    found = jnp.broadcast_to(jnp.max(found, axis=(1, 2))[:, None], (6, 128))
    found = highest(highest(found, 1), 2)
    sigma = 0.5 * (found[1] - found[2]) + jnp.mean(factors) * (0.5 * (found[4] - found[5]))
    scale = found[0] + found[3]
    scale = jnp.where(scale > 0, scale, 1.0)
    scales = jnp.stack([sigma, 1.0 / scale, scale] + [scale] * 5)

    spectrum = call(forward_kernel, f32(8, 16, 256), forward, received)
    k0 = lax.all_to_all(spectrum, GROUP, 0, 0, tiled=True)

    def operator(value, shift, out):
        left, right = beside(value)
        return call(
            lambda *refs: apply_kernel(shift, *refs), out, left, value, right, own, factor, scales
        )

    (k1,) = operator(k0, False, (f32(8, 16, 256),))
    k2x, k2y = operator(k1, True, (f32(4, 16, 256), f32(4, 16, 256)))
    (k3,) = operator(k2x, True, (f32(4, 16, 256),))

    shares = call(share_kernel, f32(8, 88, 128), k0, k1, k2x, k2y, k3, raw)
    vectors = lax.all_to_all(shares, GROUP, 0, 0, tiled=True)
    grams = lax.all_to_all(call(total_kernel, f32(32, 8, 128), vectors), RING, 0, 0, tiled=True)
    image, coef, alphas, betas = call(
        solve_kernel,
        (f32(64, 8, 128), f32(4, 128), f32(3, 4, 4), f32(3, 4, 4)),
        grams, b_prev, scales, vectors, forward,
    )
    back = lax.all_to_all(image, SEC, 0, 0, tiled=True)
    base = call(base_kernel, f32(8, 4, 8, 256), packed, coef, scalar=flip)
    out = call(last_kernel, f32(8, 4, 2048), back, base, scalar=flip)
    return out, alphas, betas


def solution(mesh):
    fine = Mesh(mesh.devices.reshape(8, 4, 2, 4), ("z", "y", "core", "xs"))
    in_specs = (
        P(SEC, None, "xs"),
        P(SEC, None, "xs"),
        P(),
        P("xs", None, None, None),
        P("xs", None, None, None),
        P("xs", None),
        P(),
    )
    out_specs = (P(SEC, None, "xs"), P(), P())
    return jax.shard_map(
        per_device, mesh=fine, in_specs=in_specs, out_specs=out_specs, check_vma=False
    )
```

time: 171 us -> 122 us (0.71)
  starting transfers between devices: 71 us -> 36.6 us
  waiting for transfers between devices: 36.1 us -> 26.6 us
  local copies, waits for them, and re-layouts: 12.5 us -> 7.49 us
  Pallas kernels: 13.2 us -> 15.9 us
    ppermute x22 -> x8, starting transfers between devices: 54.6 us -> 12.4 us  [the longest x6 8.46 us: beside(): return (lax.ppermute(value, RING, after), lax.ppermute(value, RING, before))]
    ppermute x22 -> x8, waiting for transfers between devices: 26.9 us -> 5.37 us  [the longest x6 5.14 us: beside(): return (lax.ppermute(value, RING, after), lax.ppermute(value, RING, before))]
    all_to_all x1 -> x2, waiting for transfers between devices: 4.71 us -> 17.2 us  [the longest x1 12 us: per_device(): back = lax.all_to_all(image, SEC, 0, 0, tiled=True)]
    all_to_all x1 -> x2, starting transfers between devices: 3.33 us -> 11 us  [the longest x1 6.34 us: per_device(): back = lax.all_to_all(image, SEC, 0, 0, tiled=True)]
    unnamed x16, local copies, waits for them, and re-layouts: 11.8 us -> 6.88 us
    pallas_call x10 -> x12, Pallas kernels: 13.2 us -> 15.9 us  [the longest x11 14.6 us: call(): pl.pallas_call(kernel, out_shape=out, in_specs=specs, out_specs=jax.tree....]
  transfers between devices with their start and end apart: 24 -> 11, of which waited for: 14 -> 7; matrix products, arithmetic and copies ran while one was open for 2% -> 2% of each run, Pallas kernels for 1% -> 4%
where the time goes in v2:
time: 122 us
  starting transfers between devices  36.6 us (30%)
  blocking collectives  31.8 us (26%)
  waiting for transfers between devices  26.6 us (22%)
  Pallas kernels  15.9 us (13%)
  local copies, waits for them, and re-layouts  7.49 us (6%)
  other arithmetic  2 us (2%)
  between operations  1.43 us (1%)
    all_to_all x1, blocking collectives, per_device(): lax.all_to_all(call(total_kernel, f32(32, 8, 128), vectors), RING, 0, 0,...  17.6 us
    pallas_call x11, Pallas kernels, call(): pl.pallas_call(kernel, out_shape=out, in_specs=specs, out_specs=jax.tree....  14.6 us
    all_to_all x1, blocking collectives, per_device(): vectors = lax.all_to_all(shares, GROUP, 0, 0, tiled=True)  14.2 us
    all_to_all x1, starting transfers between devices, per_device(): received = lax.all_to_all(packed, SEC, 0, 0, tiled=True)  13.2 us
    all_to_all x1, waiting for transfers between devices, per_device(): back = lax.all_to_all(image, SEC, 0, 0, tiled=True)  12 us
    ppermute x6, starting transfers between devices, beside(): return (lax.ppermute(value, RING, after), lax.ppermute(value, RING, before))  8.46 us
    unnamed x16, local copies, waits for them, and re-layouts  6.88 us
    all_to_all x1, starting transfers between devices, per_device(): back = lax.all_to_all(image, SEC, 0, 0, tiled=True)  6.34 us
  transfers between devices with their start and end apart: 11, of which 7 were waited for; matrix products, arithmetic and copies ran while one was open for 2% of the time, Pallas kernels for 4%

profile of v2, /device:TPU:1, one launch (start us, length us, event | category | flops | bytes accessed | tf_op | source)
XLA Modules:
  0.0 121.8 jit_solution(17004207109798045286)
XLA Ops:
  3.5 13.2 %all-to-all-start = ((f32[64,8,256]{2,1,0:T(8,128)}), f32[64,8,256]{2,1,0:T(8,128)S(1)}, u32[]{:S(2)}, u32[]{:S(2)}) async-start(f32[64,8,256]{2,1,0:T(8,128)} %shard_map.85.q_ref), calls=%async_computation | async-start | bytes 1048576 | tf_op jit(solution)/shard_map/all_to_all | solution.py:302
  16.7 2.5 %copy-done = f32[16,5,128,128]{3,2,1,0:T(8,128)S(1)} copy-done((f32[16,5,128,128]{3,2,1,0:T(8,128)S(1)}, f32[16,5,128,128]{3,2,1,0:T(8,128)}, u32[]{:S(2)}) %copy-start) | copy-done | bytes 5242904
  19.2 2.5 %copy-done.1 = f32[16,5,128,128]{3,2,1,0:T(8,128)S(1)} copy-done((f32[16,5,128,128]{3,2,1,0:T(8,128)S(1)}, f32[16,5,128,128]{3,2,1,0:T(8,128)}, u32[]{:S(2)}) %copy-start.1) | copy-done | bytes 5242904
  21.7 1.3 %shard_map.87 = (f32[6,8,128]{2,1,0:T(8,128)S(1)}, f32[2,256,640]{2,1,0:T(8,128)S(1)}) custom-call(s32[1]{0:T(128)S(6)} %add.60.pair_ref, f32[16,5,128,128]{3,2,1,0:T(8,128)S(1)} %copy-done, f32[16,5,128,128]{3,2,1,0:T(8,128)S(1)} %copy-done.1), custom_call_target="tpu_custom_call" | custom-call | tf_op jit(solution)/shard_map/pallas_call | solution.py:309
  23.2 1.2 collective-permute-start.2
  26.0 2.7 %collective-permute-start.3 = (f32[6,128]{1,0:T(8,128)S(1)}, f32[6,128]{1,0:T(8,128)S(1)}, u32[]{:S(2)}, u32[]{:S(2)}) collective-permute-start(f32[6,128]{1,0:T(8,128)S(1)} %broadcast_maximum_fusion), channel_id=1, source_target_pairs={{0,2},{1,3},{2,0},{3,1},{4,6},{5,7},{6,4},{7,5},{8,10},{9,11},{10,... | collective-permute-start | bytes 9224 | tf_op jit(solution)/shard_map/ppermute | solution.py:293
  30.3 4.1 %all-to-all-done.r_ref = f32[64,8,256]{2,1,0:T(8,128)S(1)} async-done(((f32[64,8,256]{2,1,0:T(8,128)}), f32[64,8,256]{2,1,0:T(8,128)S(1)}, u32[]{:S(2)}, u32[]{:S(2)}) %all-to-all-start) | async-done | bytes 524320 | tf_op jit(solution)/shard_map/all_to_all | solution.py:302
  35.5 4.7 %all-to-all-start.1 = ((f32[8,16,256]{2,1,0:T(8,128)}), f32[8,16,256]{2,1,0:T(8,128)S(1)}, u32[]{:S(2)}, u32[]{:S(2)}) async-start(f32[8,16,256]{2,1,0:T(8,128)} %shard_map.86), calls=%async_computation.1 | async-start | bytes 262144 | tf_op jit(solution)/shard_map/all_to_all | solution.py:331
  40.2 5.2 %all-to-all-done.1.refs_1_.k0 = f32[8,16,256]{2,1,0:T(8,128)S(1)} async-done(((f32[8,16,256]{2,1,0:T(8,128)}), f32[8,16,256]{2,1,0:T(8,128)S(1)}, u32[]{:S(2)}, u32[]{:S(2)}) %all-to-all-start.1) | async-done | bytes 131104 | tf_op jit(solution)/shard_map/all_to_all | solution.py:331
  45.8 2.3 %collective-permute-start.1 = (f32[8,16,256]{2,1,0:T(8,128)S(1)}, f32[8,16,256]{2,1,0:T(8,128)S(1)}, u32[]{:S(2)}, u32[]{:S(2)}) collective-permute-start(f32[8,16,256]{2,1,0:T(8,128)S(1)} %all-to-all-done.1.refs_1_.k0), channel_id=1, source_target_pairs={{32,0},{64,32},{96,64},{128,96},{160,128},{192,160},{224,192},{225... | collective-permute-start | bytes 393224 | tf_op jit(solution)/shard_map/ppermute | solution.py:289
  48.1 2.6 %collective-permute-done.refs_0_ = f32[8,16,256]{2,1,0:T(8,128)S(1)} collective-permute-done((f32[8,16,256]{2,1,0:T(8,128)S(1)}, f32[8,16,256]{2,1,0:T(8,128)S(1)}, u32[]{:S(2)}, u32[]{:S(2)}) %collective-permute-start) | collective-permute-done | bytes 131104 | tf_op jit(solution)/shard_map/ppermute | solution.py:289
  50.9 1.4 %shard_map.88.refs_1_.k1 = f32[8,16,256]{2,1,0:T(8,128)S(1)} custom-call(f32[8,16,256]{2,1,0:T(8,128)S(1)} %collective-permute-done.refs_0_, f32[8,16,256]{2,1,0:T(8,128)S(1)} %all-to-all-done.1.refs_1_.k0, f32[8,16,256]{2,1,0:T(8,128)S(1)} %collective-permute-done.1.refs_2_, f32[2,256,640]{2,1,0:T(8,128)S(1)} %get-tuple-element.11.refs_3_, ...), custom_call_target="tpu_custom_call" | custom-call | tf_op jit(solution)/shard_map/pallas_call | solution.py:35
  52.8 2.2 %collective-permute-start.5 = (f32[8,16,256]{2,1,0:T(8,128)S(1)}, f32[8,16,256]{2,1,0:T(8,128)S(1)}, u32[]{:S(2)}, u32[]{:S(2)}) collective-permute-start(f32[8,16,256]{2,1,0:T(8,128)S(1)} %shard_map.88.refs_1_.k1), channel_id=1, source_target_pairs={{32,0},{64,32},{96,64},{128,96},{160,128},{192,160},{224,192},{225... | collective-permute-start | bytes 393224 | tf_op jit(solution)/shard_map/ppermute | solution.py:289
  55.0 2.4 %collective-permute-done.4.refs_0_ = f32[8,16,256]{2,1,0:T(8,128)S(1)} collective-permute-done((f32[8,16,256]{2,1,0:T(8,128)S(1)}, f32[8,16,256]{2,1,0:T(8,128)S(1)}, u32[]{:S(2)}, u32[]{:S(2)}) %collective-permute-start.4) | collective-permute-done | bytes 131104 | tf_op jit(solution)/shard_map/ppermute | solution.py:289
  57.3 1.4 %shard_map.89 = (f32[4,16,256]{2,1,0:T(8,128)S(1)}, f32[4,16,256]{2,1,0:T(8,128)S(1)}) custom-call(f32[8,16,256]{2,1,0:T(8,128)S(1)} %collective-permute-done.4.refs_0_, f32[8,16,256]{2,1,0:T(8,128)S(1)} %shard_map.88.refs_1_.k1, f32[8,16,256]{2,1,0:T(8,128)S(1)} %collective-permute-done.5.refs_2_, f32[2,256,640]{2,1,0:T(8,128)S(1)} %get-tuple-element.11.refs_3_, ...), custom_call_target="tpu_custom_call" | custom-call | tf_op jit(solution)/shard_map/pallas_call | solution.py:35
  59.0 2.7 %collective-permute-start.7 = (f32[4,16,256]{2,1,0:T(8,128)S(1)}, f32[4,16,256]{2,1,0:T(8,128)S(1)}, u32[]{:S(2)}, u32[]{:S(2)}) collective-permute-start(f32[4,16,256]{2,1,0:T(8,128)S(1)} %get-tuple-element.13.refs_1_.k2x), channel_id=1, source_target_pairs={{32,0},{64,32},{96,64},{128,96},{160,128},{192,160},{224,192},{225... | collective-permute-start | bytes 196616 | tf_op jit(solution)/shard_map/ppermute | solution.py:289
  61.7 1.2 %shard_map.91.raw_ref = f32[8,128]{1,0:T(8,128)S(1)} custom-call(f32[8,4,2048]{2,1,0:T(4,128)S(1)} %copy-done.3, f32[8,4,2048]{2,1,0:T(4,128)S(1)} %copy-done.5), custom_call_target="tpu_custom_call" | custom-call | tf_op jit(solution)/shard_map/pallas_call | solution.py:35
  63.1 1.4 %shard_map.90.k3 = f32[4,16,256]{2,1,0:T(8,128)S(1)} custom-call(f32[4,16,256]{2,1,0:T(8,128)S(1)} %collective-permute-done.6.refs_0_, f32[4,16,256]{2,1,0:T(8,128)S(1)} %get-tuple-element.13.refs_1_.k2x, f32[4,16,256]{2,1,0:T(8,128)S(1)} %collective-permute-done.7.refs_2_, f32[2,256,640]{2,1,0:T(8,128)S(1)} %get-tuple-element.11.refs_3_, ...), custom_call_target="tpu_custom_call" | custom-call | tf_op jit(solution)/shard_map/pallas_call | solution.py:35
  65.2 14.2 %all_to_all.25.v_ref = f32[8,88,128]{2,1,0:T(8,128)S(1)} all-to-all(f32[8,88,128]{2,1,0:T(8,128)S(1)} %shard_map.92), channel_id=1, replica_groups=mesh['z'=8,'y'=4,'core'=2,'xs'=4] {'y','core'}, dimensions={0} | all-to-all | bytes 720896 | tf_op jit(solution)/shard_map/all_to_all | solution.py:344
  79.4 17.6 %all_to_all.26.g_ref = f32[32,8,128]{2,1,0:T(8,128)S(1)} all-to-all(f32[32,8,128]{2,1,0:T(8,128)S(1)} %shard_map.93), channel_id=1, replica_groups=mesh['z'=8,'y'=4,'core'=2,'xs'=4] {'z','xs'}, dimensions={0} | all-to-all | bytes 262144 | tf_op jit(solution)/shard_map/all_to_all | solution.py:345
  97.0 4.2 %shard_map.94 = (f32[64,8,128]{2,1,0:T(8,128)}, f32[4,128]{1,0:T(4,128)S(1)}, f32[3,4,4]{2,1,0:T(4,128)}, f32[3,4,4]{2,1,0:T(4,128)}) custom-call(f32[32,8,128]{2,1,0:T(8,128)S(1)} %all_to_all.26.g_ref, f32[4,4]{1,0:T(4,128)S(1)} %copy-done.6, f32[8,128]{1,0:T(8,128)S(1)} %stack.2.refs_5_.k_ref, f32[8,88,128]{2,1,0:T(8,128)S(1)} %all_to_all.25.v_ref, ...), custom_call_target="tpu_custom_call" | custom-call | tf_op jit(solution)/shard_map/pallas_call | solution.py:35
  101.2 6.3 %all-to-all-start.4 = ((f32[64,8,128]{2,1,0:T(8,128)}), f32[64,8,128]{2,1,0:T(8,128)S(1)}, u32[]{:S(2)}, u32[]{:S(2)}) async-start(f32[64,8,128]{2,1,0:T(8,128)} %get-tuple-element.15), calls=%async_computation.4 | async-start | bytes 524288 | tf_op jit(solution)/shard_map/all_to_all | solution.py:351
  107.6 1.3 %shard_map.95.base_ref = f32[8,4,8,256]{3,2,1,0:T(8,128)S(1)} custom-call(s32[1]{0:T(128)} %bitcast.flip_ref, f32[64,8,256]{2,1,0:T(8,128)} %shard_map.85.q_ref, f32[4,128]{1,0:T(4,128)S(1)} %get-tuple-element.16.coef_ref), custom_call_target="tpu_custom_call" | custom-call | tf_op jit(solution)/shard_map/pallas_call | solution.py:35
  108.9 12.0 %all-to-all-done.4.r_ref = f32[64,8,128]{2,1,0:T(8,128)S(1)} async-done(((f32[64,8,128]{2,1,0:T(8,128)}), f32[64,8,128]{2,1,0:T(8,128)S(1)}, u32[]{:S(2)}, u32[]{:S(2)}) %all-to-all-start.4) | async-done | bytes 262176 | tf_op jit(solution)/shard_map/all_to_all | solution.py:351
  (44 shorter events, 9.9 us)
Async XLA Ops:
  0.6 1.0 copy-start.2
  1.6 0.9 copy-start.4
  3.5 30.9 %all-to-all-start = ((f32[64,8,256]{2,1,0:T(8,128)}), f32[64,8,256]{2,1,0:T(8,128)S(1)}, u32[]{:S(2)}, u32[]{:S(2)}) async-start(f32[64,8,256]{2,1,0:T(8,128)} %shard_map.85.q_ref), calls=%async_computation | async-start | bytes 1048576 | tf_op jit(solution)/shard_map/all_to_all | solution.py:302
  16.7 2.5 %copy-start = (f32[16,5,128,128]{3,2,1,0:T(8,128)S(1)}, f32[16,5,128,128]{3,2,1,0:T(8,128)}, u32[]{:S(2)}) copy-start(f32[16,5,128,128]{3,2,1,0:T(8,128)} %s_ref.1) | copy-start | bytes 15728644
  19.2 2.5 %copy-start.1 = (f32[16,5,128,128]{3,2,1,0:T(8,128)S(1)}, f32[16,5,128,128]{3,2,1,0:T(8,128)}, u32[]{:S(2)}) copy-start(f32[16,5,128,128]{3,2,1,0:T(8,128)} %c_ref.1) | copy-start | bytes 15728644
  21.7 2.7 %copy-start.7 = (s32[64]{0:T(128)S(1)}, s32[64]{0:T(128)}, u32[]{:S(2)}) copy-start(s32[64]{0:T(128)} %param.12) | copy-start | bytes 772
  21.7 40.1 %copy-start.3 = (f32[8,4,2048]{2,1,0:T(4,128)S(1)}, f32[8,4,2048]{2,1,0:T(4,128)}, u32[]{:S(2)}) copy-start(f32[8,4,2048]{2,1,0:T(4,128)} %q_ref.3) | copy-start | bytes 786436
  21.7 40.1 %copy-start.5 = (f32[8,4,2048]{2,1,0:T(4,128)S(1)}, f32[8,4,2048]{2,1,0:T(4,128)}, u32[]{:S(2)}) copy-start(f32[8,4,2048]{2,1,0:T(4,128)} %p_ref.3) | copy-start | bytes 786436
  23.0 74.1 %copy-start.6 = (f32[4,4]{1,0:T(4,128)S(1)}, f32[4,4]{1,0:T(4,128)}, u32[]{:S(2)}) copy-start(f32[4,4]{1,0:T(4,128)} %b_ref.1) | copy-start | bytes 196
  23.2 2.8 %collective-permute-start.2 = (f32[6,128]{1,0:T(8,128)S(1)}, f32[6,128]{1,0:T(8,128)S(1)}, u32[]{:S(2)}, u32[]{:S(2)}) collective-permute-start(f32[6,128]{1,0:T(8,128)S(1)} %broadcast_in_dim.45), channel_id=1, source_target_pairs={{0,1},{1,0},{2,3},{3,2},{4,5},{5,4},{6,7},{7,6},{8,9},{9,8},{10,11... | collective-permute-start | bytes 9224 | tf_op jit(solution)/shard_map/ppermute | solution.py:293
  26.0 14.1 %collective-permute-start.3 = (f32[6,128]{1,0:T(8,128)S(1)}, f32[6,128]{1,0:T(8,128)S(1)}, u32[]{:S(2)}, u32[]{:S(2)}) collective-permute-start(f32[6,128]{1,0:T(8,128)S(1)} %broadcast_maximum_fusion), channel_id=1, source_target_pairs={{0,2},{1,3},{2,0},{3,1},{4,6},{5,7},{6,4},{7,5},{8,10},{9,11},{10,... | collective-permute-start | bytes 9224 | tf_op jit(solution)/shard_map/ppermute | solution.py:293
  35.5 9.9 %all-to-all-start.1 = ((f32[8,16,256]{2,1,0:T(8,128)}), f32[8,16,256]{2,1,0:T(8,128)S(1)}, u32[]{:S(2)}, u32[]{:S(2)}) async-start(f32[8,16,256]{2,1,0:T(8,128)} %shard_map.86), calls=%async_computation.1 | async-start | bytes 262144 | tf_op jit(solution)/shard_map/all_to_all | solution.py:331
  45.4 5.4 %collective-permute-start = (f32[8,16,256]{2,1,0:T(8,128)S(1)}, f32[8,16,256]{2,1,0:T(8,128)S(1)}, u32[]{:S(2)}, u32[]{:S(2)}) collective-permute-start(f32[8,16,256]{2,1,0:T(8,128)S(1)} %all-to-all-done.1.refs_1_.k0), channel_id=1, source_target_pairs={{0,32},{32,64},{64,96},{96,128},{128,160},{160,192},{192,224},{224... | collective-permute-start | bytes 393224 | tf_op jit(solution)/shard_map/ppermute | solution.py:289
  45.8 5.0 %collective-permute-start.1 = (f32[8,16,256]{2,1,0:T(8,128)S(1)}, f32[8,16,256]{2,1,0:T(8,128)S(1)}, u32[]{:S(2)}, u32[]{:S(2)}) collective-permute-start(f32[8,16,256]{2,1,0:T(8,128)S(1)} %all-to-all-done.1.refs_1_.k0), channel_id=1, source_target_pairs={{32,0},{64,32},{96,64},{128,96},{160,128},{192,160},{224,192},{225... | collective-permute-start | bytes 393224 | tf_op jit(solution)/shard_map/ppermute | solution.py:289
  52.2 5.1 %collective-permute-start.4 = (f32[8,16,256]{2,1,0:T(8,128)S(1)}, f32[8,16,256]{2,1,0:T(8,128)S(1)}, u32[]{:S(2)}, u32[]{:S(2)}) collective-permute-start(f32[8,16,256]{2,1,0:T(8,128)S(1)} %shard_map.88.refs_1_.k1), channel_id=1, source_target_pairs={{0,32},{32,64},{64,96},{96,128},{128,160},{160,192},{192,224},{224... | collective-permute-start | bytes 393224 | tf_op jit(solution)/shard_map/ppermute | solution.py:289
  52.8 4.6 %collective-permute-start.5 = (f32[8,16,256]{2,1,0:T(8,128)S(1)}, f32[8,16,256]{2,1,0:T(8,128)S(1)}, u32[]{:S(2)}, u32[]{:S(2)}) collective-permute-start(f32[8,16,256]{2,1,0:T(8,128)S(1)} %shard_map.88.refs_1_.k1), channel_id=1, source_target_pairs={{32,0},{64,32},{96,64},{128,96},{160,128},{192,160},{224,192},{225... | collective-permute-start | bytes 393224 | tf_op jit(solution)/shard_map/ppermute | solution.py:289
  58.7 4.4 %collective-permute-start.6 = (f32[4,16,256]{2,1,0:T(8,128)S(1)}, f32[4,16,256]{2,1,0:T(8,128)S(1)}, u32[]{:S(2)}, u32[]{:S(2)}) collective-permute-start(f32[4,16,256]{2,1,0:T(8,128)S(1)} %get-tuple-element.13.refs_1_.k2x), channel_id=1, source_target_pairs={{0,32},{32,64},{64,96},{96,128},{128,160},{160,192},{192,224},{224... | collective-permute-start | bytes 196616 | tf_op jit(solution)/shard_map/ppermute | solution.py:289
  59.0 4.1 %collective-permute-start.7 = (f32[4,16,256]{2,1,0:T(8,128)S(1)}, f32[4,16,256]{2,1,0:T(8,128)S(1)}, u32[]{:S(2)}, u32[]{:S(2)}) collective-permute-start(f32[4,16,256]{2,1,0:T(8,128)S(1)} %get-tuple-element.13.refs_1_.k2x), channel_id=1, source_target_pairs={{32,0},{64,32},{96,64},{128,96},{160,128},{192,160},{224,192},{225... | collective-permute-start | bytes 196616 | tf_op jit(solution)/shard_map/ppermute | solution.py:289
  101.2 19.6 %all-to-all-start.4 = ((f32[64,8,128]{2,1,0:T(8,128)}), f32[64,8,128]{2,1,0:T(8,128)S(1)}, u32[]{:S(2)}, u32[]{:S(2)}) async-start(f32[64,8,128]{2,1,0:T(8,128)} %get-tuple-element.15), calls=%async_computation.4 | async-start | bytes 524288 | tf_op jit(solution)/shard_map/all_to_all | solution.py:351

commit v3 on v2

--- a/solution.py
+++ b/solution.py
@@ -24,6 +24,19 @@
 
 def dot(a, b, dims=(((1,), (0,)), ((), ()))):
     return lax.dot_general(a, b, dims, precision=HI, preferred_element_type=jnp.float32)
+
+
+def bf16(*shape):
+    return jax.ShapeDtypeStruct(shape, jnp.bfloat16)
+
+
+def split(value):
+    high = value.astype(jnp.bfloat16)
+    return high, (value - high.astype(jnp.float32)).astype(jnp.bfloat16)
+
+
+def fast(a, b):
+    return lax.dot_general(a, b, (((1,), (0,)), ((), ())), preferred_element_type=jnp.float32)
 
 
 def call(kernel, out, *args, scalar=None, **kw):
@@ -46,14 +59,55 @@
     return pair + flip * (7 - 2 * pair)
 
 
-def pack_kernel(flip_ref, q_ref, p_ref, out_ref):
+def pack_kernel(flip_ref, q_hbm, p_hbm, out_hbm, q_ref, p_ref, o_ref, in_sem, out_sem):
     flip = flip_ref[0]
+    arriving = []
+    for i in range(4):
+        lanes = pl.ds(i * 512, 512)
+        both = []
+        for j, (source, target) in enumerate(((q_hbm, q_ref), (p_hbm, p_ref))):
+            copy = pltpu.make_async_copy(
+                source.at[:, :, lanes], target.at[:, :, lanes], in_sem.at[i, j]
+            )
+            copy.start()
+            both.append(copy)
+        arriving.append(both)
+    leaving = []
     for pair in range(8):
-        place = turned(pair, flip) * 8
+        if pair % 2 == 0:
+            for copy in arriving[pair // 2]:
+                copy.wait()
         lanes = pl.ds(pair * 256, 256)
         for col in range(4):
-            out_ref[place + col] = q_ref[:, col, lanes]
-            out_ref[place + 4 + col] = p_ref[:, col, lanes]
+            o_ref[pair * 8 + col] = q_ref[:, col, lanes]
+            o_ref[pair * 8 + 4 + col] = p_ref[:, col, lanes]
+        copy = pltpu.make_async_copy(
+            o_ref.at[pl.ds(pair * 8, 8)],
+            out_hbm.at[pl.ds(turned(pair, flip) * 8, 8)],
+            out_sem.at[pair],
+        )
+        copy.start()
+        leaving.append(copy)
+    for copy in leaving:
+        copy.wait()
+
+
+def pack(flip, q_block, q_prev):
+    hbm = pl.BlockSpec(memory_space=pltpu.HBM)
+    return pl.pallas_call(
+        pack_kernel,
+        out_shape=f32(64, 8, 256),
+        in_specs=[pl.BlockSpec(memory_space=pltpu.SMEM), hbm, hbm],
+        out_specs=hbm,
+        scratch_shapes=[
+            pltpu.VMEM((8, 4, 2048), jnp.float32),
+            pltpu.VMEM((8, 4, 2048), jnp.float32),
+            pltpu.VMEM((64, 8, 256), jnp.float32),
+            pltpu.SemaphoreType.DMA((4, 2)),
+            pltpu.SemaphoreType.DMA((8,)),
+        ],
+        compiler_params=pltpu.CompilerParams(vmem_limit_bytes=VMEM_LIMIT),
+    )(flip, q_block, q_prev)
 
 
 def raw_kernel(q_ref, p_ref, gram_ref):
@@ -65,7 +119,7 @@
     gram_ref[:, 0:8] = total
 
 
-def stats_kernel(pair_ref, s_ref, c_ref, out_ref, own_ref):
+def stats_kernel(pair_ref, s_ref, c_ref, out_ref, high_ref, low_ref):
     step = pl.program_id(0)
     row = lax.broadcasted_iota(jnp.int32, (128, 128), 0)
     col = lax.broadcasted_iota(jnp.int32, (128, 128), 1)
@@ -94,26 +148,39 @@
         @pl.when(step == pair_ref[0] * 2 + half)
         def _():
             for k in range(5):
-                lanes = pl.ds(k * 128, 128)
-                own_ref[half, 0:128, lanes] = s_ref[0, k]
-                own_ref[half, 128:256, lanes] = c_ref[0, k]
+                high, low = split(jnp.concatenate([s_ref[0, k].T, c_ref[0, k].T], axis=1))
+                high_ref[half, k * 128 : k * 128 + 128] = high
+                low_ref[half, k * 128 : k * 128 + 128] = low
+
+
+def table_kernel(f_ref, rows_ref, turned_ref):
+    high, low = split(f_ref[...])
+    rows_ref[0:128], rows_ref[128:256] = high, low
+    high, low = split(f_ref[...].T)
+    turned_ref[:, 0:128], turned_ref[:, 128:256] = high, low
 
 
 def forward_kernel(f_ref, r_ref, out_ref):
-    out_ref[...] = dot(f_ref[...], r_ref[...].reshape(SECTORS, 256)).reshape(8, 16, 256)
-
-
-def apply_kernel(shift, left_ref, own_ref, right_ref, w_ref, f_ref, k_ref, *out_refs):
+    high, low = split(r_ref[...].reshape(SECTORS, 256))
+    both = fast(f_ref[...], high)
+    out_ref[...] = (both[:128] + both[128:] + fast(f_ref[0:128], low)).reshape(8, 16, 256)
+
+
+def apply_kernel(shift, left_ref, own_ref, right_ref, high_ref, low_ref, f_ref, k_ref, *out_refs):
     count = own_ref.shape[0]
     rows = count * 16
     own = own_ref[...].reshape(rows, 256)
     wide = jnp.concatenate(
         [left_ref[...].reshape(rows, 256), own, right_ref[...].reshape(rows, 256)], axis=1
     )
+    high, low = split(wide)
+    stacked = jnp.concatenate([high, low], axis=0)
     factor = f_ref[...][None]
     sigma, inverse = k_ref[0:1, :][None], k_ref[1:2, :][None]
     for half in range(2):
-        both = dot(wide[:, half * 128 : half * 128 + 640], w_ref[half], NT)
+        lanes = slice(half * 128, half * 128 + 640)
+        both = fast(stacked[:, lanes], high_ref[half])
+        both = both[:rows] + both[rows:] + fast(high[:, lanes], low_ref[half])
         value = both[:, :128].reshape(count, 16, 128)
         value = value + factor * both[:, 128:].reshape(count, 16, 128)
         if shift:
@@ -165,17 +232,23 @@
         out_ref[d] = total
 
 
-def mixed(weights, rows):
-    total = weights[:, 0:1] * rows[0:1, :]
+def mixed(columns, rows):
+    total = columns[0] * rows[0:1, :]
     for l in range(1, 4):
-        total += weights[:, l : l + 1] * rows[l : l + 1, :]
+        total += columns[l] * rows[l : l + 1, :]
     return total
 
 
 def products(a, b):
-    return jnp.concatenate(
-        [jnp.sum(a * b[l : l + 1, :], axis=1, keepdims=True) for l in range(4)], axis=1
-    )
+    return [jnp.sum(a * b[l : l + 1, :], axis=1, keepdims=True) for l in range(4)]
+
+
+def square_of(columns):
+    col = lax.broadcasted_iota(jnp.int32, (4, 4), 1)
+    value = columns[0] + jnp.zeros((4, 4), jnp.float32)
+    for l in range(1, 4):
+        value = jnp.where(col == l, columns[l], value)
+    return value
 
 
 def solve_kernel(g_ref, b_ref, k_ref, v_ref, f_ref, image_ref, coef_ref, alpha_ref, beta_ref):
@@ -196,42 +269,54 @@
     cur = (lane == row).astype(jnp.float32)
     prev = (lane == row + 4).astype(jnp.float32)
     cur_g, prev_g = gram[0:4], gram[4:8]
-    coupling = b_ref[...]
+    coupling = [b_ref[:, l : l + 1] for l in range(4)]
     one_row = lax.broadcasted_iota(jnp.int32, (4, 1), 0)
-    small_row = lax.broadcasted_iota(jnp.int32, (4, 4), 0)
-    small_col = lax.broadcasted_iota(jnp.int32, (4, 4), 1)
     for step in range(3):
         moved = scale * pltpu.roll(jnp.where(lane < 20, cur, 0.0), 8, 1)
         moved += sigma * jnp.where(lane >= 8, cur, 0.0)
         w = moved - mixed(coupling, prev)
         w_g = dot(moved[:, 0:32], gram) - mixed(coupling, prev_g)
         across = products(w_g, cur)
-        alpha_ref[step] = products(cur_g, w)
+        alpha_ref[step] = square_of(products(cur_g, w))
         r = w - mixed(across, cur)
         r_g = w_g - mixed(across, cur_g)
         square = products(r_g, r)
         pivots = jnp.zeros((4, 1), jnp.float32)
         for i in range(4):
-            pivot = square[i : i + 1, i : i + 1]
+            pivot = square[i][i : i + 1, :]
             pivots = jnp.where(one_row == i, pivot, pivots)
             if i < 3:
-                times = jnp.where(one_row > i, square[:, i : i + 1] / pivot, 0.0)
+                times = jnp.where(one_row > i, square[i] / pivot, 0.0)
                 r = r - times * r[i : i + 1, :]
                 r_g = r_g - times * r_g[i : i + 1, :]
-                square = square - times * square[i : i + 1, :]
+                square = [
+                    v - times * v[i : i + 1, :] if l > i else v for l, v in enumerate(square)
+                ]
         root = 1.0 / jnp.sqrt(pivots)
-        upper = jnp.where(small_col >= small_row, square * root, 0.0)
-        beta_ref[step] = upper
+        upper = [jnp.where(one_row <= l, square[l] * root, 0.0) for l in range(4)]
+        beta_ref[step] = square_of(upper)
         prev, prev_g, coupling = cur, cur_g, upper
         cur, cur_g = r * root, r_g * root
     coef_ref[...] = cur
+    group = lane[0:1] // 32
     spread = (lane // 32 == row).astype(jnp.float32)
     weights = dot(cur, spread, TN)
-    same = lax.broadcasted_iota(jnp.int32, (32, 128), 1) % 32 == lax.broadcasted_iota(jnp.int32, (32, 128), 0)
-    mixing = jnp.concatenate([jnp.where(same, weights[8 + k : 9 + k, :], 0.0) for k in range(20)], axis=0)
-    vectors = jnp.concatenate([v_ref[:, m * 16 : m * 16 + 16].reshape(128, 128) for m in range(5)], axis=1)
-    field = dot(vectors, mixing)
-    image_ref[...] = dot(f_ref[...], field, TN).reshape(64, 8, 128)
+    field = jnp.zeros((128, 128), jnp.float32)
+    for m in range(5):
+        tile = v_ref[:, m * 16 : m * 16 + 16].reshape(128, 128)
+        for by in range(4):
+            line = None
+            for c in range(4):
+                from_row = weights[8 + 4 * m + c : 9 + 4 * m + c, :]
+                line = from_row if line is None else jnp.where(group == (c + by) % 4, from_row, line)
+            field += line * (pltpu.roll(tile, 32 * by, 1) if by else tile)
+    high, low = split(field)
+    none = jnp.zeros((128, 128), jnp.bfloat16)
+    right = jnp.concatenate(
+        [jnp.concatenate([high, low], axis=1), jnp.concatenate([high, none], axis=1)], axis=0
+    )
+    both = fast(f_ref[...], right)
+    image_ref[...] = (both[:, :128] + both[:, 128:]).reshape(64, 8, 128)
 
 
 def base_kernel(flip_ref, q_ref, coef_ref, out_ref):
@@ -298,24 +383,25 @@
     pair = turned(lax.axis_index("z"), flip)
     group = lax.axis_index("y") * 2 + lax.axis_index("core")
 
-    packed = call(pack_kernel, f32(64, 8, 256), q_block, q_prev, scalar=flip)
+    packed = pack(flip, q_block, q_prev)
     received = lax.all_to_all(packed, SEC, 0, 0, tiled=True)
 
-    forward = table(assign)
+    forward, inverse = call(table_kernel, (bf16(256, 512), bf16(512, 256)), table(assign))
     factors = jnp.cos(2.0 * math.pi / SECTORS * assign.astype(jnp.float32))
     mine = lax.dynamic_slice_in_dim(factors, group * 8, 8)
     factor = jnp.broadcast_to(jnp.repeat(mine, 2)[:, None], (16, 128))
     raw = call(raw_kernel, f32(8, 128), q_block, q_prev)
-    found, own = pl.pallas_call(
+    found, own_high, own_low = pl.pallas_call(
         stats_kernel,
-        out_shape=(f32(6, 8, 128), f32(2, 256, 640)),
+        out_shape=(f32(6, 8, 128), bf16(2, 640, 256), bf16(2, 640, 256)),
         grid_spec=pltpu.PrefetchScalarGridSpec(
             num_scalar_prefetch=1,
             grid=(16,),
             in_specs=[pl.BlockSpec((1, 5, 128, 128), lambda i, p: (i, 0, 0, 0))] * 2,
             out_specs=(
                 pl.BlockSpec((6, 8, 128), lambda i, p: (0, 0, 0)),
-                pl.BlockSpec((2, 256, 640), lambda i, p: (0, 0, 0)),
+                pl.BlockSpec((2, 640, 256), lambda i, p: (0, 0, 0)),
+                pl.BlockSpec((2, 640, 256), lambda i, p: (0, 0, 0)),
             ),
         ),
         compiler_params=pltpu.CompilerParams(vmem_limit_bytes=VMEM_LIMIT),
@@ -333,7 +419,7 @@
     def operator(value, shift, out):
         left, right = beside(value)
         return call(
-            lambda *refs: apply_kernel(shift, *refs), out, left, value, right, own, factor, scales
+            lambda *refs: apply_kernel(shift, *refs), out, left, value, right, own_high, own_low, factor, scales
         )
 
     (k1,) = operator(k0, False, (f32(8, 16, 256),))
@@ -346,7 +432,7 @@
     image, coef, alphas, betas = call(
         solve_kernel,
         (f32(64, 8, 128), f32(4, 128), f32(3, 4, 4), f32(3, 4, 4)),
-        grams, b_prev, scales, vectors, forward,
+        grams, b_prev, scales, vectors, inverse,
     )
     back = lax.all_to_all(image, SEC, 0, 0, tiled=True)
     base = call(base_kernel, f32(8, 4, 8, 256), packed, coef, scalar=flip)

time: 122 us -> 118 us (0.967)
  Pallas kernels: 15.9 us -> 12 us
    pallas_call x11, Pallas kernels: 14.6 us -> 9.31 us  [call(): pl.pallas_call(kernel, out_shape=out, in_specs=specs, out_specs=jax.tree....]
    pallas_call x1 -> x2, Pallas kernels: 1.29 us -> 2.74 us  [the longest x1 1.67 us: per_device(): pl.pallas_call(stats_kernel, out_shape=(f32(6, 8, 128), bf16(2, 640, 256)...]
  transfers between devices with their start and end apart: 11 -> 11, of which waited for: 7 -> 7; matrix products, arithmetic and copies ran while one was open for 2% -> 2% of each run, Pallas kernels for 4% -> 5%
where the time goes in v3:
time: 118 us; the launch traced here: 117 us
  starting transfers between devices  36.4 us (31%)
  blocking collectives  31.6 us (27%)
  waiting for transfers between devices  26.3 us (22%)
  Pallas kernels  12 us (10%)
  local copies, waits for them, and re-layouts  7.5 us (6%)
  other arithmetic  2 us (2%)
  between operations  1.47 us (1%)
    all_to_all x1, blocking collectives, per_device(): lax.all_to_all(call(total_kernel, f32(32, 8, 128), vectors), RING, 0, 0,...  17 us
    all_to_all x1, blocking collectives, per_device(): vectors = lax.all_to_all(shares, GROUP, 0, 0, tiled=True)  14.6 us
    all_to_all x1, starting transfers between devices, per_device(): received = lax.all_to_all(packed, SEC, 0, 0, tiled=True)  13.2 us
    all_to_all x1, waiting for transfers between devices, per_device(): back = lax.all_to_all(image, SEC, 0, 0, tiled=True)  12 us
    pallas_call x11, Pallas kernels, call(): pl.pallas_call(kernel, out_shape=out, in_specs=specs, out_specs=jax.tree....  9.31 us
    ppermute x6, starting transfers between devices, beside(): return (lax.ppermute(value, RING, after), lax.ppermute(value, RING, before))  8.27 us
    unnamed x16, local copies, waits for them, and re-layouts  6.88 us
    all_to_all x1, starting transfers between devices, per_device(): back = lax.all_to_all(image, SEC, 0, 0, tiled=True)  6.34 us
  transfers between devices with their start and end apart: 11, of which 7 were waited for; matrix products, arithmetic and copies ran while one was open for 2% of the time, Pallas kernels for 5%

profile of v3, /device:TPU:1, one launch (start us, length us, event | category | flops | bytes accessed | tf_op | source)
XLA Modules:
  0.0 117.3 jit_solution(5633685094673374408)
XLA Ops:
  2.5 1.1 shard_map.86.q_ref
  3.6 13.2 %all-to-all-start = ((f32[64,8,256]{2,1,0:T(8,128)}), f32[64,8,256]{2,1,0:T(8,128)S(1)}, u32[]{:S(2)}, u32[]{:S(2)}) async-start(f32[64,8,256]{2,1,0:T(8,128)} %shard_map.86.q_ref), calls=%async_computation | async-start | bytes 1048576 | tf_op jit(solution)/shard_map/all_to_all | solution.py:387
  16.8 2.5 %copy-done = f32[16,5,128,128]{3,2,1,0:T(8,128)S(1)} copy-done((f32[16,5,128,128]{3,2,1,0:T(8,128)S(1)}, f32[16,5,128,128]{3,2,1,0:T(8,128)}, u32[]{:S(2)}) %copy-start) | copy-done | bytes 5242904
  19.3 2.5 %copy-done.1 = f32[16,5,128,128]{3,2,1,0:T(8,128)S(1)} copy-done((f32[16,5,128,128]{3,2,1,0:T(8,128)S(1)}, f32[16,5,128,128]{3,2,1,0:T(8,128)}, u32[]{:S(2)}) %copy-start.1) | copy-done | bytes 5242904
  21.8 1.7 %shard_map.88 = (f32[6,8,128]{2,1,0:T(8,128)S(1)}, bf16[2,640,256]{2,1,0:T(8,128)(2,1)S(1)}, bf16[2,640,256]{2,1,0:T(8,128)(2,1)S(1)}) custom-call(s32[1]{0:T(128)S(6)} %add.60.pair_ref, f32[16,5,128,128]{3,2,1,0:T(8,128)S(1)} %copy-done, f32[16,5,128,128]{3,2,1,0:T(8,128)S(1)} %copy-done.1), custom_call_target="tpu_custom_call" | custom-call | tf_op jit(solution)/shard_map/pallas_call | solution.py:394
  23.7 1.2 %collective-permute-start.2 = (f32[6,128]{1,0:T(8,128)S(1)}, f32[6,128]{1,0:T(8,128)S(1)}, u32[]{:S(2)}, u32[]{:S(2)}) collective-permute-start(f32[6,128]{1,0:T(8,128)S(1)} %broadcast_in_dim.45), channel_id=1, source_target_pairs={{0,1},{1,0},{2,3},{3,2},{4,5},{5,4},{6,7},{7,6},{8,9},{9,8},{10,11... | collective-permute-start | bytes 9224 | tf_op jit(solution)/shard_map/ppermute | solution.py:378
  25.1 1.1 fusion.4.f_ref
  26.5 2.7 %collective-permute-start.3 = (f32[6,128]{1,0:T(8,128)S(1)}, f32[6,128]{1,0:T(8,128)S(1)}, u32[]{:S(2)}, u32[]{:S(2)}) collective-permute-start(f32[6,128]{1,0:T(8,128)S(1)} %broadcast_maximum_fusion), channel_id=1, source_target_pairs={{0,2},{1,3},{2,0},{3,1},{4,6},{5,7},{6,4},{7,5},{8,10},{9,11},{10,... | collective-permute-start | bytes 9224 | tf_op jit(solution)/shard_map/ppermute | solution.py:378
  31.0 3.5 %all-to-all-done.r_ref = f32[64,8,256]{2,1,0:T(8,128)S(1)} async-done(((f32[64,8,256]{2,1,0:T(8,128)}), f32[64,8,256]{2,1,0:T(8,128)S(1)}, u32[]{:S(2)}, u32[]{:S(2)}) %all-to-all-start) | async-done | bytes 524320 | tf_op jit(solution)/shard_map/all_to_all | solution.py:387
  35.5 4.7 %all-to-all-start.1 = ((f32[8,16,256]{2,1,0:T(8,128)}), f32[8,16,256]{2,1,0:T(8,128)S(1)}, u32[]{:S(2)}, u32[]{:S(2)}) async-start(f32[8,16,256]{2,1,0:T(8,128)} %shard_map.87), calls=%async_computation.1 | async-start | bytes 262144 | tf_op jit(solution)/shard_map/all_to_all | solution.py:417
  40.2 5.2 %all-to-all-done.1.refs_1_.k0 = f32[8,16,256]{2,1,0:T(8,128)S(1)} async-done(((f32[8,16,256]{2,1,0:T(8,128)}), f32[8,16,256]{2,1,0:T(8,128)S(1)}, u32[]{:S(2)}, u32[]{:S(2)}) %all-to-all-start.1) | async-done | bytes 131104 | tf_op jit(solution)/shard_map/all_to_all | solution.py:417
  45.7 2.3 %collective-permute-start.1 = (f32[8,16,256]{2,1,0:T(8,128)S(1)}, f32[8,16,256]{2,1,0:T(8,128)S(1)}, u32[]{:S(2)}, u32[]{:S(2)}) collective-permute-start(f32[8,16,256]{2,1,0:T(8,128)S(1)} %all-to-all-done.1.refs_1_.k0), channel_id=1, source_target_pairs={{32,0},{64,32},{96,64},{128,96},{160,128},{192,160},{224,192},{225... | collective-permute-start | bytes 393224 | tf_op jit(solution)/shard_map/ppermute | solution.py:374
  48.1 2.6 %collective-permute-done.refs_0_ = f32[8,16,256]{2,1,0:T(8,128)S(1)} collective-permute-done((f32[8,16,256]{2,1,0:T(8,128)S(1)}, f32[8,16,256]{2,1,0:T(8,128)S(1)}, u32[]{:S(2)}, u32[]{:S(2)}) %collective-permute-start) | collective-permute-done | bytes 131104 | tf_op jit(solution)/shard_map/ppermute | solution.py:374
  51.8 2.2 %collective-permute-start.5 = (f32[8,16,256]{2,1,0:T(8,128)S(1)}, f32[8,16,256]{2,1,0:T(8,128)S(1)}, u32[]{:S(2)}, u32[]{:S(2)}) collective-permute-start(f32[8,16,256]{2,1,0:T(8,128)S(1)} %shard_map.89.refs_1_.k1), channel_id=1, source_target_pairs={{32,0},{64,32},{96,64},{128,96},{160,128},{192,160},{224,192},{225... | collective-permute-start | bytes 393224 | tf_op jit(solution)/shard_map/ppermute | solution.py:374
  54.1 2.4 %collective-permute-done.4.refs_0_ = f32[8,16,256]{2,1,0:T(8,128)S(1)} collective-permute-done((f32[8,16,256]{2,1,0:T(8,128)S(1)}, f32[8,16,256]{2,1,0:T(8,128)S(1)}, u32[]{:S(2)}, u32[]{:S(2)}) %collective-permute-start.4) | collective-permute-done | bytes 131104 | tf_op jit(solution)/shard_map/ppermute | solution.py:374
  56.9 1.2 %collective-permute-start.6 = (f32[4,16,256]{2,1,0:T(8,128)S(1)}, f32[4,16,256]{2,1,0:T(8,128)S(1)}, u32[]{:S(2)}, u32[]{:S(2)}) collective-permute-start(f32[4,16,256]{2,1,0:T(8,128)S(1)} %get-tuple-element.18.refs_1_.k2x), channel_id=1, source_target_pairs={{0,32},{32,64},{64,96},{96,128},{128,160},{160,192},{192,224},{224... | collective-permute-start | bytes 196616 | tf_op jit(solution)/shard_map/ppermute | solution.py:374
  58.1 1.7 %collective-permute-start.7 = (f32[4,16,256]{2,1,0:T(8,128)S(1)}, f32[4,16,256]{2,1,0:T(8,128)S(1)}, u32[]{:S(2)}, u32[]{:S(2)}) collective-permute-start(f32[4,16,256]{2,1,0:T(8,128)S(1)} %get-tuple-element.18.refs_1_.k2x), channel_id=1, source_target_pairs={{32,0},{64,32},{96,64},{128,96},{160,128},{192,160},{224,192},{225... | collective-permute-start | bytes 196616 | tf_op jit(solution)/shard_map/ppermute | solution.py:374
  59.7 1.2 %shard_map.92.raw_ref = f32[8,128]{1,0:T(8,128)S(1)} custom-call(f32[8,4,2048]{2,1,0:T(4,128)S(1)} %copy-done.3, f32[8,4,2048]{2,1,0:T(4,128)S(1)} %copy-done.5), custom_call_target="tpu_custom_call" | custom-call | tf_op jit(solution)/shard_map/pallas_call | solution.py:48
  62.4 14.6 %all_to_all.25.v_ref = f32[8,88,128]{2,1,0:T(8,128)S(1)} all-to-all(f32[8,88,128]{2,1,0:T(8,128)S(1)} %shard_map.93), channel_id=1, replica_groups=mesh['z'=8,'y'=4,'core'=2,'xs'=4] {'y','core'}, dimensions={0} | all-to-all | bytes 720896 | tf_op jit(solution)/shard_map/all_to_all | solution.py:430
  77.0 17.0 %all_to_all.26.g_ref = f32[32,8,128]{2,1,0:T(8,128)S(1)} all-to-all(f32[32,8,128]{2,1,0:T(8,128)S(1)} %shard_map.94), channel_id=1, replica_groups=mesh['z'=8,'y'=4,'core'=2,'xs'=4] {'z','xs'}, dimensions={0} | all-to-all | bytes 262144 | tf_op jit(solution)/shard_map/all_to_all | solution.py:431
  94.0 2.7 %shard_map.95 = (f32[64,8,128]{2,1,0:T(8,128)}, f32[4,128]{1,0:T(4,128)S(1)}, f32[3,4,4]{2,1,0:T(4,128)}, f32[3,4,4]{2,1,0:T(4,128)}) custom-call(f32[32,8,128]{2,1,0:T(8,128)S(1)} %all_to_all.26.g_ref, f32[4,4]{1,0:T(4,128)S(1)} %copy-done.6, f32[8,128]{1,0:T(8,128)S(1)} %stack.2.refs_6_.k_ref, f32[8,88,128]{2,1,0:T(8,128)S(1)} %all_to_all.25.v_ref, ...), custom_call_target="tpu_custom_call" | custom-call | tf_op jit(solution)/shard_map/pallas_call | solution.py:48
  96.7 6.3 %all-to-all-start.4 = ((f32[64,8,128]{2,1,0:T(8,128)}), f32[64,8,128]{2,1,0:T(8,128)S(1)}, u32[]{:S(2)}, u32[]{:S(2)}) async-start(f32[64,8,128]{2,1,0:T(8,128)} %get-tuple-element.21), calls=%async_computation.4 | async-start | bytes 524288 | tf_op jit(solution)/shard_map/all_to_all | solution.py:437
  103.0 1.3 %shard_map.96.base_ref = f32[8,4,8,256]{3,2,1,0:T(8,128)S(1)} custom-call(s32[1]{0:T(128)} %bitcast.flip_ref, f32[64,8,256]{2,1,0:T(8,128)} %shard_map.86.q_ref, f32[4,128]{1,0:T(4,128)S(1)} %get-tuple-element.22.coef_ref), custom_call_target="tpu_custom_call" | custom-call | tf_op jit(solution)/shard_map/pallas_call | solution.py:48
  104.3 12.0 %all-to-all-done.4.r_ref = f32[64,8,128]{2,1,0:T(8,128)S(1)} async-done(((f32[64,8,128]{2,1,0:T(8,128)}), f32[64,8,128]{2,1,0:T(8,128)S(1)}, u32[]{:S(2)}, u32[]{:S(2)}) %all-to-all-start.4) | async-done | bytes 262176 | tf_op jit(solution)/shard_map/all_to_all | solution.py:437
  (45 shorter events, 9.0 us)
Async XLA Ops:
  0.6 1.0 copy-start.2
  1.6 0.9 copy-start.4
  3.6 30.9 %all-to-all-start = ((f32[64,8,256]{2,1,0:T(8,128)}), f32[64,8,256]{2,1,0:T(8,128)S(1)}, u32[]{:S(2)}, u32[]{:S(2)}) async-start(f32[64,8,256]{2,1,0:T(8,128)} %shard_map.86.q_ref), calls=%async_computation | async-start | bytes 1048576 | tf_op jit(solution)/shard_map/all_to_all | solution.py:387
  16.8 2.5 %copy-start = (f32[16,5,128,128]{3,2,1,0:T(8,128)S(1)}, f32[16,5,128,128]{3,2,1,0:T(8,128)}, u32[]{:S(2)}) copy-start(f32[16,5,128,128]{3,2,1,0:T(8,128)} %s_ref.1) | copy-start | bytes 15728644
  19.3 2.5 %copy-start.1 = (f32[16,5,128,128]{3,2,1,0:T(8,128)S(1)}, f32[16,5,128,128]{3,2,1,0:T(8,128)}, u32[]{:S(2)}) copy-start(f32[16,5,128,128]{3,2,1,0:T(8,128)} %c_ref.1) | copy-start | bytes 15728644
  21.8 3.1 %copy-start.7 = (s32[64]{0:T(128)S(1)}, s32[64]{0:T(128)}, u32[]{:S(2)}) copy-start(s32[64]{0:T(128)} %param.12) | copy-start | bytes 772
  23.5 36.3 %copy-start.3 = (f32[8,4,2048]{2,1,0:T(4,128)S(1)}, f32[8,4,2048]{2,1,0:T(4,128)}, u32[]{:S(2)}) copy-start(f32[8,4,2048]{2,1,0:T(4,128)} %q_ref.1) | copy-start | bytes 786436
  23.5 36.3 %copy-start.5 = (f32[8,4,2048]{2,1,0:T(4,128)S(1)}, f32[8,4,2048]{2,1,0:T(4,128)}, u32[]{:S(2)}) copy-start(f32[8,4,2048]{2,1,0:T(4,128)} %p_ref.1) | copy-start | bytes 786436
  23.5 70.5 %copy-start.6 = (f32[4,4]{1,0:T(4,128)S(1)}, f32[4,4]{1,0:T(4,128)}, u32[]{:S(2)}) copy-start(f32[4,4]{1,0:T(4,128)} %b_ref.1) | copy-start | bytes 196
  23.7 2.8 %collective-permute-start.2 = (f32[6,128]{1,0:T(8,128)S(1)}, f32[6,128]{1,0:T(8,128)S(1)}, u32[]{:S(2)}, u32[]{:S(2)}) collective-permute-start(f32[6,128]{1,0:T(8,128)S(1)} %broadcast_in_dim.45), channel_id=1, source_target_pairs={{0,1},{1,0},{2,3},{3,2},{4,5},{5,4},{6,7},{7,6},{8,9},{9,8},{10,11... | collective-permute-start | bytes 9224 | tf_op jit(solution)/shard_map/ppermute | solution.py:378
  26.5 13.6 %collective-permute-start.3 = (f32[6,128]{1,0:T(8,128)S(1)}, f32[6,128]{1,0:T(8,128)S(1)}, u32[]{:S(2)}, u32[]{:S(2)}) collective-permute-start(f32[6,128]{1,0:T(8,128)S(1)} %broadcast_maximum_fusion), channel_id=1, source_target_pairs={{0,2},{1,3},{2,0},{3,1},{4,6},{5,7},{6,4},{7,5},{8,10},{9,11},{10,... | collective-permute-start | bytes 9224 | tf_op jit(solution)/shard_map/ppermute | solution.py:378
  35.5 9.9 %all-to-all-start.1 = ((f32[8,16,256]{2,1,0:T(8,128)}), f32[8,16,256]{2,1,0:T(8,128)S(1)}, u32[]{:S(2)}, u32[]{:S(2)}) async-start(f32[8,16,256]{2,1,0:T(8,128)} %shard_map.87), calls=%async_computation.1 | async-start | bytes 262144 | tf_op jit(solution)/shard_map/all_to_all | solution.py:417
  45.4 5.4 %collective-permute-start = (f32[8,16,256]{2,1,0:T(8,128)S(1)}, f32[8,16,256]{2,1,0:T(8,128)S(1)}, u32[]{:S(2)}, u32[]{:S(2)}) collective-permute-start(f32[8,16,256]{2,1,0:T(8,128)S(1)} %all-to-all-done.1.refs_1_.k0), channel_id=1, source_target_pairs={{0,32},{32,64},{64,96},{96,128},{128,160},{160,192},{192,224},{224... | collective-permute-start | bytes 393224 | tf_op jit(solution)/shard_map/ppermute | solution.py:374
  45.7 5.0 %collective-permute-start.1 = (f32[8,16,256]{2,1,0:T(8,128)S(1)}, f32[8,16,256]{2,1,0:T(8,128)S(1)}, u32[]{:S(2)}, u32[]{:S(2)}) collective-permute-start(f32[8,16,256]{2,1,0:T(8,128)S(1)} %all-to-all-done.1.refs_1_.k0), channel_id=1, source_target_pairs={{32,0},{64,32},{96,64},{128,96},{160,128},{192,160},{224,192},{225... | collective-permute-start | bytes 393224 | tf_op jit(solution)/shard_map/ppermute | solution.py:374
  51.3 5.1 %collective-permute-start.4 = (f32[8,16,256]{2,1,0:T(8,128)S(1)}, f32[8,16,256]{2,1,0:T(8,128)S(1)}, u32[]{:S(2)}, u32[]{:S(2)}) collective-permute-start(f32[8,16,256]{2,1,0:T(8,128)S(1)} %shard_map.89.refs_1_.k1), channel_id=1, source_target_pairs={{0,32},{32,64},{64,96},{96,128},{128,160},{160,192},{192,224},{224... | collective-permute-start | bytes 393224 | tf_op jit(solution)/shard_map/ppermute | solution.py:374
  51.8 4.6 %collective-permute-start.5 = (f32[8,16,256]{2,1,0:T(8,128)S(1)}, f32[8,16,256]{2,1,0:T(8,128)S(1)}, u32[]{:S(2)}, u32[]{:S(2)}) collective-permute-start(f32[8,16,256]{2,1,0:T(8,128)S(1)} %shard_map.89.refs_1_.k1), channel_id=1, source_target_pairs={{32,0},{64,32},{96,64},{128,96},{160,128},{192,160},{224,192},{225... | collective-permute-start | bytes 393224 | tf_op jit(solution)/shard_map/ppermute | solution.py:374
  56.9 4.4 %collective-permute-start.6 = (f32[4,16,256]{2,1,0:T(8,128)S(1)}, f32[4,16,256]{2,1,0:T(8,128)S(1)}, u32[]{:S(2)}, u32[]{:S(2)}) collective-permute-start(f32[4,16,256]{2,1,0:T(8,128)S(1)} %get-tuple-element.18.refs_1_.k2x), channel_id=1, source_target_pairs={{0,32},{32,64},{64,96},{96,128},{128,160},{160,192},{192,224},{224... | collective-permute-start | bytes 196616 | tf_op jit(solution)/shard_map/ppermute | solution.py:374
  58.1 3.2 %collective-permute-start.7 = (f32[4,16,256]{2,1,0:T(8,128)S(1)}, f32[4,16,256]{2,1,0:T(8,128)S(1)}, u32[]{:S(2)}, u32[]{:S(2)}) collective-permute-start(f32[4,16,256]{2,1,0:T(8,128)S(1)} %get-tuple-element.18.refs_1_.k2x), channel_id=1, source_target_pairs={{32,0},{64,32},{96,64},{128,96},{160,128},{192,160},{224,192},{225... | collective-permute-start | bytes 196616 | tf_op jit(solution)/shard_map/ppermute | solution.py:374
  96.7 19.6 %all-to-all-start.4 = ((f32[64,8,128]{2,1,0:T(8,128)}), f32[64,8,128]{2,1,0:T(8,128)S(1)}, u32[]{:S(2)}, u32[]{:S(2)}) async-start(f32[64,8,128]{2,1,0:T(8,128)} %get-tuple-element.21), calls=%async_computation.4 | async-start | bytes 524288 | tf_op jit(solution)/shard_map/all_to_all | solution.py:437

commit v4 on v3

--- a/solution.py
+++ b/solution.py
@@ -16,6 +16,7 @@
 NT = (((1,), (1,)), ((), ()))
 TN = (((0,), (0,)), ((), ()))
 VMEM_LIMIT = 32 * 1024 * 1024
+PACK_LIMIT = 60 * 1024 * 1024
 
 
 def f32(*shape):
@@ -106,7 +107,7 @@
             pltpu.SemaphoreType.DMA((4, 2)),
             pltpu.SemaphoreType.DMA((8,)),
         ],
-        compiler_params=pltpu.CompilerParams(vmem_limit_bytes=VMEM_LIMIT),
+        compiler_params=pltpu.CompilerParams(vmem_limit_bytes=PACK_LIMIT),
     )(flip, q_block, q_prev)
 
 
@@ -117,6 +118,26 @@
         total += dot(rows, rows, NT)
     gram_ref[...] = jnp.zeros((8, 128), jnp.float32)
     gram_ref[:, 0:8] = total
+
+
+def rest_kernel(k0_ref, raw_ref, b_ref, k_ref, out_ref):
+    inside = jnp.zeros((8, 8), jnp.float32)
+    for r in range(16):
+        rows = k0_ref[:, r, :]
+        inside += dot(rows, rows, NT)
+    outside = raw_ref[:, 0:8] - inside
+    row = lax.broadcasted_iota(jnp.int32, (4, 4), 0)
+    col = lax.broadcasted_iota(jnp.int32, (4, 4), 1)
+    none = jnp.zeros((4, 4), jnp.float32)
+    change = jnp.concatenate(
+        [
+            jnp.concatenate([(row == col).astype(jnp.float32), none], axis=1),
+            jnp.concatenate([none, -k_ref[1:2, 0:1] * b_ref[...]], axis=1),
+        ],
+        axis=0,
+    )
+    out_ref[...] = jnp.zeros((8, 128), jnp.float32)
+    out_ref[:, 0:8] = dot(dot(change, outside), change, NT)
 
 
 def stats_kernel(pair_ref, s_ref, c_ref, out_ref, high_ref, low_ref):
@@ -166,12 +187,11 @@
     out_ref[...] = (both[:128] + both[128:] + fast(f_ref[0:128], low)).reshape(8, 16, 256)
 
 
-def apply_kernel(shift, left_ref, own_ref, right_ref, high_ref, low_ref, f_ref, k_ref, *out_refs):
-    count = own_ref.shape[0]
+def apply_kernel(stage, left_ref, own_ref, right_ref, high_ref, low_ref, f_ref, k_ref, *refs):
+    count = left_ref.shape[0]
     rows = count * 16
-    own = own_ref[...].reshape(rows, 256)
     wide = jnp.concatenate(
-        [left_ref[...].reshape(rows, 256), own, right_ref[...].reshape(rows, 256)], axis=1
+        [ref[0:count].reshape(rows, 256) for ref in (left_ref, own_ref, right_ref)], axis=1
     )
     high, low = split(wide)
     stacked = jnp.concatenate([high, low], axis=0)
@@ -183,33 +203,40 @@
         both = both[:rows] + both[rows:] + fast(high[:, lanes], low_ref[half])
         value = both[:, :128].reshape(count, 16, 128)
         value = value + factor * both[:, 128:].reshape(count, 16, 128)
-        if shift:
-            mine = own[:, half * 128 : half * 128 + 128].reshape(count, 16, 128)
-            value = value - sigma * mine
-        value = value * inverse
-        size = count // len(out_refs)
-        for i, ref in enumerate(out_refs):
-            ref[:, :, half * 128 : half * 128 + 128] = value[i * size : (i + 1) * size]
-
-
-def share_kernel(k0, k1, k2x, k2y, k3, raw_ref, out_ref):
-    total = jnp.zeros((32, 32), jnp.float32)
+        here = slice(half * 128, half * 128 + 128)
+        if stage == 1:
+            b_ref, out_ref = refs
+            value = value * inverse
+            out_ref[0:4, :, here] = value
+            for i in range(4):
+                taken = b_ref[i, 0] * own_ref[4, :, here]
+                for l in range(1, 4):
+                    taken += b_ref[i, l] * own_ref[4 + l, :, here]
+                out_ref[4 + i, :, here] = value[i] - inverse[0] * taken
+        elif stage == 2:
+            x_ref, w_ref = refs
+            x_ref[:, :, here] = (value[0:4] - sigma * own_ref[0:4, :, here]) * inverse
+            w_ref[:, :, here] = value[4:8] * inverse
+        else:
+            (out_ref,) = refs
+            out_ref[:, :, here] = (value - sigma * own_ref[:, :, here]) * inverse
+
+
+def share_kernel(k0, s1, k2x, k2w, k3, rest_ref, out_ref):
+    total = jnp.zeros((24, 24), jnp.float32)
     for r in range(16):
         rows = jnp.concatenate(
-            [k0[:, r, :], k1[:, r, :], k2x[:, r, :], k2y[:, r, :], k3[:, r, :], jnp.zeros((4, 256), jnp.float32)],
+            [k0[0:4, r, :], s1[4:8, r, :], s1[0:4, r, :], k2w[:, r, :], k2x[:, r, :], k3[:, r, :]],
             axis=0,
         )
         total += dot(rows, rows, NT)
-    first = jnp.concatenate([raw_ref[:, 0:8], total[0:8, 8:32]], axis=1)
-    packed = jnp.concatenate([first, total[8:16], total[16:24], total[24:32]], axis=1)
+    first = jnp.concatenate([total[0:8, 0:8] + rest_ref[:, 0:8], total[0:8, 8:24]], axis=1)
+    pad = jnp.zeros((8, 8), jnp.float32)
+    packed = jnp.concatenate(
+        [first, pad, total[8:16], pad, total[16:24], pad, jnp.zeros((8, 32), jnp.float32)], axis=1
+    )
     group = lax.broadcasted_iota(jnp.int32, (16, 128), 1) // 32
-    sets = (
-        [k1[c] for c in range(4)],
-        [k1[4 + c] for c in range(4)],
-        [k2x[c] for c in range(4)],
-        [k2y[c] for c in range(4)],
-        [k3[c] for c in range(4)],
-    )
+    sets = tuple([ref[c] for c in range(4)] for ref in (s1, k2w, k2x, k3))
     for m, columns in enumerate(sets):
         for half in range(2):
             tiles = [v[:, half * 128 : half * 128 + 128] for v in columns]
@@ -221,13 +248,13 @@
                     value = moved if value is None else jnp.where(group == c, moved, value)
                 out_ref[half * 4 + q, m * 16 : m * 16 + 16] = value
     for d in range(8):
-        out_ref[d, 80:88] = packed
+        out_ref[d, 64:72] = packed
 
 
 def total_kernel(v_ref, out_ref):
-    total = v_ref[0, 80:88]
+    total = v_ref[0, 64:72]
     for d in range(1, 8):
-        total += v_ref[d, 80:88]
+        total += v_ref[d, 64:72]
     for d in range(32):
         out_ref[d] = total
 
@@ -262,20 +289,23 @@
     gram = jnp.concatenate(
         [
             jnp.where(narrow, packed if q == 0 else pltpu.roll(packed, 128 - 32 * q, 1), 0.0)
-            for q in range(4)
+            for q in range(3)
         ],
         axis=0,
     )
     cur = (lane == row).astype(jnp.float32)
-    prev = (lane == row + 4).astype(jnp.float32)
-    cur_g, prev_g = gram[0:4], gram[4:8]
-    coupling = [b_ref[:, l : l + 1] for l in range(4)]
+    cur_g = gram[0:4]
+    prev = prev_g = coupling = None
     one_row = lax.broadcasted_iota(jnp.int32, (4, 1), 0)
     for step in range(3):
-        moved = scale * pltpu.roll(jnp.where(lane < 20, cur, 0.0), 8, 1)
-        moved += sigma * jnp.where(lane >= 8, cur, 0.0)
-        w = moved - mixed(coupling, prev)
-        w_g = dot(moved[:, 0:32], gram) - mixed(coupling, prev_g)
+        if step == 0:
+            w = scale * (lane == row + 4).astype(jnp.float32)
+            w_g = scale * gram[4:8]
+        else:
+            moved = scale * pltpu.roll(jnp.where(lane < 16, cur, 0.0), 8, 1)
+            moved += sigma * jnp.where(lane >= 8, cur, 0.0)
+            w = moved - mixed(coupling, prev)
+            w_g = dot(moved[:, 0:24], gram) - mixed(coupling, prev_g)
         across = products(w_g, cur)
         alpha_ref[step] = square_of(products(cur_g, w))
         r = w - mixed(across, cur)
@@ -298,11 +328,16 @@
         prev, prev_g, coupling = cur, cur_g, upper
         cur, cur_g = r * root, r_g * root
     coef_ref[...] = cur
+    behind = cur[:, 4:5] * b_ref[0:1, :]
+    for l in range(1, 4):
+        behind += cur[:, 4 + l : 5 + l] * b_ref[l : l + 1, :]
+    coef_ref[:, 4:8] = -k_ref[1:2, 0:1] * behind
+    cur += pltpu.roll(jnp.where((lane >= 4) & (lane < 8), cur, 0.0), 4, 1)
     group = lane[0:1] // 32
     spread = (lane // 32 == row).astype(jnp.float32)
     weights = dot(cur, spread, TN)
     field = jnp.zeros((128, 128), jnp.float32)
-    for m in range(5):
+    for m in range(4):
         tile = v_ref[:, m * 16 : m * 16 + 16].reshape(128, 128)
         for by in range(4):
             line = None
@@ -416,17 +451,24 @@
     spectrum = call(forward_kernel, f32(8, 16, 256), forward, received)
     k0 = lax.all_to_all(spectrum, GROUP, 0, 0, tiled=True)
 
-    def operator(value, shift, out):
-        left, right = beside(value)
-        return call(
-            lambda *refs: apply_kernel(shift, *refs), out, left, value, right, own_high, own_low, factor, scales
-        )
-
-    (k1,) = operator(k0, False, (f32(8, 16, 256),))
-    k2x, k2y = operator(k1, True, (f32(4, 16, 256), f32(4, 16, 256)))
-    (k3,) = operator(k2x, True, (f32(4, 16, 256),))
-
-    shares = call(share_kernel, f32(8, 88, 128), k0, k1, k2x, k2y, k3, raw)
+    def operator(stage, sent, value, out, *more):
+        left, right = beside(sent)
+        specs = [pl.BlockSpec(memory_space=pltpu.VMEM)] * 7
+        specs += [pl.BlockSpec(memory_space=pltpu.SMEM)] * len(more)
+        return pl.pallas_call(
+            lambda *refs: apply_kernel(stage, *refs),
+            out_shape=out,
+            in_specs=specs,
+            out_specs=jax.tree.map(lambda _: specs[0], out),
+            compiler_params=pltpu.CompilerParams(vmem_limit_bytes=VMEM_LIMIT),
+        )(left, value, right, own_high, own_low, factor, scales, *more)
+
+    s1 = operator(1, k0[0:4], k0, f32(8, 16, 256), b_prev)
+    rest = call(rest_kernel, f32(8, 128), k0, raw, b_prev, scales)
+    k2x, k2w = operator(2, s1, s1, (f32(4, 16, 256), f32(4, 16, 256)))
+    k3 = operator(3, k2w, k2w, f32(4, 16, 256))
+
+    shares = call(share_kernel, f32(8, 72, 128), k0, s1, k2x, k2w, k3, rest)
     vectors = lax.all_to_all(shares, GROUP, 0, 0, tiled=True)
     grams = lax.all_to_all(call(total_kernel, f32(32, 8, 128), vectors), RING, 0, 0, tiled=True)
     image, coef, alphas, betas = call(

time: 118 us -> 116 us (0.983)
  local copies, waits for them, and re-layouts: 7.5 us -> 6.31 us
    pallas_call x11 -> x9, Pallas kernels: 9.31 us -> 7.49 us  [call(): pl.pallas_call(kernel, out_shape=out, in_specs=specs, out_specs=jax.tree....]
    pallas_call x0 -> x3, Pallas kernels: none -> 1.74 us  [operator(): pl.pallas_call(lambda *refs: apply_kernel(stage, *refs), out_shape=out, i...]
    unnamed x16 -> x18, local copies, waits for them, and re-layouts: 6.88 us -> 5.69 us
  transfers between devices with their start and end apart: 11 -> 11, of which waited for: 7 -> 7; matrix products, arithmetic and copies ran while one was open for 2% -> 2% of each run, Pallas kernels for 5% -> 4%
where the time goes in v4:
time: 116 us; the launch traced here: 115 us
  starting transfers between devices  36.4 us (31%)
  blocking collectives  30.6 us (26%)
  waiting for transfers between devices  25.6 us (22%)
  Pallas kernels  12.8 us (11%)
  local copies, waits for them, and re-layouts  6.31 us (5%)
  other arithmetic  2 us (2%)
  between operations  1.47 us (1%)
    all_to_all x1, blocking collectives, per_device(): lax.all_to_all(call(total_kernel, f32(32, 8, 128), vectors), RING, 0, 0,...  16.3 us
    all_to_all x1, blocking collectives, per_device(): vectors = lax.all_to_all(shares, GROUP, 0, 0, tiled=True)  14.3 us
    all_to_all x1, starting transfers between devices, per_device(): received = lax.all_to_all(packed, SEC, 0, 0, tiled=True)  13.2 us
    all_to_all x1, waiting for transfers between devices, per_device(): back = lax.all_to_all(image, SEC, 0, 0, tiled=True)  13 us
    ppermute x6, starting transfers between devices, beside(): return (lax.ppermute(value, RING, after), lax.ppermute(value, RING, before))  8.44 us
    pallas_call x9, Pallas kernels, call(): pl.pallas_call(kernel, out_shape=out, in_specs=specs, out_specs=jax.tree....  7.49 us
    all_to_all x1, starting transfers between devices, per_device(): back = lax.all_to_all(image, SEC, 0, 0, tiled=True)  6.15 us
    unnamed x18, local copies, waits for them, and re-layouts  5.69 us
  transfers between devices with their start and end apart: 11, of which 7 were waited for; matrix products, arithmetic and copies ran while one was open for 2% of the time, Pallas kernels for 4%

profile of v4, /device:TPU:1, one launch (start us, length us, event | category | flops | bytes accessed | tf_op | source)
XLA Modules:
  0.0 115.1 jit_solution(18238725866966688083)
XLA Ops:
  0.6 1.9 %shard_map.86.q_ref = f32[64,8,256]{2,1,0:T(8,128)} custom-call(s32[1]{0:T(128)} %bitcast.flip_ref, f32[8,4,2048]{2,1,0:T(4,128)} %q_ref.1, f32[8,4,2048]{2,1,0:T(4,128)} %p_ref.1), custom_call_target="tpu_custom_call" | custom-call | tf_op jit(solution)/shard_map/pallas_call | solution.py:98
  2.5 13.2 %all-to-all-start = ((f32[64,8,256]{2,1,0:T(8,128)}), f32[64,8,256]{2,1,0:T(8,128)S(1)}, u32[]{:S(2)}, u32[]{:S(2)}) async-start(f32[64,8,256]{2,1,0:T(8,128)} %shard_map.86.q_ref), calls=%async_computation | async-start | bytes 1048576 | tf_op jit(solution)/shard_map/all_to_all | solution.py:422
  15.7 2.5 %copy-done = f32[16,5,128,128]{3,2,1,0:T(8,128)S(1)} copy-done((f32[16,5,128,128]{3,2,1,0:T(8,128)S(1)}, f32[16,5,128,128]{3,2,1,0:T(8,128)}, u32[]{:S(2)}) %copy-start) | copy-done | bytes 5242904
  18.2 2.5 %copy-done.1 = f32[16,5,128,128]{3,2,1,0:T(8,128)S(1)} copy-done((f32[16,5,128,128]{3,2,1,0:T(8,128)S(1)}, f32[16,5,128,128]{3,2,1,0:T(8,128)}, u32[]{:S(2)}) %copy-start.1) | copy-done | bytes 5242904
  20.7 1.7 %shard_map.88 = (f32[6,8,128]{2,1,0:T(8,128)S(1)}, bf16[2,640,256]{2,1,0:T(8,128)(2,1)S(1)}, bf16[2,640,256]{2,1,0:T(8,128)(2,1)S(1)}) custom-call(s32[1]{0:T(128)S(6)} %add.60.pair_ref, f32[16,5,128,128]{3,2,1,0:T(8,128)S(1)} %copy-done, f32[16,5,128,128]{3,2,1,0:T(8,128)S(1)} %copy-done.1), custom_call_target="tpu_custom_call" | custom-call | tf_op jit(solution)/shard_map/pallas_call | solution.py:429
  22.6 1.2 %collective-permute-start.2 = (f32[6,128]{1,0:T(8,128)S(1)}, f32[6,128]{1,0:T(8,128)S(1)}, u32[]{:S(2)}, u32[]{:S(2)}) collective-permute-start(f32[6,128]{1,0:T(8,128)S(1)} %broadcast_in_dim.45), channel_id=1, source_target_pairs={{0,1},{1,0},{2,3},{3,2},{4,5},{5,4},{6,7},{7,6},{8,9},{9,8},{10,11... | collective-permute-start | bytes 9224 | tf_op jit(solution)/shard_map/ppermute | solution.py:413
  24.1 1.1 fusion.4.f_ref
  25.4 2.7 %collective-permute-start.3 = (f32[6,128]{1,0:T(8,128)S(1)}, f32[6,128]{1,0:T(8,128)S(1)}, u32[]{:S(2)}, u32[]{:S(2)}) collective-permute-start(f32[6,128]{1,0:T(8,128)S(1)} %broadcast_maximum_fusion), channel_id=1, source_target_pairs={{0,2},{1,3},{2,0},{3,1},{4,6},{5,7},{6,4},{7,5},{8,10},{9,11},{10,... | collective-permute-start | bytes 9224 | tf_op jit(solution)/shard_map/ppermute | solution.py:413
  30.6 2.9 %all-to-all-done.r_ref = f32[64,8,256]{2,1,0:T(8,128)S(1)} async-done(((f32[64,8,256]{2,1,0:T(8,128)}), f32[64,8,256]{2,1,0:T(8,128)S(1)}, u32[]{:S(2)}, u32[]{:S(2)}) %all-to-all-start) | async-done | bytes 524320 | tf_op jit(solution)/shard_map/all_to_all | solution.py:422
  33.4 1.0 shard_map.87
  34.4 4.7 %all-to-all-start.1 = ((f32[8,16,256]{2,1,0:T(8,128)}), f32[8,16,256]{2,1,0:T(8,128)S(1)}, u32[]{:S(2)}, u32[]{:S(2)}) async-start(f32[8,16,256]{2,1,0:T(8,128)} %shard_map.87), calls=%async_computation.1 | async-start | bytes 262144 | tf_op jit(solution)/shard_map/all_to_all | solution.py:452
  39.1 5.2 %all-to-all-done.1.refs_1_.k0_ref.k0 = f32[8,16,256]{2,1,0:T(8,128)S(1)} async-done(((f32[8,16,256]{2,1,0:T(8,128)}), f32[8,16,256]{2,1,0:T(8,128)S(1)}, u32[]{:S(2)}, u32[]{:S(2)}) %all-to-all-start.1) | async-done | bytes 131104 | tf_op jit(solution)/shard_map/all_to_all | solution.py:452
  44.7 2.3 %collective-permute-start.1 = (f32[4,16,256]{2,1,0:T(8,128)S(1)}, f32[4,16,256]{2,1,0:T(8,128)S(1)}, u32[]{:S(2)}, u32[]{:S(2)}) collective-permute-start(f32[4,16,256]{2,1,0:T(8,128)S(1)} %slice.28), channel_id=1, source_target_pairs={{32,0},{64,32},{96,64},{128,96},{160,128},{192,160},{224,192},{225... | collective-permute-start | bytes 196616 | tf_op jit(solution)/shard_map/ppermute | solution.py:409
  47.0 1.6 %collective-permute-done.refs_0_ = f32[4,16,256]{2,1,0:T(8,128)S(1)} collective-permute-done((f32[4,16,256]{2,1,0:T(8,128)S(1)}, f32[4,16,256]{2,1,0:T(8,128)S(1)}, u32[]{:S(2)}, u32[]{:S(2)}) %collective-permute-start) | collective-permute-done | bytes 65568 | tf_op jit(solution)/shard_map/ppermute | solution.py:409
  50.5 2.0 %collective-permute-start.5 = (f32[8,16,256]{2,1,0:T(8,128)S(1)}, f32[8,16,256]{2,1,0:T(8,128)S(1)}, u32[]{:S(2)}, u32[]{:S(2)}) collective-permute-start(f32[8,16,256]{2,1,0:T(8,128)S(1)} %shard_map.89.refs_1_.s1), channel_id=1, source_target_pairs={{32,0},{64,32},{96,64},{128,96},{160,128},{192,160},{224,192},{225... | collective-permute-start | bytes 393224 | tf_op jit(solution)/shard_map/ppermute | solution.py:409
  52.5 2.3 %collective-permute-done.4.refs_0_ = f32[8,16,256]{2,1,0:T(8,128)S(1)} collective-permute-done((f32[8,16,256]{2,1,0:T(8,128)S(1)}, f32[8,16,256]{2,1,0:T(8,128)S(1)}, u32[]{:S(2)}, u32[]{:S(2)}) %collective-permute-start.4) | collective-permute-done | bytes 131104 | tf_op jit(solution)/shard_map/ppermute | solution.py:409
  55.2 2.2 %collective-permute-start.6 = (f32[4,16,256]{2,1,0:T(8,128)S(1)}, f32[4,16,256]{2,1,0:T(8,128)S(1)}, u32[]{:S(2)}, u32[]{:S(2)}) collective-permute-start(f32[4,16,256]{2,1,0:T(8,128)S(1)} %get-tuple-element.19.refs_1_.k2w), channel_id=1, source_target_pairs={{0,32},{32,64},{64,96},{96,128},{128,160},{160,192},{192,224},{224... | collective-permute-start | bytes 196616 | tf_op jit(solution)/shard_map/ppermute | solution.py:409
  58.2 1.2 %shard_map.92.raw_ref = f32[8,128]{1,0:T(8,128)S(1)} custom-call(f32[8,4,2048]{2,1,0:T(4,128)S(1)} %copy-done.3, f32[8,4,2048]{2,1,0:T(4,128)S(1)} %copy-done.4), custom_call_target="tpu_custom_call" | custom-call | tf_op jit(solution)/shard_map/pallas_call | solution.py:49
  61.5 14.3 %all_to_all.25.v_ref = f32[8,72,128]{2,1,0:T(8,128)S(1)} all-to-all(f32[8,72,128]{2,1,0:T(8,128)S(1)} %shard_map.94), channel_id=1, replica_groups=mesh['z'=8,'y'=4,'core'=2,'xs'=4] {'y','core'}, dimensions={0} | all-to-all | bytes 589824 | tf_op jit(solution)/shard_map/all_to_all | solution.py:472
  75.8 16.3 %all_to_all.26.g_ref = f32[32,8,128]{2,1,0:T(8,128)S(1)} all-to-all(f32[32,8,128]{2,1,0:T(8,128)S(1)} %shard_map.95), channel_id=1, replica_groups=mesh['z'=8,'y'=4,'core'=2,'xs'=4] {'z','xs'}, dimensions={0} | all-to-all | bytes 262144 | tf_op jit(solution)/shard_map/all_to_all | solution.py:473
  92.1 2.6 %shard_map.96 = (f32[64,8,128]{2,1,0:T(8,128)}, f32[4,128]{1,0:T(4,128)S(1)}, f32[3,4,4]{2,1,0:T(4,128)}, f32[3,4,4]{2,1,0:T(4,128)}) custom-call(f32[32,8,128]{2,1,0:T(8,128)S(1)} %all_to_all.26.g_ref, f32[4,4]{1,0:T(4,128)S(1)} %copy-done.7, f32[8,128]{1,0:T(8,128)S(1)} %stack.2.refs_6_.k_ref, f32[8,72,128]{2,1,0:T(8,128)S(1)} %all_to_all.25.v_ref, ...), custom_call_target="tpu_custom_call" | custom-call | tf_op jit(solution)/shard_map/pallas_call | solution.py:49
  94.7 6.2 %all-to-all-start.4 = ((f32[64,8,128]{2,1,0:T(8,128)}), f32[64,8,128]{2,1,0:T(8,128)S(1)}, u32[]{:S(2)}, u32[]{:S(2)}) async-start(f32[64,8,128]{2,1,0:T(8,128)} %get-tuple-element.21), calls=%async_computation.4 | async-start | bytes 524288 | tf_op jit(solution)/shard_map/all_to_all | solution.py:479
  101.1 13.0 %all-to-all-done.4.r_ref = f32[64,8,128]{2,1,0:T(8,128)S(1)} async-done(((f32[64,8,128]{2,1,0:T(8,128)}), f32[64,8,128]{2,1,0:T(8,128)S(1)}, u32[]{:S(2)}, u32[]{:S(2)}) %all-to-all-start.4) | async-done | bytes 262176 | tf_op jit(solution)/shard_map/all_to_all | solution.py:479
  114.1 1.0 shard_map.98
  (49 shorter events, 8.3 us)
Async XLA Ops:
  2.5 30.9 %all-to-all-start = ((f32[64,8,256]{2,1,0:T(8,128)}), f32[64,8,256]{2,1,0:T(8,128)S(1)}, u32[]{:S(2)}, u32[]{:S(2)}) async-start(f32[64,8,256]{2,1,0:T(8,128)} %shard_map.86.q_ref), calls=%async_computation | async-start | bytes 1048576 | tf_op jit(solution)/shard_map/all_to_all | solution.py:422
  15.7 2.5 %copy-start = (f32[16,5,128,128]{3,2,1,0:T(8,128)S(1)}, f32[16,5,128,128]{3,2,1,0:T(8,128)}, u32[]{:S(2)}) copy-start(f32[16,5,128,128]{3,2,1,0:T(8,128)} %s_ref.1) | copy-start | bytes 15728644
  18.2 2.5 %copy-start.1 = (f32[16,5,128,128]{3,2,1,0:T(8,128)S(1)}, f32[16,5,128,128]{3,2,1,0:T(8,128)}, u32[]{:S(2)}) copy-start(f32[16,5,128,128]{3,2,1,0:T(8,128)} %c_ref.1) | copy-start | bytes 15728644
  20.7 3.1 %copy-start.8 = (s32[64]{0:T(128)S(1)}, s32[64]{0:T(128)}, u32[]{:S(2)}) copy-start(s32[64]{0:T(128)} %param.12) | copy-start | bytes 772
  20.7 28.0 %copy-start.7 = (f32[4,4]{1,0:T(4,128)S(1)}, f32[4,4]{1,0:T(4,128)}, u32[]{:S(2)}) copy-start(f32[4,4]{1,0:T(4,128)} %b_ref.3) | copy-start | bytes 196
  22.4 35.8 %copy-start.3 = (f32[8,4,2048]{2,1,0:T(4,128)S(1)}, f32[8,4,2048]{2,1,0:T(4,128)}, u32[]{:S(2)}) copy-start(f32[8,4,2048]{2,1,0:T(4,128)} %q_ref.1) | copy-start | bytes 786436
  22.4 35.8 %copy-start.4 = (f32[8,4,2048]{2,1,0:T(4,128)S(1)}, f32[8,4,2048]{2,1,0:T(4,128)}, u32[]{:S(2)}) copy-start(f32[8,4,2048]{2,1,0:T(4,128)} %p_ref.1) | copy-start | bytes 786436
  22.6 2.8 %collective-permute-start.2 = (f32[6,128]{1,0:T(8,128)S(1)}, f32[6,128]{1,0:T(8,128)S(1)}, u32[]{:S(2)}, u32[]{:S(2)}) collective-permute-start(f32[6,128]{1,0:T(8,128)S(1)} %broadcast_in_dim.45), channel_id=1, source_target_pairs={{0,1},{1,0},{2,3},{3,2},{4,5},{5,4},{6,7},{7,6},{8,9},{9,8},{10,11... | collective-permute-start | bytes 9224 | tf_op jit(solution)/shard_map/ppermute | solution.py:413
  25.4 13.6 %collective-permute-start.3 = (f32[6,128]{1,0:T(8,128)S(1)}, f32[6,128]{1,0:T(8,128)S(1)}, u32[]{:S(2)}, u32[]{:S(2)}) collective-permute-start(f32[6,128]{1,0:T(8,128)S(1)} %broadcast_maximum_fusion), channel_id=1, source_target_pairs={{0,2},{1,3},{2,0},{3,1},{4,6},{5,7},{6,4},{7,5},{8,10},{9,11},{10,... | collective-permute-start | bytes 9224 | tf_op jit(solution)/shard_map/ppermute | solution.py:413
  28.8 72.0 %copy-start.2 = (f32[64,8,256]{2,1,0:T(8,128)S(1)}, f32[64,8,256]{2,1,0:T(8,128)}, u32[]{:S(2)}) copy-start(f32[64,8,256]{2,1,0:T(8,128)} %shard_map.86.q_ref) | copy-start | bytes 1572868
  29.0 0.7 copy-start.5
  29.7 62.4 %copy-start.6 = (bf16[512,256]{1,0:T(8,128)(2,1)S(1)}, bf16[512,256]{1,0:T(8,128)(2,1)}, u32[]{:S(2)}) copy-start(bf16[512,256]{1,0:T(8,128)(2,1)} %copy-done.5) | copy-start | bytes 786436
  34.4 9.9 %all-to-all-start.1 = ((f32[8,16,256]{2,1,0:T(8,128)}), f32[8,16,256]{2,1,0:T(8,128)S(1)}, u32[]{:S(2)}, u32[]{:S(2)}) async-start(f32[8,16,256]{2,1,0:T(8,128)} %shard_map.87), calls=%async_computation.1 | async-start | bytes 262144 | tf_op jit(solution)/shard_map/all_to_all | solution.py:452
  44.3 4.3 %collective-permute-start = (f32[4,16,256]{2,1,0:T(8,128)S(1)}, f32[4,16,256]{2,1,0:T(8,128)S(1)}, u32[]{:S(2)}, u32[]{:S(2)}) collective-permute-start(f32[4,16,256]{2,1,0:T(8,128)S(1)} %slice.28), channel_id=1, source_target_pairs={{0,32},{32,64},{64,96},{96,128},{128,160},{160,192},{192,224},{224... | collective-permute-start | bytes 196616 | tf_op jit(solution)/shard_map/ppermute | solution.py:409
  44.7 4.0 %collective-permute-start.1 = (f32[4,16,256]{2,1,0:T(8,128)S(1)}, f32[4,16,256]{2,1,0:T(8,128)S(1)}, u32[]{:S(2)}, u32[]{:S(2)}) collective-permute-start(f32[4,16,256]{2,1,0:T(8,128)S(1)} %slice.28), channel_id=1, source_target_pairs={{32,0},{64,32},{96,64},{128,96},{160,128},{192,160},{224,192},{225... | collective-permute-start | bytes 196616 | tf_op jit(solution)/shard_map/ppermute | solution.py:409
  49.6 5.1 %collective-permute-start.4 = (f32[8,16,256]{2,1,0:T(8,128)S(1)}, f32[8,16,256]{2,1,0:T(8,128)S(1)}, u32[]{:S(2)}, u32[]{:S(2)}) collective-permute-start(f32[8,16,256]{2,1,0:T(8,128)S(1)} %shard_map.89.refs_1_.s1), channel_id=1, source_target_pairs={{0,32},{32,64},{64,96},{96,128},{128,160},{160,192},{192,224},{224... | collective-permute-start | bytes 393224 | tf_op jit(solution)/shard_map/ppermute | solution.py:409
  50.5 4.3 %collective-permute-start.5 = (f32[8,16,256]{2,1,0:T(8,128)S(1)}, f32[8,16,256]{2,1,0:T(8,128)S(1)}, u32[]{:S(2)}, u32[]{:S(2)}) collective-permute-start(f32[8,16,256]{2,1,0:T(8,128)S(1)} %shard_map.89.refs_1_.s1), channel_id=1, source_target_pairs={{32,0},{64,32},{96,64},{128,96},{160,128},{192,160},{224,192},{225... | collective-permute-start | bytes 393224 | tf_op jit(solution)/shard_map/ppermute | solution.py:409
  55.2 4.9 %collective-permute-start.6 = (f32[4,16,256]{2,1,0:T(8,128)S(1)}, f32[4,16,256]{2,1,0:T(8,128)S(1)}, u32[]{:S(2)}, u32[]{:S(2)}) collective-permute-start(f32[4,16,256]{2,1,0:T(8,128)S(1)} %get-tuple-element.19.refs_1_.k2w), channel_id=1, source_target_pairs={{0,32},{32,64},{64,96},{96,128},{128,160},{160,192},{192,224},{224... | collective-permute-start | bytes 196616 | tf_op jit(solution)/shard_map/ppermute | solution.py:409
  57.4 3.1 %collective-permute-start.7 = (f32[4,16,256]{2,1,0:T(8,128)S(1)}, f32[4,16,256]{2,1,0:T(8,128)S(1)}, u32[]{:S(2)}, u32[]{:S(2)}) collective-permute-start(f32[4,16,256]{2,1,0:T(8,128)S(1)} %get-tuple-element.19.refs_1_.k2w), channel_id=1, source_target_pairs={{32,0},{64,32},{96,64},{128,96},{160,128},{192,160},{224,192},{225... | collective-permute-start | bytes 196616 | tf_op jit(solution)/shard_map/ppermute | solution.py:409
  94.7 19.4 %all-to-all-start.4 = ((f32[64,8,128]{2,1,0:T(8,128)}), f32[64,8,128]{2,1,0:T(8,128)S(1)}, u32[]{:S(2)}, u32[]{:S(2)}) async-start(f32[64,8,128]{2,1,0:T(8,128)} %get-tuple-element.21), calls=%async_computation.4 | async-start | bytes 524288 | tf_op jit(solution)/shard_map/all_to_all | solution.py:479

commit v5 on v4

--- a/solution.py
+++ b/solution.py
@@ -40,28 +40,27 @@
     return lax.dot_general(a, b, (((1,), (0,)), ((), ())), preferred_element_type=jnp.float32)
 
 
-def call(kernel, out, *args, scalar=None, **kw):
+def call(kernel, out, *args):
     whole = pl.BlockSpec(memory_space=pltpu.VMEM)
-    specs = [whole] * len(args)
-    if scalar is not None:
-        specs = [pl.BlockSpec(memory_space=pltpu.SMEM)] + specs
-        args = (scalar,) + args
     return pl.pallas_call(
         kernel,
         out_shape=out,
-        in_specs=specs,
+        in_specs=[whole] * len(args),
         out_specs=jax.tree.map(lambda _: whole, out),
         compiler_params=pltpu.CompilerParams(vmem_limit_bytes=VMEM_LIMIT),
-        **kw,
     )(*args)
+
+
+def odd_slab():
+    return lax.rem(lax.axis_index("xs"), 2)
 
 
 def turned(pair, flip):
     return pair + flip * (7 - 2 * pair)
 
 
-def pack_kernel(flip_ref, q_hbm, p_hbm, out_hbm, q_ref, p_ref, o_ref, in_sem, out_sem):
-    flip = flip_ref[0]
+def pack_kernel(q_hbm, p_hbm, out_hbm, q_ref, p_ref, o_ref, in_sem, out_sem):
+    flip = odd_slab()
     arriving = []
     for i in range(4):
         lanes = pl.ds(i * 512, 512)
@@ -93,12 +92,12 @@
         copy.wait()
 
 
-def pack(flip, q_block, q_prev):
+def pack(q_block, q_prev):
     hbm = pl.BlockSpec(memory_space=pltpu.HBM)
     return pl.pallas_call(
         pack_kernel,
         out_shape=f32(64, 8, 256),
-        in_specs=[pl.BlockSpec(memory_space=pltpu.SMEM), hbm, hbm],
+        in_specs=[hbm, hbm],
         out_specs=hbm,
         scratch_shapes=[
             pltpu.VMEM((8, 4, 2048), jnp.float32),
@@ -108,7 +107,7 @@
             pltpu.SemaphoreType.DMA((8,)),
         ],
         compiler_params=pltpu.CompilerParams(vmem_limit_bytes=PACK_LIMIT),
-    )(flip, q_block, q_prev)
+    )(q_block, q_prev)
 
 
 def raw_kernel(q_ref, p_ref, gram_ref):
@@ -140,7 +139,7 @@
     out_ref[:, 0:8] = dot(dot(change, outside), change, NT)
 
 
-def stats_kernel(pair_ref, s_ref, c_ref, out_ref, high_ref, low_ref):
+def stats_kernel(pair_ref, s_ref, c_ref, out_ref, high_ref, low_ref, best_ref):
     step = pl.program_id(0)
     row = lax.broadcasted_iota(jnp.int32, (128, 128), 0)
     col = lax.broadcasted_iota(jnp.int32, (128, 128), 1)
@@ -157,12 +156,19 @@
     @pl.when(step == 0)
     def _():
         for i, v in enumerate(found):
-            out_ref[i] = v
+            best_ref[i] = v
 
     @pl.when(step > 0)
     def _():
         for i, v in enumerate(found):
-            out_ref[i] = jnp.maximum(out_ref[i], v)
+            best_ref[i] = jnp.maximum(best_ref[i], v)
+
+    @pl.when(step == 15)
+    def _():
+        out_ref[...] = jnp.zeros((8, 128), jnp.float32)
+        for i in range(6):
+            best = jnp.max(best_ref[i], axis=(0, 1), keepdims=True)
+            out_ref[i : i + 1] = best + jnp.zeros((1, 128), jnp.float32)
 
     for half in range(2):
 
@@ -181,7 +187,8 @@
     turned_ref[:, 0:128], turned_ref[:, 128:256] = high, low
 
 
-def forward_kernel(f_ref, r_ref, out_ref):
+def forward_kernel(f_ref, r_ref, *refs):
+    out_ref = refs[-1]
     high, low = split(r_ref[...].reshape(SECTORS, 256))
     both = fast(f_ref[...], high)
     out_ref[...] = (both[:128] + both[128:] + fast(f_ref[0:128], low)).reshape(8, 16, 256)
@@ -209,9 +216,9 @@
             value = value * inverse
             out_ref[0:4, :, here] = value
             for i in range(4):
-                taken = b_ref[i, 0] * own_ref[4, :, here]
+                taken = b_ref[4 * i : 4 * i + 1] * own_ref[4, :, here]
                 for l in range(1, 4):
-                    taken += b_ref[i, l] * own_ref[4 + l, :, here]
+                    taken += b_ref[4 * i + l : 4 * i + l + 1] * own_ref[4 + l, :, here]
                 out_ref[4 + i, :, here] = value[i] - inverse[0] * taken
         elif stage == 2:
             x_ref, w_ref = refs
@@ -334,15 +341,17 @@
     coef_ref[:, 4:8] = -k_ref[1:2, 0:1] * behind
     cur += pltpu.roll(jnp.where((lane >= 4) & (lane < 8), cur, 0.0), 4, 1)
     group = lane[0:1] // 32
-    spread = (lane // 32 == row).astype(jnp.float32)
-    weights = dot(cur, spread, TN)
+    own = lane // 32 == row
+    weights = [
+        jnp.sum(jnp.where(own, cur[:, k : k + 1], 0.0), axis=0, keepdims=True) for k in range(8, 24)
+    ]
     field = jnp.zeros((128, 128), jnp.float32)
     for m in range(4):
         tile = v_ref[:, m * 16 : m * 16 + 16].reshape(128, 128)
         for by in range(4):
             line = None
             for c in range(4):
-                from_row = weights[8 + 4 * m + c : 9 + 4 * m + c, :]
+                from_row = weights[4 * m + c]
                 line = from_row if line is None else jnp.where(group == (c + by) % 4, from_row, line)
             field += line * (pltpu.roll(tile, 32 * by, 1) if by else tile)
     high, low = split(field)
@@ -354,29 +363,18 @@
     image_ref[...] = (both[:, :128] + both[:, 128:]).reshape(64, 8, 128)
 
 
-def base_kernel(flip_ref, q_ref, coef_ref, out_ref):
-    flip = flip_ref[0]
+def last_kernel(r_ref, q_ref, coef_ref, out_ref):
+    flip = odd_slab()
+    group = lax.broadcasted_iota(jnp.int32, (8, 128), 1) // 32
     coef = coef_ref[...]
     scalars = [
-        [coef[c : c + 1, k : k + 1] + jnp.zeros((8, 256), jnp.float32) for k in range(8)]
+        [coef[c : c + 1, k : k + 1] + jnp.zeros((8, 128), jnp.float32) for k in range(8)]
         for c in range(4)
     ]
     for pair in range(8):
         place = turned(pair, flip) * 8
-        tiles = [q_ref[place + k] for k in range(8)]
-        for c in range(4):
-            total = scalars[c][0] * tiles[0]
-            for k in range(1, 8):
-                total += scalars[c][k] * tiles[k]
-            out_ref[pair, c] = total
-
-
-def last_kernel(flip_ref, r_ref, base_ref, out_ref):
-    flip = flip_ref[0]
-    group = lax.broadcasted_iota(jnp.int32, (8, 128), 1) // 32
-    for pair in range(8):
-        place = turned(pair, flip) * 8
         for half in range(2):
+            lanes = slice(half * 128, half * 128 + 128)
             tiles = [r_ref[place + half * 4 + q] for q in range(4)]
             for c in range(4):
                 value = None
@@ -384,7 +382,8 @@
                     by = (q - c) % 4 * 32
                     moved = pltpu.roll(tiles[q], by, 1) if by else tiles[q]
                     value = moved if value is None else jnp.where(group == q, moved, value)
-                value += base_ref[pair, c, :, half * 128 : half * 128 + 128]
+                for k in range(8):
+                    value += scalars[c][k] * q_ref[place + k, :, lanes]
                 out_ref[:, c, pl.ds(pair * 256 + half * 128, 128)] = value
 
 
@@ -414,11 +413,11 @@
 
 
 def per_device(q_block, q_prev, b_prev, stiff_blocks, couple_blocks, block_cols, assign):
-    flip = (lax.axis_index("xs") % 2).astype(jnp.int32).reshape(1)
-    pair = turned(lax.axis_index("z"), flip)
     group = lax.axis_index("y") * 2 + lax.axis_index("core")
 
-    packed = pack(flip, q_block, q_prev)
+    pair = turned(lax.axis_index("z"), odd_slab()).astype(jnp.int32).reshape(1)
+    packed = pack(q_block, q_prev)
+    packed, pair = lax.optimization_barrier((packed, pair))
     received = lax.all_to_all(packed, SEC, 0, 0, tiled=True)
 
     forward, inverse = call(table_kernel, (bf16(256, 512), bf16(512, 256)), table(assign))
@@ -428,42 +427,40 @@
     raw = call(raw_kernel, f32(8, 128), q_block, q_prev)
     found, own_high, own_low = pl.pallas_call(
         stats_kernel,
-        out_shape=(f32(6, 8, 128), bf16(2, 640, 256), bf16(2, 640, 256)),
+        out_shape=(f32(8, 128), bf16(2, 640, 256), bf16(2, 640, 256)),
         grid_spec=pltpu.PrefetchScalarGridSpec(
             num_scalar_prefetch=1,
             grid=(16,),
             in_specs=[pl.BlockSpec((1, 5, 128, 128), lambda i, p: (i, 0, 0, 0))] * 2,
             out_specs=(
-                pl.BlockSpec((6, 8, 128), lambda i, p: (0, 0, 0)),
+                pl.BlockSpec((8, 128), lambda i, p: (0, 0)),
                 pl.BlockSpec((2, 640, 256), lambda i, p: (0, 0, 0)),
                 pl.BlockSpec((2, 640, 256), lambda i, p: (0, 0, 0)),
             ),
+            scratch_shapes=[pltpu.VMEM((6, 8, 128), jnp.float32)],
         ),
         compiler_params=pltpu.CompilerParams(vmem_limit_bytes=VMEM_LIMIT),
     )(pair, stiff_blocks, couple_blocks)
-    found = jnp.broadcast_to(jnp.max(found, axis=(1, 2))[:, None], (6, 128))
     found = highest(highest(found, 1), 2)
     sigma = 0.5 * (found[1] - found[2]) + jnp.mean(factors) * (0.5 * (found[4] - found[5]))
     scale = found[0] + found[3]
     scale = jnp.where(scale > 0, scale, 1.0)
     scales = jnp.stack([sigma, 1.0 / scale, scale] + [scale] * 5)
 
-    spectrum = call(forward_kernel, f32(8, 16, 256), forward, received)
+    b_rows = jnp.broadcast_to(b_prev.reshape(16, 1), (16, 128))
+    spectrum = call(
+        forward_kernel, f32(8, 16, 256), forward, received, scales, factor, b_rows
+    )
     k0 = lax.all_to_all(spectrum, GROUP, 0, 0, tiled=True)
 
     def operator(stage, sent, value, out, *more):
         left, right = beside(sent)
-        specs = [pl.BlockSpec(memory_space=pltpu.VMEM)] * 7
-        specs += [pl.BlockSpec(memory_space=pltpu.SMEM)] * len(more)
-        return pl.pallas_call(
+        return call(
             lambda *refs: apply_kernel(stage, *refs),
-            out_shape=out,
-            in_specs=specs,
-            out_specs=jax.tree.map(lambda _: specs[0], out),
-            compiler_params=pltpu.CompilerParams(vmem_limit_bytes=VMEM_LIMIT),
-        )(left, value, right, own_high, own_low, factor, scales, *more)
-
-    s1 = operator(1, k0[0:4], k0, f32(8, 16, 256), b_prev)
+            out, left, value, right, own_high, own_low, factor, scales, *more,
+        )
+
+    s1 = operator(1, k0[0:4], k0, f32(8, 16, 256), b_rows)
     rest = call(rest_kernel, f32(8, 128), k0, raw, b_prev, scales)
     k2x, k2w = operator(2, s1, s1, (f32(4, 16, 256), f32(4, 16, 256)))
     k3 = operator(3, k2w, k2w, f32(4, 16, 256))
@@ -477,8 +474,7 @@
         grams, b_prev, scales, vectors, inverse,
     )
     back = lax.all_to_all(image, SEC, 0, 0, tiled=True)
-    base = call(base_kernel, f32(8, 4, 8, 256), packed, coef, scalar=flip)
-    out = call(last_kernel, f32(8, 4, 2048), back, base, scalar=flip)
+    out = call(last_kernel, f32(8, 4, 2048), back, packed, coef)
     return out, alphas, betas
 
 

time: 116 us -> 113 us (0.974)
  blocking collectives: 30.6 us -> 59.2 us
  waiting for transfers between devices: 25.6 us -> 7.56 us
  starting transfers between devices: 36.4 us -> 25.6 us
  Pallas kernels: 12.8 us -> 11.1 us
    all_to_all x0 -> x2, blocking collectives: none -> 28.3 us  [the longest x1 18.6 us: per_device(): back = lax.all_to_all(image, SEC, 0, 0, tiled=True)]
    all_to_all x2 -> x0, waiting for transfers between devices: 18.2 us -> none  [the longest x1 13 us: per_device(): back = lax.all_to_all(image, SEC, 0, 0, tiled=True)]
    all_to_all x2 -> x0, starting transfers between devices: 10.8 us -> none  [the longest x1 6.15 us: per_device(): back = lax.all_to_all(image, SEC, 0, 0, tiled=True)]
    pallas_call x14 -> x13, Pallas kernels: 12.8 us -> 11.1 us  [the longest x11 7.36 us: call(): pl.pallas_call(kernel, out_shape=out, in_specs=[whole] * len(args), out_s...]
    unnamed x18 -> x14, local copies, waits for them, and re-layouts: 5.69 us -> 4.99 us
  transfers between devices with their start and end apart: 11 -> 9, of which waited for: 7 -> 4; matrix products, arithmetic and copies ran while one was open for 2% -> 2% of each run, Pallas kernels for 4% -> 4%
where the time goes in v5:
time: 113 us; the launch traced here: 112 us
  blocking collectives  59.2 us (52%)
  starting transfers between devices  25.6 us (23%)
  Pallas kernels  11.1 us (10%)
  waiting for transfers between devices  7.56 us (7%)
  local copies, waits for them, and re-layouts  5.69 us (5%)
  other arithmetic  1.74 us (2%)
  between operations  1.47 us (1%)
    all_to_all x1, blocking collectives, per_device(): back = lax.all_to_all(image, SEC, 0, 0, tiled=True)  18.6 us
    all_to_all x1, blocking collectives, per_device(): lax.all_to_all(call(total_kernel, f32(32, 8, 128), vectors), RING, 0, 0,...  16.5 us
    all_to_all x1, blocking collectives, per_device(): vectors = lax.all_to_all(shares, GROUP, 0, 0, tiled=True)  14.4 us
    all_to_all x1, starting transfers between devices, per_device(): received = lax.all_to_all(packed, SEC, 0, 0, tiled=True)  13.2 us
    all_to_all x1, blocking collectives, per_device(): k0 = lax.all_to_all(spectrum, GROUP, 0, 0, tiled=True)  9.72 us
    ppermute x6, starting transfers between devices, beside(): return (lax.ppermute(value, RING, after), lax.ppermute(value, RING, before))  8.44 us
    pallas_call x11, Pallas kernels, call(): pl.pallas_call(kernel, out_shape=out, in_specs=[whole] * len(args), out_s...  7.36 us
    unnamed x14, local copies, waits for them, and re-layouts  4.99 us
  transfers between devices with their start and end apart: 9, of which 4 were waited for; matrix products, arithmetic and copies ran while one was open for 2% of the time, Pallas kernels for 4%

profile of v5, /device:TPU:1, one launch (start us, length us, event | category | flops | bytes accessed | tf_op | source)
XLA Modules:
  0.0 112.4 jit_solution(15865384206593277360)
XLA Ops:
  0.6 1.9 %shard_map.86.q_ref = f32[64,8,256]{2,1,0:T(8,128)} custom-call(f32[8,4,2048]{2,1,0:T(4,128)} %q_ref.1, f32[8,4,2048]{2,1,0:T(4,128)} %p_ref.1), custom_call_target="tpu_custom_call" | custom-call | tf_op jit(solution)/shard_map/pallas_call | solution.py:97
  2.5 13.2 %all-to-all-start = ((f32[64,8,256]{2,1,0:T(8,128)}), f32[64,8,256]{2,1,0:T(8,128)S(1)}, u32[]{:S(2)}, u32[]{:S(2)}) async-start(f32[64,8,256]{2,1,0:T(8,128)} %shard_map.86.q_ref), calls=%async_computation | async-start | bytes 1048576 | tf_op jit(solution)/shard_map/all_to_all | solution.py:421
  15.7 2.5 %copy-done = f32[16,5,128,128]{3,2,1,0:T(8,128)S(1)} copy-done((f32[16,5,128,128]{3,2,1,0:T(8,128)S(1)}, f32[16,5,128,128]{3,2,1,0:T(8,128)}, u32[]{:S(2)}) %copy-start) | copy-done | bytes 5242904
  18.2 2.5 %copy-done.1 = f32[16,5,128,128]{3,2,1,0:T(8,128)S(1)} copy-done((f32[16,5,128,128]{3,2,1,0:T(8,128)S(1)}, f32[16,5,128,128]{3,2,1,0:T(8,128)}, u32[]{:S(2)}) %copy-start.1) | copy-done | bytes 5242904
  20.7 1.9 %shard_map.87 = (f32[8,128]{1,0:T(8,128)S(1)}, bf16[2,640,256]{2,1,0:T(8,128)(2,1)S(1)}, bf16[2,640,256]{2,1,0:T(8,128)(2,1)S(1)}) custom-call(s32[1]{0:T(128)} %bitcast.pair_ref, f32[16,5,128,128]{3,2,1,0:T(8,128)S(1)} %copy-done, f32[16,5,128,128]{3,2,1,0:T(8,128)S(1)} %copy-done.1), custom_call_target="tpu_custom_call" | custom-call | tf_op jit(solution)/shard_map/pallas_call | solution.py:428
  22.6 1.3 %collective-permute-start = (f32[8,128]{1,0:T(8,128)S(1)}, f32[8,128]{1,0:T(8,128)S(1)}, u32[]{:S(2)}, u32[]{:S(2)}) collective-permute-start(f32[8,128]{1,0:T(8,128)S(1)} %get-tuple-element.19), channel_id=1, source_target_pairs={{0,1},{1,0},{2,3},{3,2},{4,5},{5,4},{6,7},{7,6},{8,9},{9,8},{10,11... | collective-permute-start | bytes 12296 | tf_op jit(solution)/shard_map/ppermute | solution.py:412
  24.1 1.1 fusion.4.f_ref
  25.4 2.7 %collective-permute-start.1 = (f32[8,128]{1,0:T(8,128)S(1)}, f32[8,128]{1,0:T(8,128)S(1)}, u32[]{:S(2)}, u32[]{:S(2)}) collective-permute-start(f32[8,128]{1,0:T(8,128)S(1)} %max.6), channel_id=1, source_target_pairs={{0,2},{1,3},{2,0},{3,1},{4,6},{5,7},{6,4},{7,5},{8,10},{9,11},{10,... | collective-permute-start | bytes 12296 | tf_op jit(solution)/shard_map/ppermute | solution.py:412
  28.2 0.6 multiply_cosine_fusion
  30.0 3.4 %all-to-all-done.r_ref = f32[64,8,256]{2,1,0:T(8,128)S(1)} async-done(((f32[64,8,256]{2,1,0:T(8,128)}), f32[64,8,256]{2,1,0:T(8,128)S(1)}, u32[]{:S(2)}, u32[]{:S(2)}) %all-to-all-start) | async-done | bytes 524320 | tf_op jit(solution)/shard_map/all_to_all | solution.py:421
  33.9 9.7 %all_to_all.25.refs_1_.k0_ref.k0 = f32[8,16,256]{2,1,0:T(8,128)S(1)} all-to-all(f32[8,16,256]{2,1,0:T(8,128)S(1)} %shard_map.88), channel_id=1, replica_groups=mesh['z'=8,'y'=4,'core'=2,'xs'=4] {'y','core'}, dimensions={0} | all-to-all | bytes 262144 | tf_op jit(solution)/shard_map/all_to_all | solution.py:454
  43.9 2.3 %collective-permute-start.3 = (f32[4,16,256]{2,1,0:T(8,128)S(1)}, f32[4,16,256]{2,1,0:T(8,128)S(1)}, u32[]{:S(2)}, u32[]{:S(2)}) collective-permute-start(f32[4,16,256]{2,1,0:T(8,128)S(1)} %slice.28), channel_id=1, source_target_pairs={{32,0},{64,32},{96,64},{128,96},{160,128},{192,160},{224,192},{225... | collective-permute-start | bytes 196616 | tf_op jit(solution)/shard_map/ppermute | solution.py:408
  46.3 1.6 %collective-permute-done.2.refs_0_ = f32[4,16,256]{2,1,0:T(8,128)S(1)} collective-permute-done((f32[4,16,256]{2,1,0:T(8,128)S(1)}, f32[4,16,256]{2,1,0:T(8,128)S(1)}, u32[]{:S(2)}, u32[]{:S(2)}) %collective-permute-start.2) | collective-permute-done | bytes 65568 | tf_op jit(solution)/shard_map/ppermute | solution.py:408
  48.5 2.6 %collective-permute-start.5 = (f32[8,16,256]{2,1,0:T(8,128)S(1)}, f32[8,16,256]{2,1,0:T(8,128)S(1)}, u32[]{:S(2)}, u32[]{:S(2)}) collective-permute-start(f32[8,16,256]{2,1,0:T(8,128)S(1)} %shard_map.89.refs_1_.s1), channel_id=1, source_target_pairs={{32,0},{64,32},{96,64},{128,96},{160,128},{192,160},{224,192},{225... | collective-permute-start | bytes 393224 | tf_op jit(solution)/shard_map/ppermute | solution.py:408
  51.1 2.3 %collective-permute-done.4.refs_0_ = f32[8,16,256]{2,1,0:T(8,128)S(1)} collective-permute-done((f32[8,16,256]{2,1,0:T(8,128)S(1)}, f32[8,16,256]{2,1,0:T(8,128)S(1)}, u32[]{:S(2)}, u32[]{:S(2)}) %collective-permute-start.4) | collective-permute-done | bytes 131104 | tf_op jit(solution)/shard_map/ppermute | solution.py:408
  53.9 1.8 %collective-permute-start.6 = (f32[4,16,256]{2,1,0:T(8,128)S(1)}, f32[4,16,256]{2,1,0:T(8,128)S(1)}, u32[]{:S(2)}, u32[]{:S(2)}) collective-permute-start(f32[4,16,256]{2,1,0:T(8,128)S(1)} %get-tuple-element.23.refs_1_.k2w), channel_id=1, source_target_pairs={{0,32},{32,64},{64,96},{96,128},{128,160},{160,192},{192,224},{224... | collective-permute-start | bytes 196616 | tf_op jit(solution)/shard_map/ppermute | solution.py:408
  55.7 1.1 %collective-permute-start.7 = (f32[4,16,256]{2,1,0:T(8,128)S(1)}, f32[4,16,256]{2,1,0:T(8,128)S(1)}, u32[]{:S(2)}, u32[]{:S(2)}) collective-permute-start(f32[4,16,256]{2,1,0:T(8,128)S(1)} %get-tuple-element.23.refs_1_.k2w), channel_id=1, source_target_pairs={{32,0},{64,32},{96,64},{128,96},{160,128},{192,160},{224,192},{225... | collective-permute-start | bytes 196616 | tf_op jit(solution)/shard_map/ppermute | solution.py:408
  56.8 1.2 %shard_map.92.raw_ref = f32[8,128]{1,0:T(8,128)S(1)} custom-call(f32[8,4,2048]{2,1,0:T(4,128)S(1)} %copy-done.3, f32[8,4,2048]{2,1,0:T(4,128)S(1)} %copy-done.4), custom_call_target="tpu_custom_call" | custom-call | tf_op jit(solution)/shard_map/pallas_call | solution.py:45
  58.1 0.7 shard_map.93.rest_ref
  59.7 14.4 %all_to_all.26.v_ref = f32[8,72,128]{2,1,0:T(8,128)S(1)} all-to-all(f32[8,72,128]{2,1,0:T(8,128)S(1)} %shard_map.94), channel_id=1, replica_groups=mesh['z'=8,'y'=4,'core'=2,'xs'=4] {'y','core'}, dimensions={0} | all-to-all | bytes 589824 | tf_op jit(solution)/shard_map/all_to_all | solution.py:469
  74.1 16.5 %all_to_all.27.g_ref = f32[32,8,128]{2,1,0:T(8,128)S(1)} all-to-all(f32[32,8,128]{2,1,0:T(8,128)S(1)} %shard_map.95), channel_id=1, replica_groups=mesh['z'=8,'y'=4,'core'=2,'xs'=4] {'z','xs'}, dimensions={0} | all-to-all | bytes 262144 | tf_op jit(solution)/shard_map/all_to_all | solution.py:470
  90.6 2.0 %shard_map.96 = (f32[64,8,128]{2,1,0:T(8,128)S(1)}, f32[4,128]{1,0:T(4,128)S(1)}, f32[3,4,4]{2,1,0:T(4,128)}, f32[3,4,4]{2,1,0:T(4,128)}) custom-call(f32[32,8,128]{2,1,0:T(8,128)S(1)} %all_to_all.27.g_ref, f32[4,4]{1,0:T(4,128)S(1)} %copy-done.5, f32[8,128]{1,0:T(8,128)S(1)} %stack.2.refs_0_.refs_6_.k_ref, f32[8,72,128]{2,1,0:T(8,128)S(1)} %all_to_all.26.v_ref, ...), custom_call_target="tpu_custom_call" | custom-call | tf_op jit(solution)/shard_map/pallas_call | solution.py:45
  92.7 18.6 %all_to_all.28.r_ref = f32[64,8,128]{2,1,0:T(8,128)S(1)} all-to-all(f32[64,8,128]{2,1,0:T(8,128)S(1)} %get-tuple-element.25), channel_id=1, replica_groups=mesh['z'=8,'y'=4,'core'=2,'xs'=4] {'z','y','core'}, dimensions={0} | all-to-all | bytes 524288 | tf_op jit(solution)/shard_map/all_to_all | solution.py:476
  111.2 1.1 %shard_map.97 = f32[8,4,2048]{2,1,0:T(4,128)} custom-call(f32[64,8,128]{2,1,0:T(8,128)S(1)} %all_to_all.28.r_ref, f32[64,8,256]{2,1,0:T(8,128)S(1)} %copy-done.2, f32[4,128]{1,0:T(4,128)S(1)} %get-tuple-element.26.coef_ref), custom_call_target="tpu_custom_call" | custom-call | tf_op jit(solution)/shard_map/pallas_call | solution.py:45
  (42 shorter events, 3.8 us)
Async XLA Ops:
  2.5 30.9 %all-to-all-start = ((f32[64,8,256]{2,1,0:T(8,128)}), f32[64,8,256]{2,1,0:T(8,128)S(1)}, u32[]{:S(2)}, u32[]{:S(2)}) async-start(f32[64,8,256]{2,1,0:T(8,128)} %shard_map.86.q_ref), calls=%async_computation | async-start | bytes 1048576 | tf_op jit(solution)/shard_map/all_to_all | solution.py:421
  15.7 2.5 %copy-start = (f32[16,5,128,128]{3,2,1,0:T(8,128)S(1)}, f32[16,5,128,128]{3,2,1,0:T(8,128)}, u32[]{:S(2)}) copy-start(f32[16,5,128,128]{3,2,1,0:T(8,128)} %s_ref.1) | copy-start | bytes 15728644
  18.2 2.5 %copy-start.1 = (f32[16,5,128,128]{3,2,1,0:T(8,128)S(1)}, f32[16,5,128,128]{3,2,1,0:T(8,128)}, u32[]{:S(2)}) copy-start(f32[16,5,128,128]{3,2,1,0:T(8,128)} %c_ref.1) | copy-start | bytes 15728644
  20.7 3.2 %copy-start.6 = (s32[64]{0:T(128)S(1)}, s32[64]{0:T(128)}, u32[]{:S(2)}) copy-start(s32[64]{0:T(128)} %param.12) | copy-start | bytes 772
  20.7 8.5 %copy-start.5 = (f32[4,4]{1,0:T(4,128)S(1)}, f32[4,4]{1,0:T(4,128)}, u32[]{:S(2)}) copy-start(f32[4,4]{1,0:T(4,128)} %b_ref.3) | copy-start | bytes 196
  22.6 34.3 %copy-start.3 = (f32[8,4,2048]{2,1,0:T(4,128)S(1)}, f32[8,4,2048]{2,1,0:T(4,128)}, u32[]{:S(2)}) copy-start(f32[8,4,2048]{2,1,0:T(4,128)} %q_ref.1) | copy-start | bytes 786436
  22.6 34.2 %copy-start.4 = (f32[8,4,2048]{2,1,0:T(4,128)S(1)}, f32[8,4,2048]{2,1,0:T(4,128)}, u32[]{:S(2)}) copy-start(f32[8,4,2048]{2,1,0:T(4,128)} %p_ref.1) | copy-start | bytes 786436
  22.6 2.8 %collective-permute-start = (f32[8,128]{1,0:T(8,128)S(1)}, f32[8,128]{1,0:T(8,128)S(1)}, u32[]{:S(2)}, u32[]{:S(2)}) collective-permute-start(f32[8,128]{1,0:T(8,128)S(1)} %get-tuple-element.19), channel_id=1, source_target_pairs={{0,1},{1,0},{2,3},{3,2},{4,5},{5,4},{6,7},{7,6},{8,9},{9,8},{10,11... | collective-permute-start | bytes 12296 | tf_op jit(solution)/shard_map/ppermute | solution.py:412
  25.4 4.5 %collective-permute-start.1 = (f32[8,128]{1,0:T(8,128)S(1)}, f32[8,128]{1,0:T(8,128)S(1)}, u32[]{:S(2)}, u32[]{:S(2)}) collective-permute-start(f32[8,128]{1,0:T(8,128)S(1)} %max.6), channel_id=1, source_target_pairs={{0,2},{1,3},{2,0},{3,1},{4,6},{5,7},{6,4},{7,5},{8,10},{9,11},{10,... | collective-permute-start | bytes 12296 | tf_op jit(solution)/shard_map/ppermute | solution.py:412
  29.0 82.3 %copy-start.2 = (f32[64,8,256]{2,1,0:T(8,128)S(1)}, f32[64,8,256]{2,1,0:T(8,128)}, u32[]{:S(2)}) copy-start(f32[64,8,256]{2,1,0:T(8,128)} %shard_map.86.q_ref) | copy-start | bytes 1572868
  43.6 4.3 %collective-permute-start.2 = (f32[4,16,256]{2,1,0:T(8,128)S(1)}, f32[4,16,256]{2,1,0:T(8,128)S(1)}, u32[]{:S(2)}, u32[]{:S(2)}) collective-permute-start(f32[4,16,256]{2,1,0:T(8,128)S(1)} %slice.28), channel_id=1, source_target_pairs={{0,32},{32,64},{64,96},{96,128},{128,160},{160,192},{192,224},{224... | collective-permute-start | bytes 196616 | tf_op jit(solution)/shard_map/ppermute | solution.py:408
  43.9 4.0 %collective-permute-start.3 = (f32[4,16,256]{2,1,0:T(8,128)S(1)}, f32[4,16,256]{2,1,0:T(8,128)S(1)}, u32[]{:S(2)}, u32[]{:S(2)}) collective-permute-start(f32[4,16,256]{2,1,0:T(8,128)S(1)} %slice.28), channel_id=1, source_target_pairs={{32,0},{64,32},{96,64},{128,96},{160,128},{192,160},{224,192},{225... | collective-permute-start | bytes 196616 | tf_op jit(solution)/shard_map/ppermute | solution.py:408
  48.3 5.1 %collective-permute-start.4 = (f32[8,16,256]{2,1,0:T(8,128)S(1)}, f32[8,16,256]{2,1,0:T(8,128)S(1)}, u32[]{:S(2)}, u32[]{:S(2)}) collective-permute-start(f32[8,16,256]{2,1,0:T(8,128)S(1)} %shard_map.89.refs_1_.s1), channel_id=1, source_target_pairs={{0,32},{32,64},{64,96},{96,128},{128,160},{160,192},{192,224},{224... | collective-permute-start | bytes 393224 | tf_op jit(solution)/shard_map/ppermute | solution.py:408
  48.5 4.9 %collective-permute-start.5 = (f32[8,16,256]{2,1,0:T(8,128)S(1)}, f32[8,16,256]{2,1,0:T(8,128)S(1)}, u32[]{:S(2)}, u32[]{:S(2)}) collective-permute-start(f32[8,16,256]{2,1,0:T(8,128)S(1)} %shard_map.89.refs_1_.s1), channel_id=1, source_target_pairs={{32,0},{64,32},{96,64},{128,96},{160,128},{192,160},{224,192},{225... | collective-permute-start | bytes 393224 | tf_op jit(solution)/shard_map/ppermute | solution.py:408
  53.9 4.9 %collective-permute-start.6 = (f32[4,16,256]{2,1,0:T(8,128)S(1)}, f32[4,16,256]{2,1,0:T(8,128)S(1)}, u32[]{:S(2)}, u32[]{:S(2)}) collective-permute-start(f32[4,16,256]{2,1,0:T(8,128)S(1)} %get-tuple-element.23.refs_1_.k2w), channel_id=1, source_target_pairs={{0,32},{32,64},{64,96},{96,128},{128,160},{160,192},{192,224},{224... | collective-permute-start | bytes 196616 | tf_op jit(solution)/shard_map/ppermute | solution.py:408
  55.7 3.1 %collective-permute-start.7 = (f32[4,16,256]{2,1,0:T(8,128)S(1)}, f32[4,16,256]{2,1,0:T(8,128)S(1)}, u32[]{:S(2)}, u32[]{:S(2)}) collective-permute-start(f32[4,16,256]{2,1,0:T(8,128)S(1)} %get-tuple-element.23.refs_1_.k2w), channel_id=1, source_target_pairs={{32,0},{64,32},{96,64},{128,96},{160,128},{192,160},{224,192},{225... | collective-permute-start | bytes 196616 | tf_op jit(solution)/shard_map/ppermute | solution.py:408

commit v6 on v5

--- a/solution.py
+++ b/solution.py
@@ -119,7 +119,7 @@
     gram_ref[:, 0:8] = total
 
 
-def rest_kernel(k0_ref, raw_ref, b_ref, k_ref, out_ref):
+def rest_kernel(k0_ref, raw_ref, b_ref, out_ref):
     inside = jnp.zeros((8, 8), jnp.float32)
     for r in range(16):
         rows = k0_ref[:, r, :]
@@ -131,7 +131,7 @@
     change = jnp.concatenate(
         [
             jnp.concatenate([(row == col).astype(jnp.float32), none], axis=1),
-            jnp.concatenate([none, -k_ref[1:2, 0:1] * b_ref[...]], axis=1),
+            jnp.concatenate([none, -b_ref[...]], axis=1),
         ],
         axis=0,
     )
@@ -180,11 +180,46 @@
                 low_ref[half, k * 128 : k * 128 + 128] = low
 
 
-def table_kernel(f_ref, rows_ref, turned_ref):
-    high, low = split(f_ref[...])
-    rows_ref[0:128], rows_ref[128:256] = high, low
-    high, low = split(f_ref[...].T)
-    turned_ref[:, 0:128], turned_ref[:, 128:256] = high, low
+def circle(k):
+    near = ((k + 64) & 127) - 64
+    quarter = ((k + 64) >> 7) & 3
+    t = near.astype(jnp.float32) * (2.0 * math.pi / SECTORS)
+    u = t * t
+    cosine = 1.0 + u * (-1 / 2 + u * (1 / 24 + u * (-1 / 720 + u * (1 / 40320 - u * (1 / 3628800)))))
+    sine = t * (1.0 + u * (-1 / 6 + u * (1 / 120 + u * (-1 / 5040 + u * (1 / 362880)))))
+    value = jnp.where((quarter & 1) == 1, sine, cosine)
+    return jnp.where((quarter == 1) | (quarter == 2), -value, value)
+
+
+def table_kernel(h_ref, rows_ref, turned_ref, factor_ref, mean_ref, all_ref):
+    harmonic = h_ref[...]
+    parity = lax.broadcasted_iota(jnp.int32, (128, 128), 0) & 1
+    weight = jnp.where(harmonic == 0, math.sqrt(1.0 / SECTORS), math.sqrt(2.0 / SECTORS))
+    for part in range(4):
+        sector = lax.broadcasted_iota(jnp.int32, (128, 128), 1) + 128 * part
+        value = circle((harmonic * sector + 128 * parity) & 511) * weight
+        here = slice(part * 128, part * 128 + 128)
+        rows_ref[0:128, here], rows_ref[128:256, here] = split(value)
+        turned_ref[here, 0:128], turned_ref[here, 128:256] = split(value.T)
+    factors = circle(harmonic)
+    all_ref[...] = factors
+    group = lax.axis_index("y") * 2 + lax.axis_index("core")
+    factor_ref[...] = all_ref[pl.ds(pl.multiple_of(group * 16, 16), 16), :]
+    mean_ref[...] = jnp.sum(factors, axis=0, keepdims=True) * (1.0 / 128.0) + jnp.zeros((8, 128), jnp.float32)
+
+
+def table(assign):
+    vmem = pl.BlockSpec(memory_space=pltpu.VMEM)
+    harmonic = jnp.broadcast_to(jnp.repeat(assign, 2)[:, None], (128, 128))
+    return pl.pallas_call(
+        table_kernel,
+        out_shape=(bf16(256, 512), bf16(512, 256), f32(16, 128), f32(8, 128)),
+        in_specs=[vmem],
+        out_specs=(vmem,) * 4,
+        scratch_shapes=[pltpu.VMEM((128, 128), jnp.float32)],
+        cost_estimate=pl.CostEstimate(flops=0, bytes_accessed=0, transcendentals=0),
+        compiler_params=pltpu.CompilerParams(vmem_limit_bytes=VMEM_LIMIT),
+    )(harmonic)
 
 
 def forward_kernel(f_ref, r_ref, *refs):
@@ -194,7 +229,7 @@
     out_ref[...] = (both[:128] + both[128:] + fast(f_ref[0:128], low)).reshape(8, 16, 256)
 
 
-def apply_kernel(stage, left_ref, own_ref, right_ref, high_ref, low_ref, f_ref, k_ref, *refs):
+def apply_kernel(stage, left_ref, own_ref, right_ref, high_ref, low_ref, f_ref, *refs):
     count = left_ref.shape[0]
     rows = count * 16
     wide = jnp.concatenate(
@@ -203,7 +238,9 @@
     high, low = split(wide)
     stacked = jnp.concatenate([high, low], axis=0)
     factor = f_ref[...][None]
-    sigma, inverse = k_ref[0:1, :][None], k_ref[1:2, :][None]
+    if stage > 1:
+        k_ref, refs = refs[0], refs[1:]
+        sigma, inverse = k_ref[0:1, :][None], k_ref[1:2, :][None]
     for half in range(2):
         lanes = slice(half * 128, half * 128 + 640)
         both = fast(stacked[:, lanes], high_ref[half])
@@ -213,13 +250,12 @@
         here = slice(half * 128, half * 128 + 128)
         if stage == 1:
             b_ref, out_ref = refs
-            value = value * inverse
             out_ref[0:4, :, here] = value
             for i in range(4):
                 taken = b_ref[4 * i : 4 * i + 1] * own_ref[4, :, here]
                 for l in range(1, 4):
                     taken += b_ref[4 * i + l : 4 * i + l + 1] * own_ref[4 + l, :, here]
-                out_ref[4 + i, :, here] = value[i] - inverse[0] * taken
+                out_ref[4 + i, :, here] = value[i] - taken
         elif stage == 2:
             x_ref, w_ref = refs
             x_ref[:, :, here] = (value[0:4] - sigma * own_ref[0:4, :, here]) * inverse
@@ -306,10 +342,10 @@
     one_row = lax.broadcasted_iota(jnp.int32, (4, 1), 0)
     for step in range(3):
         if step == 0:
-            w = scale * (lane == row + 4).astype(jnp.float32)
-            w_g = scale * gram[4:8]
+            w = (lane == row + 4).astype(jnp.float32)
+            w_g = gram[4:8]
         else:
-            moved = scale * pltpu.roll(jnp.where(lane < 16, cur, 0.0), 8, 1)
+            moved = pltpu.roll(jnp.where(lane < 4, cur, jnp.where(lane < 16, scale * cur, 0.0)), 8, 1)
             moved += sigma * jnp.where(lane >= 8, cur, 0.0)
             w = moved - mixed(coupling, prev)
             w_g = dot(moved[:, 0:24], gram) - mixed(coupling, prev_g)
@@ -338,7 +374,7 @@
     behind = cur[:, 4:5] * b_ref[0:1, :]
     for l in range(1, 4):
         behind += cur[:, 4 + l : 5 + l] * b_ref[l : l + 1, :]
-    coef_ref[:, 4:8] = -k_ref[1:2, 0:1] * behind
+    coef_ref[:, 4:8] = -behind
     cur += pltpu.roll(jnp.where((lane >= 4) & (lane < 8), cur, 0.0), 4, 1)
     group = lane[0:1] // 32
     own = lane // 32 == row
@@ -387,16 +423,6 @@
                 out_ref[:, c, pl.ds(pair * 256 + half * 128, 128)] = value
 
 
-def table(assign):
-    harmonic = jnp.repeat(assign, 2)
-    parity = jnp.arange(harmonic.shape[0], dtype=jnp.int32) % 2
-    sectors = jnp.arange(SECTORS, dtype=jnp.int32)
-    phases = (harmonic[:, None] * sectors[None, :] + 128 * parity[:, None]) % SECTORS
-    weights = jnp.where(harmonic == 0, math.sqrt(1.0 / SECTORS), math.sqrt(2.0 / SECTORS))
-    weights = jnp.where((harmonic == 0) & (parity == 1), 0.0, weights).astype(jnp.float32)
-    return jnp.cos(2.0 * math.pi / SECTORS * phases.astype(jnp.float32)) * weights[:, None]
-
-
 def ring_place(pair):
     slab, at = pair // 8 % 4, pair % 8
     return (at if slab % 2 == 0 else 7 - at) * 4 + slab
@@ -408,26 +434,23 @@
     return lax.ppermute(value, RING, after), lax.ppermute(value, RING, before)
 
 
-def highest(value, step):
-    return jnp.maximum(value, lax.ppermute(value, "xs", [(i, i ^ step) for i in range(4)]))
+def highest(value):
+    others = [lax.ppermute(value, "xs", [(i, (i + k) % 4) for i in range(4)]) for k in (1, 2, 3)]
+    return jnp.maximum(jnp.maximum(value, others[0]), jnp.maximum(others[1], others[2]))
 
 
 def per_device(q_block, q_prev, b_prev, stiff_blocks, couple_blocks, block_cols, assign):
-    group = lax.axis_index("y") * 2 + lax.axis_index("core")
-
     pair = turned(lax.axis_index("z"), odd_slab()).astype(jnp.int32).reshape(1)
     packed = pack(q_block, q_prev)
     packed, pair = lax.optimization_barrier((packed, pair))
     received = lax.all_to_all(packed, SEC, 0, 0, tiled=True)
 
-    forward, inverse = call(table_kernel, (bf16(256, 512), bf16(512, 256)), table(assign))
-    factors = jnp.cos(2.0 * math.pi / SECTORS * assign.astype(jnp.float32))
-    mine = lax.dynamic_slice_in_dim(factors, group * 8, 8)
-    factor = jnp.broadcast_to(jnp.repeat(mine, 2)[:, None], (16, 128))
+    forward, inverse, factor, mean = table(assign)
     raw = call(raw_kernel, f32(8, 128), q_block, q_prev)
     found, own_high, own_low = pl.pallas_call(
         stats_kernel,
         out_shape=(f32(8, 128), bf16(2, 640, 256), bf16(2, 640, 256)),
+        cost_estimate=pl.CostEstimate(flops=0, bytes_accessed=0, transcendentals=0),
         grid_spec=pltpu.PrefetchScalarGridSpec(
             num_scalar_prefetch=1,
             grid=(16,),
@@ -441,8 +464,8 @@
         ),
         compiler_params=pltpu.CompilerParams(vmem_limit_bytes=VMEM_LIMIT),
     )(pair, stiff_blocks, couple_blocks)
-    found = highest(highest(found, 1), 2)
-    sigma = 0.5 * (found[1] - found[2]) + jnp.mean(factors) * (0.5 * (found[4] - found[5]))
+    found = highest(found)
+    sigma = 0.5 * (found[1] - found[2]) + mean[0] * (0.5 * (found[4] - found[5]))
     scale = found[0] + found[3]
     scale = jnp.where(scale > 0, scale, 1.0)
     scales = jnp.stack([sigma, 1.0 / scale, scale] + [scale] * 5)
@@ -457,13 +480,13 @@
         left, right = beside(sent)
         return call(
             lambda *refs: apply_kernel(stage, *refs),
-            out, left, value, right, own_high, own_low, factor, scales, *more,
+            out, left, value, right, own_high, own_low, factor, *more,
         )
 
     s1 = operator(1, k0[0:4], k0, f32(8, 16, 256), b_rows)
-    rest = call(rest_kernel, f32(8, 128), k0, raw, b_prev, scales)
-    k2x, k2w = operator(2, s1, s1, (f32(4, 16, 256), f32(4, 16, 256)))
-    k3 = operator(3, k2w, k2w, f32(4, 16, 256))
+    rest = call(rest_kernel, f32(8, 128), k0, raw, b_prev)
+    k2x, k2w = operator(2, s1, s1, (f32(4, 16, 256), f32(4, 16, 256)), scales)
+    k3 = operator(3, k2w, k2w, f32(4, 16, 256), scales)
 
     shares = call(share_kernel, f32(8, 72, 128), k0, s1, k2x, k2w, k3, rest)
     vectors = lax.all_to_all(shares, GROUP, 0, 0, tiled=True)

time: 113 us -> 112 us (level)
  other arithmetic: 1.74 us -> 0.02 us
  waiting for transfers between devices: 7.56 us -> 8.88 us
    ppermute x2 -> x3, starting transfers between devices: 4.03 us -> 4.89 us  [highest(): lax.ppermute(value, 'xs', [(i, (i + k) % 4) for i in range(4)])]
    pallas_call x11 -> x10, Pallas kernels: 7.36 us -> 7.23 us  [call(): pl.pallas_call(kernel, out_shape=out, in_specs=[whole] * len(args), out_s...]
  transfers between devices with their start and end apart: 9 -> 10, of which waited for: 4 -> 4; matrix products, arithmetic and copies ran while one was open for 2% -> 0% of each run, Pallas kernels for 4% -> 4%
where the time goes in v6:
time: 112 us
  blocking collectives  58.6 us (52%)
  starting transfers between devices  26.5 us (24%)
  Pallas kernels  11.5 us (10%)
  waiting for transfers between devices  8.88 us (8%)
  local copies, waits for them, and re-layouts  5.46 us (5%)
    all_to_all x1, blocking collectives, per_device(): back = lax.all_to_all(image, SEC, 0, 0, tiled=True)  18.6 us
    all_to_all x1, blocking collectives, per_device(): lax.all_to_all(call(total_kernel, f32(32, 8, 128), vectors), RING, 0, 0,...  16.7 us
    all_to_all x1, blocking collectives, per_device(): vectors = lax.all_to_all(shares, GROUP, 0, 0, tiled=True)  13.6 us
    all_to_all x1, starting transfers between devices, per_device(): received = lax.all_to_all(packed, SEC, 0, 0, tiled=True)  13.2 us
    all_to_all x1, blocking collectives, per_device(): k0 = lax.all_to_all(spectrum, GROUP, 0, 0, tiled=True)  9.73 us
    ppermute x6, starting transfers between devices, beside(): return (lax.ppermute(value, RING, after), lax.ppermute(value, RING, before))  8.44 us
    pallas_call x10, Pallas kernels, call(): pl.pallas_call(kernel, out_shape=out, in_specs=[whole] * len(args), out_s...  7.23 us
    unnamed x14, local copies, waits for them, and re-layouts  4.99 us
  transfers between devices with their start and end apart: 10, of which 4 were waited for; matrix products, arithmetic and copies ran while one was open for 0% of the time, Pallas kernels for 4%

profile of v6, /device:TPU:1, one launch (start us, length us, event | category | flops | bytes accessed | tf_op | source)
XLA Modules:
  0.0 111.7 jit_solution(18252093822117874186)
XLA Ops:
  0.6 1.9 %shard_map.86.q_ref = f32[64,8,256]{2,1,0:T(8,128)} custom-call(f32[8,4,2048]{2,1,0:T(4,128)} %q_ref.1, f32[8,4,2048]{2,1,0:T(4,128)} %p_ref.1), custom_call_target="tpu_custom_call" | custom-call | tf_op jit(solution)/shard_map/pallas_call | solution.py:97
  2.5 13.2 %all-to-all-start = ((f32[64,8,256]{2,1,0:T(8,128)}), f32[64,8,256]{2,1,0:T(8,128)S(1)}, u32[]{:S(2)}, u32[]{:S(2)}) async-start(f32[64,8,256]{2,1,0:T(8,128)} %shard_map.86.q_ref), calls=%async_computation | async-start | bytes 1048576 | tf_op jit(solution)/shard_map/all_to_all | solution.py:446
  15.7 2.5 %copy-done = f32[16,5,128,128]{3,2,1,0:T(8,128)S(1)} copy-done((f32[16,5,128,128]{3,2,1,0:T(8,128)S(1)}, f32[16,5,128,128]{3,2,1,0:T(8,128)}, u32[]{:S(2)}) %copy-start) | copy-done | bytes 5242904
  18.2 2.5 %copy-done.1 = f32[16,5,128,128]{3,2,1,0:T(8,128)S(1)} copy-done((f32[16,5,128,128]{3,2,1,0:T(8,128)S(1)}, f32[16,5,128,128]{3,2,1,0:T(8,128)}, u32[]{:S(2)}) %copy-start.1) | copy-done | bytes 5242904
  20.7 1.9 %shard_map.87 = (f32[8,128]{1,0:T(8,128)S(1)}, bf16[2,640,256]{2,1,0:T(8,128)(2,1)S(1)}, bf16[2,640,256]{2,1,0:T(8,128)(2,1)S(1)}) custom-call(s32[1]{0:T(128)} %bitcast.pair_ref, f32[16,5,128,128]{3,2,1,0:T(8,128)S(1)} %copy-done, f32[16,5,128,128]{3,2,1,0:T(8,128)S(1)} %copy-done.1), custom_call_target="tpu_custom_call" | custom-call | tf_op jit(solution)/shard_map/pallas_call | solution.py:450
  22.6 1.3 %collective-permute-start = (f32[8,128]{1,0:T(8,128)S(1)}, f32[8,128]{1,0:T(8,128)S(1)}, u32[]{:S(2)}, u32[]{:S(2)}) collective-permute-start(f32[8,128]{1,0:T(8,128)S(1)} %get-tuple-element.21), channel_id=1, source_target_pairs={{0,1},{1,2},{2,3},{3,0},{4,5},{5,6},{6,7},{7,4},{8,9},{9,10},{10,1... | collective-permute-start | bytes 12296 | tf_op jit(solution)/shard_map/ppermute | solution.py:438
  23.9 2.5 %collective-permute-start.1 = (f32[8,128]{1,0:T(8,128)S(1)}, f32[8,128]{1,0:T(8,128)S(1)}, u32[]{:S(2)}, u32[]{:S(2)}) collective-permute-start(f32[8,128]{1,0:T(8,128)S(1)} %get-tuple-element.21), channel_id=1, source_target_pairs={{0,2},{1,3},{2,0},{3,1},{4,6},{5,7},{6,4},{7,5},{8,10},{9,11},{10,... | collective-permute-start | bytes 12296 | tf_op jit(solution)/shard_map/ppermute | solution.py:438
  26.3 1.2 %collective-permute-start.2 = (f32[8,128]{1,0:T(8,128)S(1)}, f32[8,128]{1,0:T(8,128)S(1)}, u32[]{:S(2)}, u32[]{:S(2)}) collective-permute-start(f32[8,128]{1,0:T(8,128)S(1)} %get-tuple-element.21), channel_id=1, source_target_pairs={{0,3},{1,0},{2,1},{3,2},{4,7},{5,4},{6,5},{7,6},{8,11},{9,8},{10,9... | collective-permute-start | bytes 12296 | tf_op jit(solution)/shard_map/ppermute | solution.py:438
  28.4 0.6 collective-permute-done.2
  29.1 4.3 %all-to-all-done.r_ref = f32[64,8,256]{2,1,0:T(8,128)S(1)} async-done(((f32[64,8,256]{2,1,0:T(8,128)}), f32[64,8,256]{2,1,0:T(8,128)S(1)}, u32[]{:S(2)}, u32[]{:S(2)}) %all-to-all-start) | async-done | bytes 524320 | tf_op jit(solution)/shard_map/all_to_all | solution.py:446
  33.8 9.7 %all_to_all.25.refs_1_.k0_ref.k0 = f32[8,16,256]{2,1,0:T(8,128)S(1)} all-to-all(f32[8,16,256]{2,1,0:T(8,128)S(1)} %shard_map.88), channel_id=1, replica_groups=mesh['z'=8,'y'=4,'core'=2,'xs'=4] {'y','core'}, dimensions={0} | all-to-all | bytes 262144 | tf_op jit(solution)/shard_map/all_to_all | solution.py:477
  43.9 2.3 %collective-permute-start.4 = (f32[4,16,256]{2,1,0:T(8,128)S(1)}, f32[4,16,256]{2,1,0:T(8,128)S(1)}, u32[]{:S(2)}, u32[]{:S(2)}) collective-permute-start(f32[4,16,256]{2,1,0:T(8,128)S(1)} %slice.32), channel_id=1, source_target_pairs={{32,0},{64,32},{96,64},{128,96},{160,128},{192,160},{224,192},{225... | collective-permute-start | bytes 196616 | tf_op jit(solution)/shard_map/ppermute | solution.py:434
  46.2 1.6 %collective-permute-done.3.refs_0_ = f32[4,16,256]{2,1,0:T(8,128)S(1)} collective-permute-done((f32[4,16,256]{2,1,0:T(8,128)S(1)}, f32[4,16,256]{2,1,0:T(8,128)S(1)}, u32[]{:S(2)}, u32[]{:S(2)}) %collective-permute-start.3) | collective-permute-done | bytes 65568 | tf_op jit(solution)/shard_map/ppermute | solution.py:434
  48.4 2.6 %collective-permute-start.6 = (f32[8,16,256]{2,1,0:T(8,128)S(1)}, f32[8,16,256]{2,1,0:T(8,128)S(1)}, u32[]{:S(2)}, u32[]{:S(2)}) collective-permute-start(f32[8,16,256]{2,1,0:T(8,128)S(1)} %shard_map.89.refs_1_.s1), channel_id=1, source_target_pairs={{32,0},{64,32},{96,64},{128,96},{160,128},{192,160},{224,192},{225... | collective-permute-start | bytes 393224 | tf_op jit(solution)/shard_map/ppermute | solution.py:434
  51.1 2.3 %collective-permute-done.5.refs_0_ = f32[8,16,256]{2,1,0:T(8,128)S(1)} collective-permute-done((f32[8,16,256]{2,1,0:T(8,128)S(1)}, f32[8,16,256]{2,1,0:T(8,128)S(1)}, u32[]{:S(2)}, u32[]{:S(2)}) %collective-permute-start.5) | collective-permute-done | bytes 131104 | tf_op jit(solution)/shard_map/ppermute | solution.py:434
  53.8 1.0 collective-permute-start.7
  54.8 1.9 %collective-permute-start.8 = (f32[4,16,256]{2,1,0:T(8,128)S(1)}, f32[4,16,256]{2,1,0:T(8,128)S(1)}, u32[]{:S(2)}, u32[]{:S(2)}) collective-permute-start(f32[4,16,256]{2,1,0:T(8,128)S(1)} %get-tuple-element.27.refs_1_.k2w), channel_id=1, source_target_pairs={{32,0},{64,32},{96,64},{128,96},{160,128},{192,160},{224,192},{225... | collective-permute-start | bytes 196616 | tf_op jit(solution)/shard_map/ppermute | solution.py:434
  56.7 1.2 %shard_map.92.raw_ref = f32[8,128]{1,0:T(8,128)S(1)} custom-call(f32[8,4,2048]{2,1,0:T(4,128)S(1)} %copy-done.3, f32[8,4,2048]{2,1,0:T(4,128)S(1)} %copy-done.4), custom_call_target="tpu_custom_call" | custom-call | tf_op jit(solution)/shard_map/pallas_call | solution.py:45
  58.0 0.7 shard_map.93.rest_ref
  59.7 13.6 %all_to_all.26.v_ref = f32[8,72,128]{2,1,0:T(8,128)S(1)} all-to-all(f32[8,72,128]{2,1,0:T(8,128)S(1)} %shard_map.94), channel_id=1, replica_groups=mesh['z'=8,'y'=4,'core'=2,'xs'=4] {'y','core'}, dimensions={0} | all-to-all | bytes 589824 | tf_op jit(solution)/shard_map/all_to_all | solution.py:492
  73.2 16.7 %all_to_all.27.g_ref = f32[32,8,128]{2,1,0:T(8,128)S(1)} all-to-all(f32[32,8,128]{2,1,0:T(8,128)S(1)} %shard_map.95), channel_id=1, replica_groups=mesh['z'=8,'y'=4,'core'=2,'xs'=4] {'z','xs'}, dimensions={0} | all-to-all | bytes 262144 | tf_op jit(solution)/shard_map/all_to_all | solution.py:493
  90.0 2.0 %shard_map.96 = (f32[64,8,128]{2,1,0:T(8,128)S(1)}, f32[4,128]{1,0:T(4,128)S(1)}, f32[3,4,4]{2,1,0:T(4,128)}, f32[3,4,4]{2,1,0:T(4,128)}) custom-call(f32[32,8,128]{2,1,0:T(8,128)S(1)} %all_to_all.27.g_ref, f32[4,4]{1,0:T(4,128)S(1)} %copy-done.5, f32[8,128]{1,0:T(8,128)S(1)} %stack.2.refs_0_.refs_6_.k_ref, f32[8,72,128]{2,1,0:T(8,128)S(1)} %all_to_all.26.v_ref, ...), custom_call_target="tpu_custom_call" | custom-call | tf_op jit(solution)/shard_map/pallas_call | solution.py:45
  92.0 18.6 %all_to_all.28.r_ref = f32[64,8,128]{2,1,0:T(8,128)S(1)} all-to-all(f32[64,8,128]{2,1,0:T(8,128)S(1)} %get-tuple-element.29), channel_id=1, replica_groups=mesh['z'=8,'y'=4,'core'=2,'xs'=4] {'z','y','core'}, dimensions={0} | all-to-all | bytes 524288 | tf_op jit(solution)/shard_map/all_to_all | solution.py:499
  110.6 1.1 %shard_map.97 = f32[8,4,2048]{2,1,0:T(4,128)} custom-call(f32[64,8,128]{2,1,0:T(8,128)S(1)} %all_to_all.28.r_ref, f32[64,8,256]{2,1,0:T(8,128)S(1)} %copy-done.2, f32[4,128]{1,0:T(4,128)S(1)} %get-tuple-element.30.coef_ref), custom_call_target="tpu_custom_call" | custom-call | tf_op jit(solution)/shard_map/pallas_call | solution.py:45
  (36 shorter events, 3.7 us)
Async XLA Ops:
  2.5 30.9 %all-to-all-start = ((f32[64,8,256]{2,1,0:T(8,128)}), f32[64,8,256]{2,1,0:T(8,128)S(1)}, u32[]{:S(2)}, u32[]{:S(2)}) async-start(f32[64,8,256]{2,1,0:T(8,128)} %shard_map.86.q_ref), calls=%async_computation | async-start | bytes 1048576 | tf_op jit(solution)/shard_map/all_to_all | solution.py:446
  15.7 2.5 %copy-start = (f32[16,5,128,128]{3,2,1,0:T(8,128)S(1)}, f32[16,5,128,128]{3,2,1,0:T(8,128)}, u32[]{:S(2)}) copy-start(f32[16,5,128,128]{3,2,1,0:T(8,128)} %s_ref.1) | copy-start | bytes 15728644
  18.2 2.5 %copy-start.1 = (f32[16,5,128,128]{3,2,1,0:T(8,128)S(1)}, f32[16,5,128,128]{3,2,1,0:T(8,128)}, u32[]{:S(2)}) copy-start(f32[16,5,128,128]{3,2,1,0:T(8,128)} %c_ref.1) | copy-start | bytes 15728644
  20.7 6.8 %copy-start.6 = (s32[64]{0:T(128)S(1)}, s32[64]{0:T(128)}, u32[]{:S(2)}) copy-start(s32[64]{0:T(128)} %param.12) | copy-start | bytes 772
  20.7 7.6 %copy-start.5 = (f32[4,4]{1,0:T(4,128)S(1)}, f32[4,4]{1,0:T(4,128)}, u32[]{:S(2)}) copy-start(f32[4,4]{1,0:T(4,128)} %b_ref.3) | copy-start | bytes 196
  20.7 36.0 %copy-start.3 = (f32[8,4,2048]{2,1,0:T(4,128)S(1)}, f32[8,4,2048]{2,1,0:T(4,128)}, u32[]{:S(2)}) copy-start(f32[8,4,2048]{2,1,0:T(4,128)} %q_ref.1) | copy-start | bytes 786436
  20.7 36.0 %copy-start.4 = (f32[8,4,2048]{2,1,0:T(4,128)S(1)}, f32[8,4,2048]{2,1,0:T(4,128)}, u32[]{:S(2)}) copy-start(f32[8,4,2048]{2,1,0:T(4,128)} %p_ref.1) | copy-start | bytes 786436
  22.6 5.8 %collective-permute-start = (f32[8,128]{1,0:T(8,128)S(1)}, f32[8,128]{1,0:T(8,128)S(1)}, u32[]{:S(2)}, u32[]{:S(2)}) collective-permute-start(f32[8,128]{1,0:T(8,128)S(1)} %get-tuple-element.21), channel_id=1, source_target_pairs={{0,1},{1,2},{2,3},{3,0},{4,5},{5,6},{6,7},{7,4},{8,9},{9,10},{10,1... | collective-permute-start | bytes 12296 | tf_op jit(solution)/shard_map/ppermute | solution.py:438
  23.9 4.6 %collective-permute-start.1 = (f32[8,128]{1,0:T(8,128)S(1)}, f32[8,128]{1,0:T(8,128)S(1)}, u32[]{:S(2)}, u32[]{:S(2)}) collective-permute-start(f32[8,128]{1,0:T(8,128)S(1)} %get-tuple-element.21), channel_id=1, source_target_pairs={{0,2},{1,3},{2,0},{3,1},{4,6},{5,7},{6,4},{7,5},{8,10},{9,11},{10,... | collective-permute-start | bytes 12296 | tf_op jit(solution)/shard_map/ppermute | solution.py:438
  26.3 2.8 %collective-permute-start.2 = (f32[8,128]{1,0:T(8,128)S(1)}, f32[8,128]{1,0:T(8,128)S(1)}, u32[]{:S(2)}, u32[]{:S(2)}) collective-permute-start(f32[8,128]{1,0:T(8,128)S(1)} %get-tuple-element.21), channel_id=1, source_target_pairs={{0,3},{1,0},{2,1},{3,2},{4,7},{5,4},{6,5},{7,6},{8,11},{9,8},{10,9... | collective-permute-start | bytes 12296 | tf_op jit(solution)/shard_map/ppermute | solution.py:438
  27.7 82.9 %copy-start.2 = (f32[64,8,256]{2,1,0:T(8,128)S(1)}, f32[64,8,256]{2,1,0:T(8,128)}, u32[]{:S(2)}) copy-start(f32[64,8,256]{2,1,0:T(8,128)} %shard_map.86.q_ref) | copy-start | bytes 1572868
  43.5 4.3 %collective-permute-start.3 = (f32[4,16,256]{2,1,0:T(8,128)S(1)}, f32[4,16,256]{2,1,0:T(8,128)S(1)}, u32[]{:S(2)}, u32[]{:S(2)}) collective-permute-start(f32[4,16,256]{2,1,0:T(8,128)S(1)} %slice.32), channel_id=1, source_target_pairs={{0,32},{32,64},{64,96},{96,128},{128,160},{160,192},{192,224},{224... | collective-permute-start | bytes 196616 | tf_op jit(solution)/shard_map/ppermute | solution.py:434
  43.9 4.0 %collective-permute-start.4 = (f32[4,16,256]{2,1,0:T(8,128)S(1)}, f32[4,16,256]{2,1,0:T(8,128)S(1)}, u32[]{:S(2)}, u32[]{:S(2)}) collective-permute-start(f32[4,16,256]{2,1,0:T(8,128)S(1)} %slice.32), channel_id=1, source_target_pairs={{32,0},{64,32},{96,64},{128,96},{160,128},{192,160},{224,192},{225... | collective-permute-start | bytes 196616 | tf_op jit(solution)/shard_map/ppermute | solution.py:434
  48.2 5.1 %collective-permute-start.5 = (f32[8,16,256]{2,1,0:T(8,128)S(1)}, f32[8,16,256]{2,1,0:T(8,128)S(1)}, u32[]{:S(2)}, u32[]{:S(2)}) collective-permute-start(f32[8,16,256]{2,1,0:T(8,128)S(1)} %shard_map.89.refs_1_.s1), channel_id=1, source_target_pairs={{0,32},{32,64},{64,96},{96,128},{128,160},{160,192},{192,224},{224... | collective-permute-start | bytes 393224 | tf_op jit(solution)/shard_map/ppermute | solution.py:434
  48.4 4.9 %collective-permute-start.6 = (f32[8,16,256]{2,1,0:T(8,128)S(1)}, f32[8,16,256]{2,1,0:T(8,128)S(1)}, u32[]{:S(2)}, u32[]{:S(2)}) collective-permute-start(f32[8,16,256]{2,1,0:T(8,128)S(1)} %shard_map.89.refs_1_.s1), channel_id=1, source_target_pairs={{32,0},{64,32},{96,64},{128,96},{160,128},{192,160},{224,192},{225... | collective-permute-start | bytes 393224 | tf_op jit(solution)/shard_map/ppermute | solution.py:434
  53.8 4.9 %collective-permute-start.7 = (f32[4,16,256]{2,1,0:T(8,128)S(1)}, f32[4,16,256]{2,1,0:T(8,128)S(1)}, u32[]{:S(2)}, u32[]{:S(2)}) collective-permute-start(f32[4,16,256]{2,1,0:T(8,128)S(1)} %get-tuple-element.27.refs_1_.k2w), channel_id=1, source_target_pairs={{0,32},{32,64},{64,96},{96,128},{128,160},{160,192},{192,224},{224... | collective-permute-start | bytes 196616 | tf_op jit(solution)/shard_map/ppermute | solution.py:434
  54.8 3.9 %collective-permute-start.8 = (f32[4,16,256]{2,1,0:T(8,128)S(1)}, f32[4,16,256]{2,1,0:T(8,128)S(1)}, u32[]{:S(2)}, u32[]{:S(2)}) collective-permute-start(f32[4,16,256]{2,1,0:T(8,128)S(1)} %get-tuple-element.27.refs_1_.k2w), channel_id=1, source_target_pairs={{32,0},{64,32},{96,64},{128,96},{160,128},{192,160},{224,192},{225... | collective-permute-start | bytes 196616 | tf_op jit(solution)/shard_map/ppermute | solution.py:434

commit v7 on v6

--- a/solution.py
+++ b/solution.py
@@ -321,7 +321,7 @@
     return value
 
 
-def solve_kernel(g_ref, b_ref, k_ref, v_ref, f_ref, image_ref, coef_ref, alpha_ref, beta_ref):
+def solve_kernel(g_ref, b_ref, k_ref, v_ref, f_ref, image_hbm, coef_ref, alpha_ref, beta_ref, image_ref, sem):
     lane = lax.broadcasted_iota(jnp.int32, (4, 128), 1)
     row = lax.broadcasted_iota(jnp.int32, (4, 128), 0)
     sigma, scale = k_ref[0:1, :], k_ref[2:3, :]
@@ -395,11 +395,20 @@
     right = jnp.concatenate(
         [jnp.concatenate([high, low], axis=1), jnp.concatenate([high, none], axis=1)], axis=0
     )
-    both = fast(f_ref[...], right)
-    image_ref[...] = (both[:, :128] + both[:, 128:]).reshape(64, 8, 128)
-
-
-def last_kernel(r_ref, q_ref, coef_ref, out_ref):
+    leaving = []
+    for part in range(4):
+        both = fast(f_ref[part * 128 : part * 128 + 128], right)
+        here = pl.ds(part * 16, 16)
+        image_ref[here] = (both[:, :128] + both[:, 128:]).reshape(16, 8, 128)
+        copy = pltpu.make_async_copy(image_ref.at[here], image_hbm.at[here], sem.at[part])
+        copy.start()
+        leaving.append(copy)
+    for copy in leaving:
+        copy.wait()
+
+
+def last_kernel(r_ref, q_ref, coef_ref, out_hbm, out_ref, sem):
+    leaving = []
     flip = odd_slab()
     group = lax.broadcasted_iota(jnp.int32, (8, 128), 1) // 32
     coef = coef_ref[...]
@@ -421,6 +430,12 @@
                 for k in range(8):
                     value += scalars[c][k] * q_ref[place + k, :, lanes]
                 out_ref[:, c, pl.ds(pair * 256 + half * 128, 128)] = value
+        here = pl.ds(pair * 256, 256)
+        copy = pltpu.make_async_copy(out_ref.at[:, :, here], out_hbm.at[:, :, here], sem.at[pair])
+        copy.start()
+        leaving.append(copy)
+    for copy in leaving:
+        copy.wait()
 
 
 def ring_place(pair):
@@ -491,13 +506,24 @@
     shares = call(share_kernel, f32(8, 72, 128), k0, s1, k2x, k2w, k3, rest)
     vectors = lax.all_to_all(shares, GROUP, 0, 0, tiled=True)
     grams = lax.all_to_all(call(total_kernel, f32(32, 8, 128), vectors), RING, 0, 0, tiled=True)
-    image, coef, alphas, betas = call(
+    vmem, hbm = (pl.BlockSpec(memory_space=space) for space in (pltpu.VMEM, pltpu.HBM))
+    image, coef, alphas, betas = pl.pallas_call(
         solve_kernel,
-        (f32(64, 8, 128), f32(4, 128), f32(3, 4, 4), f32(3, 4, 4)),
-        grams, b_prev, scales, vectors, inverse,
-    )
+        out_shape=(f32(64, 8, 128), f32(4, 128), f32(3, 4, 4), f32(3, 4, 4)),
+        in_specs=[vmem] * 5,
+        out_specs=(hbm, vmem, vmem, vmem),
+        scratch_shapes=[pltpu.VMEM((64, 8, 128), jnp.float32), pltpu.SemaphoreType.DMA((4,))],
+        compiler_params=pltpu.CompilerParams(vmem_limit_bytes=VMEM_LIMIT),
+    )(grams, b_prev, scales, vectors, inverse)
     back = lax.all_to_all(image, SEC, 0, 0, tiled=True)
-    out = call(last_kernel, f32(8, 4, 2048), back, packed, coef)
+    out = pl.pallas_call(
+        last_kernel,
+        out_shape=f32(8, 4, 2048),
+        in_specs=[vmem] * 3,
+        out_specs=hbm,
+        scratch_shapes=[pltpu.VMEM((8, 4, 2048), jnp.float32), pltpu.SemaphoreType.DMA((8,))],
+        compiler_params=pltpu.CompilerParams(vmem_limit_bytes=VMEM_LIMIT),
+    )(back, packed, coef)
     return out, alphas, betas
 
 

time: 112 us -> 113 us (level)
    pallas_call x0 -> x2, Pallas kernels: none -> 4.23 us  [the longest x1 3.11 us: per_device(): pl.pallas_call(solve_kernel, out_shape=(f32(64, 8, 128), f32(4, 128), f32...]
    pallas_call x10 -> x8, Pallas kernels: 7.23 us -> 4.03 us  [call(): pl.pallas_call(kernel, out_shape=out, in_specs=[whole] * len(args), out_s...]
where the time goes in v7:
time: 113 us
  blocking collectives  58.6 us (52%)
  starting transfers between devices  26.5 us (23%)
  Pallas kernels  12.6 us (11%)
  waiting for transfers between devices  8.88 us (8%)
  local copies, waits for them, and re-layouts  5.46 us (5%)
    all_to_all x1, blocking collectives, per_device(): back = lax.all_to_all(image, SEC, 0, 0, tiled=True)  18.6 us
    all_to_all x1, blocking collectives, per_device(): lax.all_to_all(call(total_kernel, f32(32, 8, 128), vectors), RING, 0, 0,...  16.7 us
    all_to_all x1, blocking collectives, per_device(): vectors = lax.all_to_all(shares, GROUP, 0, 0, tiled=True)  13.6 us
    all_to_all x1, starting transfers between devices, per_device(): received = lax.all_to_all(packed, SEC, 0, 0, tiled=True)  13.2 us
    all_to_all x1, blocking collectives, per_device(): k0 = lax.all_to_all(spectrum, GROUP, 0, 0, tiled=True)  9.72 us
    ppermute x6, starting transfers between devices, beside(): return (lax.ppermute(value, RING, after), lax.ppermute(value, RING, before))  8.44 us
    unnamed x14, local copies, waits for them, and re-layouts  4.99 us
    ppermute x3, starting transfers between devices, highest(): lax.ppermute(value, 'xs', [(i, (i + k) % 4) for i in range(4)])  4.89 us
  transfers between devices with their start and end apart: 10, of which 4 were waited for; matrix products, arithmetic and copies ran while one was open for 0% of the time, Pallas kernels for 4%

profile of v7, /device:TPU:1, one launch (start us, length us, event | category | flops | bytes accessed | tf_op | source)
XLA Modules:
  0.0 113.0 jit_solution(6401015809199543191)
XLA Ops:
  0.6 1.9 %shard_map.86.q_ref = f32[64,8,256]{2,1,0:T(8,128)} custom-call(f32[8,4,2048]{2,1,0:T(4,128)} %q_ref.1, f32[8,4,2048]{2,1,0:T(4,128)} %p_ref.1), custom_call_target="tpu_custom_call" | custom-call | tf_op jit(solution)/shard_map/pallas_call | solution.py:97
  2.5 13.2 %all-to-all-start = ((f32[64,8,256]{2,1,0:T(8,128)}), f32[64,8,256]{2,1,0:T(8,128)S(1)}, u32[]{:S(2)}, u32[]{:S(2)}) async-start(f32[64,8,256]{2,1,0:T(8,128)} %shard_map.86.q_ref), calls=%async_computation | async-start | bytes 1048576 | tf_op jit(solution)/shard_map/all_to_all | solution.py:461
  15.7 2.5 %copy-done = f32[16,5,128,128]{3,2,1,0:T(8,128)S(1)} copy-done((f32[16,5,128,128]{3,2,1,0:T(8,128)S(1)}, f32[16,5,128,128]{3,2,1,0:T(8,128)}, u32[]{:S(2)}) %copy-start) | copy-done | bytes 5242904
  18.2 2.5 %copy-done.1 = f32[16,5,128,128]{3,2,1,0:T(8,128)S(1)} copy-done((f32[16,5,128,128]{3,2,1,0:T(8,128)S(1)}, f32[16,5,128,128]{3,2,1,0:T(8,128)}, u32[]{:S(2)}) %copy-start.1) | copy-done | bytes 5242904
  20.7 1.9 %shard_map.87 = (f32[8,128]{1,0:T(8,128)S(1)}, bf16[2,640,256]{2,1,0:T(8,128)(2,1)S(1)}, bf16[2,640,256]{2,1,0:T(8,128)(2,1)S(1)}) custom-call(s32[1]{0:T(128)} %bitcast.pair_ref, f32[16,5,128,128]{3,2,1,0:T(8,128)S(1)} %copy-done, f32[16,5,128,128]{3,2,1,0:T(8,128)S(1)} %copy-done.1), custom_call_target="tpu_custom_call" | custom-call | tf_op jit(solution)/shard_map/pallas_call | solution.py:465
  22.6 1.3 %collective-permute-start = (f32[8,128]{1,0:T(8,128)S(1)}, f32[8,128]{1,0:T(8,128)S(1)}, u32[]{:S(2)}, u32[]{:S(2)}) collective-permute-start(f32[8,128]{1,0:T(8,128)S(1)} %get-tuple-element.21), channel_id=1, source_target_pairs={{0,1},{1,2},{2,3},{3,0},{4,5},{5,6},{6,7},{7,4},{8,9},{9,10},{10,1... | collective-permute-start | bytes 12296 | tf_op jit(solution)/shard_map/ppermute | solution.py:453
  23.9 2.5 %collective-permute-start.1 = (f32[8,128]{1,0:T(8,128)S(1)}, f32[8,128]{1,0:T(8,128)S(1)}, u32[]{:S(2)}, u32[]{:S(2)}) collective-permute-start(f32[8,128]{1,0:T(8,128)S(1)} %get-tuple-element.21), channel_id=1, source_target_pairs={{0,2},{1,3},{2,0},{3,1},{4,6},{5,7},{6,4},{7,5},{8,10},{9,11},{10,... | collective-permute-start | bytes 12296 | tf_op jit(solution)/shard_map/ppermute | solution.py:453
  26.3 1.2 %collective-permute-start.2 = (f32[8,128]{1,0:T(8,128)S(1)}, f32[8,128]{1,0:T(8,128)S(1)}, u32[]{:S(2)}, u32[]{:S(2)}) collective-permute-start(f32[8,128]{1,0:T(8,128)S(1)} %get-tuple-element.21), channel_id=1, source_target_pairs={{0,3},{1,0},{2,1},{3,2},{4,7},{5,4},{6,5},{7,6},{8,11},{9,8},{10,9... | collective-permute-start | bytes 12296 | tf_op jit(solution)/shard_map/ppermute | solution.py:453
  28.4 0.6 collective-permute-done.2
  29.1 4.3 %all-to-all-done.r_ref = f32[64,8,256]{2,1,0:T(8,128)S(1)} async-done(((f32[64,8,256]{2,1,0:T(8,128)}), f32[64,8,256]{2,1,0:T(8,128)S(1)}, u32[]{:S(2)}, u32[]{:S(2)}) %all-to-all-start) | async-done | bytes 524320 | tf_op jit(solution)/shard_map/all_to_all | solution.py:461
  33.8 9.7 %all_to_all.25.refs_1_.k0_ref.k0 = f32[8,16,256]{2,1,0:T(8,128)S(1)} all-to-all(f32[8,16,256]{2,1,0:T(8,128)S(1)} %shard_map.88), channel_id=1, replica_groups=mesh['z'=8,'y'=4,'core'=2,'xs'=4] {'y','core'}, dimensions={0} | all-to-all | bytes 262144 | tf_op jit(solution)/shard_map/all_to_all | solution.py:492
  43.9 2.3 %collective-permute-start.4 = (f32[4,16,256]{2,1,0:T(8,128)S(1)}, f32[4,16,256]{2,1,0:T(8,128)S(1)}, u32[]{:S(2)}, u32[]{:S(2)}) collective-permute-start(f32[4,16,256]{2,1,0:T(8,128)S(1)} %slice.32), channel_id=1, source_target_pairs={{32,0},{64,32},{96,64},{128,96},{160,128},{192,160},{224,192},{225... | collective-permute-start | bytes 196616 | tf_op jit(solution)/shard_map/ppermute | solution.py:449
  46.2 1.6 %collective-permute-done.3.refs_0_ = f32[4,16,256]{2,1,0:T(8,128)S(1)} collective-permute-done((f32[4,16,256]{2,1,0:T(8,128)S(1)}, f32[4,16,256]{2,1,0:T(8,128)S(1)}, u32[]{:S(2)}, u32[]{:S(2)}) %collective-permute-start.3) | collective-permute-done | bytes 65568 | tf_op jit(solution)/shard_map/ppermute | solution.py:449
  48.4 2.6 %collective-permute-start.6 = (f32[8,16,256]{2,1,0:T(8,128)S(1)}, f32[8,16,256]{2,1,0:T(8,128)S(1)}, u32[]{:S(2)}, u32[]{:S(2)}) collective-permute-start(f32[8,16,256]{2,1,0:T(8,128)S(1)} %shard_map.89.refs_1_.s1), channel_id=1, source_target_pairs={{32,0},{64,32},{96,64},{128,96},{160,128},{192,160},{224,192},{225... | collective-permute-start | bytes 393224 | tf_op jit(solution)/shard_map/ppermute | solution.py:449
  51.1 2.3 %collective-permute-done.5.refs_0_ = f32[8,16,256]{2,1,0:T(8,128)S(1)} collective-permute-done((f32[8,16,256]{2,1,0:T(8,128)S(1)}, f32[8,16,256]{2,1,0:T(8,128)S(1)}, u32[]{:S(2)}, u32[]{:S(2)}) %collective-permute-start.5) | collective-permute-done | bytes 131104 | tf_op jit(solution)/shard_map/ppermute | solution.py:449
  53.8 1.0 collective-permute-start.7
  54.8 1.9 %collective-permute-start.8 = (f32[4,16,256]{2,1,0:T(8,128)S(1)}, f32[4,16,256]{2,1,0:T(8,128)S(1)}, u32[]{:S(2)}, u32[]{:S(2)}) collective-permute-start(f32[4,16,256]{2,1,0:T(8,128)S(1)} %get-tuple-element.27.refs_1_.k2w), channel_id=1, source_target_pairs={{32,0},{64,32},{96,64},{128,96},{160,128},{192,160},{224,192},{225... | collective-permute-start | bytes 196616 | tf_op jit(solution)/shard_map/ppermute | solution.py:449
  56.7 1.2 %shard_map.92.raw_ref = f32[8,128]{1,0:T(8,128)S(1)} custom-call(f32[8,4,2048]{2,1,0:T(4,128)S(1)} %copy-done.3, f32[8,4,2048]{2,1,0:T(4,128)S(1)} %copy-done.4), custom_call_target="tpu_custom_call" | custom-call | tf_op jit(solution)/shard_map/pallas_call | solution.py:45
  58.0 0.7 shard_map.93.rest_ref
  59.7 13.6 %all_to_all.26.v_ref = f32[8,72,128]{2,1,0:T(8,128)S(1)} all-to-all(f32[8,72,128]{2,1,0:T(8,128)S(1)} %shard_map.94), channel_id=1, replica_groups=mesh['z'=8,'y'=4,'core'=2,'xs'=4] {'y','core'}, dimensions={0} | all-to-all | bytes 589824 | tf_op jit(solution)/shard_map/all_to_all | solution.py:507
  73.2 16.7 %all_to_all.27.g_ref = f32[32,8,128]{2,1,0:T(8,128)S(1)} all-to-all(f32[32,8,128]{2,1,0:T(8,128)S(1)} %shard_map.95), channel_id=1, replica_groups=mesh['z'=8,'y'=4,'core'=2,'xs'=4] {'z','xs'}, dimensions={0} | all-to-all | bytes 262144 | tf_op jit(solution)/shard_map/all_to_all | solution.py:508
  90.0 3.1 %shard_map.96 = (f32[64,8,128]{2,1,0:T(8,128)S(1)}, f32[4,128]{1,0:T(4,128)S(1)}, f32[3,4,4]{2,1,0:T(4,128)}, f32[3,4,4]{2,1,0:T(4,128)}) custom-call(f32[32,8,128]{2,1,0:T(8,128)S(1)} %all_to_all.27.g_ref, f32[4,4]{1,0:T(4,128)S(1)} %copy-done.5, f32[8,128]{1,0:T(8,128)S(1)} %stack.2.refs_0_.refs_6_.k_ref, f32[8,72,128]{2,1,0:T(8,128)S(1)} %all_to_all.26.v_ref, ...), custom_call_target="tpu_custom_call" | custom-call | tf_op jit(solution)/shard_map/pallas_call | solution.py:510
  93.1 18.6 %all_to_all.28.r_ref = f32[64,8,128]{2,1,0:T(8,128)S(1)} all-to-all(f32[64,8,128]{2,1,0:T(8,128)S(1)} %get-tuple-element.29), channel_id=1, replica_groups=mesh['z'=8,'y'=4,'core'=2,'xs'=4] {'z','y','core'}, dimensions={0} | all-to-all | bytes 524288 | tf_op jit(solution)/shard_map/all_to_all | solution.py:518
  111.7 1.1 shard_map.97
  (36 shorter events, 3.7 us)
Async XLA Ops:
  2.5 30.9 %all-to-all-start = ((f32[64,8,256]{2,1,0:T(8,128)}), f32[64,8,256]{2,1,0:T(8,128)S(1)}, u32[]{:S(2)}, u32[]{:S(2)}) async-start(f32[64,8,256]{2,1,0:T(8,128)} %shard_map.86.q_ref), calls=%async_computation | async-start | bytes 1048576 | tf_op jit(solution)/shard_map/all_to_all | solution.py:461
  15.7 2.5 %copy-start = (f32[16,5,128,128]{3,2,1,0:T(8,128)S(1)}, f32[16,5,128,128]{3,2,1,0:T(8,128)}, u32[]{:S(2)}) copy-start(f32[16,5,128,128]{3,2,1,0:T(8,128)} %s_ref.1) | copy-start | bytes 15728644
  18.2 2.5 %copy-start.1 = (f32[16,5,128,128]{3,2,1,0:T(8,128)S(1)}, f32[16,5,128,128]{3,2,1,0:T(8,128)}, u32[]{:S(2)}) copy-start(f32[16,5,128,128]{3,2,1,0:T(8,128)} %c_ref.1) | copy-start | bytes 15728644
  20.7 6.8 %copy-start.6 = (s32[64]{0:T(128)S(1)}, s32[64]{0:T(128)}, u32[]{:S(2)}) copy-start(s32[64]{0:T(128)} %param.12) | copy-start | bytes 772
  20.7 7.6 %copy-start.5 = (f32[4,4]{1,0:T(4,128)S(1)}, f32[4,4]{1,0:T(4,128)}, u32[]{:S(2)}) copy-start(f32[4,4]{1,0:T(4,128)} %b_ref.3) | copy-start | bytes 196
  20.7 36.0 %copy-start.3 = (f32[8,4,2048]{2,1,0:T(4,128)S(1)}, f32[8,4,2048]{2,1,0:T(4,128)}, u32[]{:S(2)}) copy-start(f32[8,4,2048]{2,1,0:T(4,128)} %q_ref.1) | copy-start | bytes 786436
  20.7 36.0 %copy-start.4 = (f32[8,4,2048]{2,1,0:T(4,128)S(1)}, f32[8,4,2048]{2,1,0:T(4,128)}, u32[]{:S(2)}) copy-start(f32[8,4,2048]{2,1,0:T(4,128)} %p_ref.1) | copy-start | bytes 786436
  22.6 5.8 %collective-permute-start = (f32[8,128]{1,0:T(8,128)S(1)}, f32[8,128]{1,0:T(8,128)S(1)}, u32[]{:S(2)}, u32[]{:S(2)}) collective-permute-start(f32[8,128]{1,0:T(8,128)S(1)} %get-tuple-element.21), channel_id=1, source_target_pairs={{0,1},{1,2},{2,3},{3,0},{4,5},{5,6},{6,7},{7,4},{8,9},{9,10},{10,1... | collective-permute-start | bytes 12296 | tf_op jit(solution)/shard_map/ppermute | solution.py:453
  23.9 4.6 %collective-permute-start.1 = (f32[8,128]{1,0:T(8,128)S(1)}, f32[8,128]{1,0:T(8,128)S(1)}, u32[]{:S(2)}, u32[]{:S(2)}) collective-permute-start(f32[8,128]{1,0:T(8,128)S(1)} %get-tuple-element.21), channel_id=1, source_target_pairs={{0,2},{1,3},{2,0},{3,1},{4,6},{5,7},{6,4},{7,5},{8,10},{9,11},{10,... | collective-permute-start | bytes 12296 | tf_op jit(solution)/shard_map/ppermute | solution.py:453
  26.3 2.8 %collective-permute-start.2 = (f32[8,128]{1,0:T(8,128)S(1)}, f32[8,128]{1,0:T(8,128)S(1)}, u32[]{:S(2)}, u32[]{:S(2)}) collective-permute-start(f32[8,128]{1,0:T(8,128)S(1)} %get-tuple-element.21), channel_id=1, source_target_pairs={{0,3},{1,0},{2,1},{3,2},{4,7},{5,4},{6,5},{7,6},{8,11},{9,8},{10,9... | collective-permute-start | bytes 12296 | tf_op jit(solution)/shard_map/ppermute | solution.py:453
  27.7 84.0 %copy-start.2 = (f32[64,8,256]{2,1,0:T(8,128)S(1)}, f32[64,8,256]{2,1,0:T(8,128)}, u32[]{:S(2)}) copy-start(f32[64,8,256]{2,1,0:T(8,128)} %shard_map.86.q_ref) | copy-start | bytes 1572868
  43.5 4.3 %collective-permute-start.3 = (f32[4,16,256]{2,1,0:T(8,128)S(1)}, f32[4,16,256]{2,1,0:T(8,128)S(1)}, u32[]{:S(2)}, u32[]{:S(2)}) collective-permute-start(f32[4,16,256]{2,1,0:T(8,128)S(1)} %slice.32), channel_id=1, source_target_pairs={{0,32},{32,64},{64,96},{96,128},{128,160},{160,192},{192,224},{224... | collective-permute-start | bytes 196616 | tf_op jit(solution)/shard_map/ppermute | solution.py:449
  43.9 4.0 %collective-permute-start.4 = (f32[4,16,256]{2,1,0:T(8,128)S(1)}, f32[4,16,256]{2,1,0:T(8,128)S(1)}, u32[]{:S(2)}, u32[]{:S(2)}) collective-permute-start(f32[4,16,256]{2,1,0:T(8,128)S(1)} %slice.32), channel_id=1, source_target_pairs={{32,0},{64,32},{96,64},{128,96},{160,128},{192,160},{224,192},{225... | collective-permute-start | bytes 196616 | tf_op jit(solution)/shard_map/ppermute | solution.py:449
  48.2 5.1 %collective-permute-start.5 = (f32[8,16,256]{2,1,0:T(8,128)S(1)}, f32[8,16,256]{2,1,0:T(8,128)S(1)}, u32[]{:S(2)}, u32[]{:S(2)}) collective-permute-start(f32[8,16,256]{2,1,0:T(8,128)S(1)} %shard_map.89.refs_1_.s1), channel_id=1, source_target_pairs={{0,32},{32,64},{64,96},{96,128},{128,160},{160,192},{192,224},{224... | collective-permute-start | bytes 393224 | tf_op jit(solution)/shard_map/ppermute | solution.py:449
  48.4 4.9 %collective-permute-start.6 = (f32[8,16,256]{2,1,0:T(8,128)S(1)}, f32[8,16,256]{2,1,0:T(8,128)S(1)}, u32[]{:S(2)}, u32[]{:S(2)}) collective-permute-start(f32[8,16,256]{2,1,0:T(8,128)S(1)} %shard_map.89.refs_1_.s1), channel_id=1, source_target_pairs={{32,0},{64,32},{96,64},{128,96},{160,128},{192,160},{224,192},{225... | collective-permute-start | bytes 393224 | tf_op jit(solution)/shard_map/ppermute | solution.py:449
  53.8 4.9 %collective-permute-start.7 = (f32[4,16,256]{2,1,0:T(8,128)S(1)}, f32[4,16,256]{2,1,0:T(8,128)S(1)}, u32[]{:S(2)}, u32[]{:S(2)}) collective-permute-start(f32[4,16,256]{2,1,0:T(8,128)S(1)} %get-tuple-element.27.refs_1_.k2w), channel_id=1, source_target_pairs={{0,32},{32,64},{64,96},{96,128},{128,160},{160,192},{192,224},{224... | collective-permute-start | bytes 196616 | tf_op jit(solution)/shard_map/ppermute | solution.py:449
  54.8 3.9 %collective-permute-start.8 = (f32[4,16,256]{2,1,0:T(8,128)S(1)}, f32[4,16,256]{2,1,0:T(8,128)S(1)}, u32[]{:S(2)}, u32[]{:S(2)}) collective-permute-start(f32[4,16,256]{2,1,0:T(8,128)S(1)} %get-tuple-element.27.refs_1_.k2w), channel_id=1, source_target_pairs={{32,0},{64,32},{96,64},{128,96},{160,128},{192,160},{224,192},{225... | collective-permute-start | bytes 196616 | tf_op jit(solution)/shard_map/ppermute | solution.py:449

commit v8 on v6

--- a/solution.py
+++ b/solution.py
@@ -431,7 +431,8 @@
 def beside(value):
     after = [(ring_place(i), ring_place(i + 1)) for i in range(32)]
     before = [(j, i) for i, j in after]
-    return lax.ppermute(value, RING, after), lax.ppermute(value, RING, before)
+    right = lax.ppermute(value, RING, before)
+    return lax.ppermute(value, RING, after), right
 
 
 def highest(value):

time: 112 us -> 112 us (level)
  no operation moved by 1% of the time
where the time goes in v8:
time: 112 us
  blocking collectives  58.6 us (52%)
  starting transfers between devices  26.5 us (24%)
  Pallas kernels  11.5 us (10%)
  waiting for transfers between devices  8.88 us (8%)
  local copies, waits for them, and re-layouts  5.46 us (5%)
    all_to_all x1, blocking collectives, per_device(): back = lax.all_to_all(image, SEC, 0, 0, tiled=True)  18.6 us
    all_to_all x1, blocking collectives, per_device(): lax.all_to_all(call(total_kernel, f32(32, 8, 128), vectors), RING, 0, 0,...  16.7 us
    all_to_all x1, blocking collectives, per_device(): vectors = lax.all_to_all(shares, GROUP, 0, 0, tiled=True)  13.6 us
    all_to_all x1, starting transfers between devices, per_device(): received = lax.all_to_all(packed, SEC, 0, 0, tiled=True)  13.2 us
    all_to_all x1, blocking collectives, per_device(): k0 = lax.all_to_all(spectrum, GROUP, 0, 0, tiled=True)  9.73 us
    pallas_call x10, Pallas kernels, call(): pl.pallas_call(kernel, out_shape=out, in_specs=[whole] * len(args), out_s...  7.23 us
    ppermute x3, starting transfers between devices, beside(): right = lax.ppermute(value, RING, before)  6.84 us
    unnamed x14, local copies, waits for them, and re-layouts  4.99 us
  transfers between devices with their start and end apart: 10, of which 4 were waited for; matrix products, arithmetic and copies ran while one was open for 0% of the time, Pallas kernels for 4%

profile of v8, /device:TPU:1, one launch (start us, length us, event | category | flops | bytes accessed | tf_op | source)
XLA Modules:
  0.0 111.7 jit_solution(18252093822117874186)
XLA Ops:
  0.6 1.9 %shard_map.86.q_ref = f32[64,8,256]{2,1,0:T(8,128)} custom-call(f32[8,4,2048]{2,1,0:T(4,128)} %q_ref.1, f32[8,4,2048]{2,1,0:T(4,128)} %p_ref.1), custom_call_target="tpu_custom_call" | custom-call | tf_op jit(solution)/shard_map/pallas_call | solution.py:97
  2.5 13.2 %all-to-all-start = ((f32[64,8,256]{2,1,0:T(8,128)}), f32[64,8,256]{2,1,0:T(8,128)S(1)}, u32[]{:S(2)}, u32[]{:S(2)}) async-start(f32[64,8,256]{2,1,0:T(8,128)} %shard_map.86.q_ref), calls=%async_computation | async-start | bytes 1048576 | tf_op jit(solution)/shard_map/all_to_all | solution.py:447
  15.7 2.5 %copy-done = f32[16,5,128,128]{3,2,1,0:T(8,128)S(1)} copy-done((f32[16,5,128,128]{3,2,1,0:T(8,128)S(1)}, f32[16,5,128,128]{3,2,1,0:T(8,128)}, u32[]{:S(2)}) %copy-start) | copy-done | bytes 5242904
  18.2 2.5 %copy-done.1 = f32[16,5,128,128]{3,2,1,0:T(8,128)S(1)} copy-done((f32[16,5,128,128]{3,2,1,0:T(8,128)S(1)}, f32[16,5,128,128]{3,2,1,0:T(8,128)}, u32[]{:S(2)}) %copy-start.1) | copy-done | bytes 5242904
  20.7 1.9 %shard_map.87 = (f32[8,128]{1,0:T(8,128)S(1)}, bf16[2,640,256]{2,1,0:T(8,128)(2,1)S(1)}, bf16[2,640,256]{2,1,0:T(8,128)(2,1)S(1)}) custom-call(s32[1]{0:T(128)} %bitcast.pair_ref, f32[16,5,128,128]{3,2,1,0:T(8,128)S(1)} %copy-done, f32[16,5,128,128]{3,2,1,0:T(8,128)S(1)} %copy-done.1), custom_call_target="tpu_custom_call" | custom-call | tf_op jit(solution)/shard_map/pallas_call | solution.py:451
  22.6 1.3 %collective-permute-start = (f32[8,128]{1,0:T(8,128)S(1)}, f32[8,128]{1,0:T(8,128)S(1)}, u32[]{:S(2)}, u32[]{:S(2)}) collective-permute-start(f32[8,128]{1,0:T(8,128)S(1)} %get-tuple-element.21), channel_id=1, source_target_pairs={{0,1},{1,2},{2,3},{3,0},{4,5},{5,6},{6,7},{7,4},{8,9},{9,10},{10,1... | collective-permute-start | bytes 12296 | tf_op jit(solution)/shard_map/ppermute | solution.py:439
  23.9 2.5 %collective-permute-start.1 = (f32[8,128]{1,0:T(8,128)S(1)}, f32[8,128]{1,0:T(8,128)S(1)}, u32[]{:S(2)}, u32[]{:S(2)}) collective-permute-start(f32[8,128]{1,0:T(8,128)S(1)} %get-tuple-element.21), channel_id=1, source_target_pairs={{0,2},{1,3},{2,0},{3,1},{4,6},{5,7},{6,4},{7,5},{8,10},{9,11},{10,... | collective-permute-start | bytes 12296 | tf_op jit(solution)/shard_map/ppermute | solution.py:439
  26.3 1.2 %collective-permute-start.2 = (f32[8,128]{1,0:T(8,128)S(1)}, f32[8,128]{1,0:T(8,128)S(1)}, u32[]{:S(2)}, u32[]{:S(2)}) collective-permute-start(f32[8,128]{1,0:T(8,128)S(1)} %get-tuple-element.21), channel_id=1, source_target_pairs={{0,3},{1,0},{2,1},{3,2},{4,7},{5,4},{6,5},{7,6},{8,11},{9,8},{10,9... | collective-permute-start | bytes 12296 | tf_op jit(solution)/shard_map/ppermute | solution.py:439
  28.4 0.6 collective-permute-done.2
  29.1 4.3 %all-to-all-done.r_ref = f32[64,8,256]{2,1,0:T(8,128)S(1)} async-done(((f32[64,8,256]{2,1,0:T(8,128)}), f32[64,8,256]{2,1,0:T(8,128)S(1)}, u32[]{:S(2)}, u32[]{:S(2)}) %all-to-all-start) | async-done | bytes 524320 | tf_op jit(solution)/shard_map/all_to_all | solution.py:447
  33.8 9.7 %all_to_all.25.refs_1_.k0_ref.k0 = f32[8,16,256]{2,1,0:T(8,128)S(1)} all-to-all(f32[8,16,256]{2,1,0:T(8,128)S(1)} %shard_map.88), channel_id=1, replica_groups=mesh['z'=8,'y'=4,'core'=2,'xs'=4] {'y','core'}, dimensions={0} | all-to-all | bytes 262144 | tf_op jit(solution)/shard_map/all_to_all | solution.py:478
  43.9 2.3 %collective-permute-start.4 = (f32[4,16,256]{2,1,0:T(8,128)S(1)}, f32[4,16,256]{2,1,0:T(8,128)S(1)}, u32[]{:S(2)}, u32[]{:S(2)}) collective-permute-start(f32[4,16,256]{2,1,0:T(8,128)S(1)} %slice.32), channel_id=1, source_target_pairs={{32,0},{64,32},{96,64},{128,96},{160,128},{192,160},{224,192},{225... | collective-permute-start | bytes 196616 | tf_op jit(solution)/shard_map/ppermute | solution.py:434
  46.2 1.6 %collective-permute-done.3.refs_0_ = f32[4,16,256]{2,1,0:T(8,128)S(1)} collective-permute-done((f32[4,16,256]{2,1,0:T(8,128)S(1)}, f32[4,16,256]{2,1,0:T(8,128)S(1)}, u32[]{:S(2)}, u32[]{:S(2)}) %collective-permute-start.3) | collective-permute-done | bytes 65568 | tf_op jit(solution)/shard_map/ppermute | solution.py:435
  48.4 2.6 %collective-permute-start.6 = (f32[8,16,256]{2,1,0:T(8,128)S(1)}, f32[8,16,256]{2,1,0:T(8,128)S(1)}, u32[]{:S(2)}, u32[]{:S(2)}) collective-permute-start(f32[8,16,256]{2,1,0:T(8,128)S(1)} %shard_map.89.refs_1_.s1), channel_id=1, source_target_pairs={{32,0},{64,32},{96,64},{128,96},{160,128},{192,160},{224,192},{225... | collective-permute-start | bytes 393224 | tf_op jit(solution)/shard_map/ppermute | solution.py:434
  51.1 2.3 %collective-permute-done.5.refs_0_ = f32[8,16,256]{2,1,0:T(8,128)S(1)} collective-permute-done((f32[8,16,256]{2,1,0:T(8,128)S(1)}, f32[8,16,256]{2,1,0:T(8,128)S(1)}, u32[]{:S(2)}, u32[]{:S(2)}) %collective-permute-start.5) | collective-permute-done | bytes 131104 | tf_op jit(solution)/shard_map/ppermute | solution.py:435
  53.8 1.0 collective-permute-start.7
  54.8 1.9 %collective-permute-start.8 = (f32[4,16,256]{2,1,0:T(8,128)S(1)}, f32[4,16,256]{2,1,0:T(8,128)S(1)}, u32[]{:S(2)}, u32[]{:S(2)}) collective-permute-start(f32[4,16,256]{2,1,0:T(8,128)S(1)} %get-tuple-element.27.refs_1_.k2w), channel_id=1, source_target_pairs={{32,0},{64,32},{96,64},{128,96},{160,128},{192,160},{224,192},{225... | collective-permute-start | bytes 196616 | tf_op jit(solution)/shard_map/ppermute | solution.py:434
  56.7 1.2 %shard_map.92.raw_ref = f32[8,128]{1,0:T(8,128)S(1)} custom-call(f32[8,4,2048]{2,1,0:T(4,128)S(1)} %copy-done.3, f32[8,4,2048]{2,1,0:T(4,128)S(1)} %copy-done.4), custom_call_target="tpu_custom_call" | custom-call | tf_op jit(solution)/shard_map/pallas_call | solution.py:45
  58.0 0.7 shard_map.93.rest_ref
  59.7 13.6 %all_to_all.26.v_ref = f32[8,72,128]{2,1,0:T(8,128)S(1)} all-to-all(f32[8,72,128]{2,1,0:T(8,128)S(1)} %shard_map.94), channel_id=1, replica_groups=mesh['z'=8,'y'=4,'core'=2,'xs'=4] {'y','core'}, dimensions={0} | all-to-all | bytes 589824 | tf_op jit(solution)/shard_map/all_to_all | solution.py:493
  73.2 16.7 %all_to_all.27.g_ref = f32[32,8,128]{2,1,0:T(8,128)S(1)} all-to-all(f32[32,8,128]{2,1,0:T(8,128)S(1)} %shard_map.95), channel_id=1, replica_groups=mesh['z'=8,'y'=4,'core'=2,'xs'=4] {'z','xs'}, dimensions={0} | all-to-all | bytes 262144 | tf_op jit(solution)/shard_map/all_to_all | solution.py:494
  90.0 2.0 %shard_map.96 = (f32[64,8,128]{2,1,0:T(8,128)S(1)}, f32[4,128]{1,0:T(4,128)S(1)}, f32[3,4,4]{2,1,0:T(4,128)}, f32[3,4,4]{2,1,0:T(4,128)}) custom-call(f32[32,8,128]{2,1,0:T(8,128)S(1)} %all_to_all.27.g_ref, f32[4,4]{1,0:T(4,128)S(1)} %copy-done.5, f32[8,128]{1,0:T(8,128)S(1)} %stack.2.refs_0_.refs_6_.k_ref, f32[8,72,128]{2,1,0:T(8,128)S(1)} %all_to_all.26.v_ref, ...), custom_call_target="tpu_custom_call" | custom-call | tf_op jit(solution)/shard_map/pallas_call | solution.py:45
  92.0 18.6 %all_to_all.28.r_ref = f32[64,8,128]{2,1,0:T(8,128)S(1)} all-to-all(f32[64,8,128]{2,1,0:T(8,128)S(1)} %get-tuple-element.29), channel_id=1, replica_groups=mesh['z'=8,'y'=4,'core'=2,'xs'=4] {'z','y','core'}, dimensions={0} | all-to-all | bytes 524288 | tf_op jit(solution)/shard_map/all_to_all | solution.py:500
  110.6 1.1 %shard_map.97 = f32[8,4,2048]{2,1,0:T(4,128)} custom-call(f32[64,8,128]{2,1,0:T(8,128)S(1)} %all_to_all.28.r_ref, f32[64,8,256]{2,1,0:T(8,128)S(1)} %copy-done.2, f32[4,128]{1,0:T(4,128)S(1)} %get-tuple-element.30.coef_ref), custom_call_target="tpu_custom_call" | custom-call | tf_op jit(solution)/shard_map/pallas_call | solution.py:45
  (36 shorter events, 3.7 us)
Async XLA Ops:
  2.5 30.9 %all-to-all-start = ((f32[64,8,256]{2,1,0:T(8,128)}), f32[64,8,256]{2,1,0:T(8,128)S(1)}, u32[]{:S(2)}, u32[]{:S(2)}) async-start(f32[64,8,256]{2,1,0:T(8,128)} %shard_map.86.q_ref), calls=%async_computation | async-start | bytes 1048576 | tf_op jit(solution)/shard_map/all_to_all | solution.py:447
  15.7 2.5 %copy-start = (f32[16,5,128,128]{3,2,1,0:T(8,128)S(1)}, f32[16,5,128,128]{3,2,1,0:T(8,128)}, u32[]{:S(2)}) copy-start(f32[16,5,128,128]{3,2,1,0:T(8,128)} %s_ref.1) | copy-start | bytes 15728644
  18.2 2.5 %copy-start.1 = (f32[16,5,128,128]{3,2,1,0:T(8,128)S(1)}, f32[16,5,128,128]{3,2,1,0:T(8,128)}, u32[]{:S(2)}) copy-start(f32[16,5,128,128]{3,2,1,0:T(8,128)} %c_ref.1) | copy-start | bytes 15728644
  20.7 6.8 %copy-start.6 = (s32[64]{0:T(128)S(1)}, s32[64]{0:T(128)}, u32[]{:S(2)}) copy-start(s32[64]{0:T(128)} %param.12) | copy-start | bytes 772
  20.7 7.6 %copy-start.5 = (f32[4,4]{1,0:T(4,128)S(1)}, f32[4,4]{1,0:T(4,128)}, u32[]{:S(2)}) copy-start(f32[4,4]{1,0:T(4,128)} %b_ref.3) | copy-start | bytes 196
  20.7 36.0 %copy-start.3 = (f32[8,4,2048]{2,1,0:T(4,128)S(1)}, f32[8,4,2048]{2,1,0:T(4,128)}, u32[]{:S(2)}) copy-start(f32[8,4,2048]{2,1,0:T(4,128)} %q_ref.1) | copy-start | bytes 786436
  20.7 36.0 %copy-start.4 = (f32[8,4,2048]{2,1,0:T(4,128)S(1)}, f32[8,4,2048]{2,1,0:T(4,128)}, u32[]{:S(2)}) copy-start(f32[8,4,2048]{2,1,0:T(4,128)} %p_ref.1) | copy-start | bytes 786436
  22.6 5.8 %collective-permute-start = (f32[8,128]{1,0:T(8,128)S(1)}, f32[8,128]{1,0:T(8,128)S(1)}, u32[]{:S(2)}, u32[]{:S(2)}) collective-permute-start(f32[8,128]{1,0:T(8,128)S(1)} %get-tuple-element.21), channel_id=1, source_target_pairs={{0,1},{1,2},{2,3},{3,0},{4,5},{5,6},{6,7},{7,4},{8,9},{9,10},{10,1... | collective-permute-start | bytes 12296 | tf_op jit(solution)/shard_map/ppermute | solution.py:439
  23.9 4.6 %collective-permute-start.1 = (f32[8,128]{1,0:T(8,128)S(1)}, f32[8,128]{1,0:T(8,128)S(1)}, u32[]{:S(2)}, u32[]{:S(2)}) collective-permute-start(f32[8,128]{1,0:T(8,128)S(1)} %get-tuple-element.21), channel_id=1, source_target_pairs={{0,2},{1,3},{2,0},{3,1},{4,6},{5,7},{6,4},{7,5},{8,10},{9,11},{10,... | collective-permute-start | bytes 12296 | tf_op jit(solution)/shard_map/ppermute | solution.py:439
  26.3 2.8 %collective-permute-start.2 = (f32[8,128]{1,0:T(8,128)S(1)}, f32[8,128]{1,0:T(8,128)S(1)}, u32[]{:S(2)}, u32[]{:S(2)}) collective-permute-start(f32[8,128]{1,0:T(8,128)S(1)} %get-tuple-element.21), channel_id=1, source_target_pairs={{0,3},{1,0},{2,1},{3,2},{4,7},{5,4},{6,5},{7,6},{8,11},{9,8},{10,9... | collective-permute-start | bytes 12296 | tf_op jit(solution)/shard_map/ppermute | solution.py:439
  27.7 82.9 %copy-start.2 = (f32[64,8,256]{2,1,0:T(8,128)S(1)}, f32[64,8,256]{2,1,0:T(8,128)}, u32[]{:S(2)}) copy-start(f32[64,8,256]{2,1,0:T(8,128)} %shard_map.86.q_ref) | copy-start | bytes 1572868
  43.5 4.3 %collective-permute-start.3 = (f32[4,16,256]{2,1,0:T(8,128)S(1)}, f32[4,16,256]{2,1,0:T(8,128)S(1)}, u32[]{:S(2)}, u32[]{:S(2)}) collective-permute-start(f32[4,16,256]{2,1,0:T(8,128)S(1)} %slice.32), channel_id=1, source_target_pairs={{0,32},{32,64},{64,96},{96,128},{128,160},{160,192},{192,224},{224... | collective-permute-start | bytes 196616 | tf_op jit(solution)/shard_map/ppermute | solution.py:435
  43.9 4.0 %collective-permute-start.4 = (f32[4,16,256]{2,1,0:T(8,128)S(1)}, f32[4,16,256]{2,1,0:T(8,128)S(1)}, u32[]{:S(2)}, u32[]{:S(2)}) collective-permute-start(f32[4,16,256]{2,1,0:T(8,128)S(1)} %slice.32), channel_id=1, source_target_pairs={{32,0},{64,32},{96,64},{128,96},{160,128},{192,160},{224,192},{225... | collective-permute-start | bytes 196616 | tf_op jit(solution)/shard_map/ppermute | solution.py:434
  48.2 5.1 %collective-permute-start.5 = (f32[8,16,256]{2,1,0:T(8,128)S(1)}, f32[8,16,256]{2,1,0:T(8,128)S(1)}, u32[]{:S(2)}, u32[]{:S(2)}) collective-permute-start(f32[8,16,256]{2,1,0:T(8,128)S(1)} %shard_map.89.refs_1_.s1), channel_id=1, source_target_pairs={{0,32},{32,64},{64,96},{96,128},{128,160},{160,192},{192,224},{224... | collective-permute-start | bytes 393224 | tf_op jit(solution)/shard_map/ppermute | solution.py:435
  48.4 4.9 %collective-permute-start.6 = (f32[8,16,256]{2,1,0:T(8,128)S(1)}, f32[8,16,256]{2,1,0:T(8,128)S(1)}, u32[]{:S(2)}, u32[]{:S(2)}) collective-permute-start(f32[8,16,256]{2,1,0:T(8,128)S(1)} %shard_map.89.refs_1_.s1), channel_id=1, source_target_pairs={{32,0},{64,32},{96,64},{128,96},{160,128},{192,160},{224,192},{225... | collective-permute-start | bytes 393224 | tf_op jit(solution)/shard_map/ppermute | solution.py:434
  53.8 4.9 %collective-permute-start.7 = (f32[4,16,256]{2,1,0:T(8,128)S(1)}, f32[4,16,256]{2,1,0:T(8,128)S(1)}, u32[]{:S(2)}, u32[]{:S(2)}) collective-permute-start(f32[4,16,256]{2,1,0:T(8,128)S(1)} %get-tuple-element.27.refs_1_.k2w), channel_id=1, source_target_pairs={{0,32},{32,64},{64,96},{96,128},{128,160},{160,192},{192,224},{224... | collective-permute-start | bytes 196616 | tf_op jit(solution)/shard_map/ppermute | solution.py:435
  54.8 3.9 %collective-permute-start.8 = (f32[4,16,256]{2,1,0:T(8,128)S(1)}, f32[4,16,256]{2,1,0:T(8,128)S(1)}, u32[]{:S(2)}, u32[]{:S(2)}) collective-permute-start(f32[4,16,256]{2,1,0:T(8,128)S(1)} %get-tuple-element.27.refs_1_.k2w), channel_id=1, source_target_pairs={{32,0},{64,32},{96,64},{128,96},{160,128},{192,160},{224,192},{225... | collective-permute-start | bytes 196616 | tf_op jit(solution)/shard_map/ppermute | solution.py:434
